TPU v7x, 32 devices: a whole 2x2x4 slice. The times are simulated.
32 devices in a mesh: date: 4 (over x, core), band: 8 (over z, y).
Axes of the slice: x: 2, y: 2, z: 4, core: 2. Of those that a mesh axis runs over, the one named last changes fastest.
Arguments:
- model_prognosis: bfloat16 [8, 2, 5, 32, 360], P('date', None, None, 'band'), may hold values from -6 to 6
- analysis_truth: bfloat16 [8, 2, 5, 128, 1440], P('date', None, None, 'band'), may hold values from -6 to 6
- expected_normal: bfloat16 [2, 5, 128, 1440], P(None, None, 'band'), may hold values from -5 to 5
- parallel_first_indices: int32 [128], P('band'), may hold values from -2 to 30, as said below
- parallel_blend_factors: float32 [128, 4], P('band'), may hold values from 0.05 to 0.5
- meridian_first_indices: int32 [1440], replicated, may hold values from 0 to 359, as said below
- meridian_blend_factors: bfloat16 [4, 1440], replicated, may hold values from 0.049804688 to 0.5
Outputs:
- sq_error: float32 [2, 5, 128, 1440], P(None, None, ('band', 'date'))
- anom_product: float32 [2, 5, 128, 1440], P(None, None, ('band', 'date'))
Inputs may be any that keep to these rules, and one draw needn't show every extreme that they name: `parallel_first_indices`: fine row r's stencil starts at coarse row r // 4 - 2 or r // 4 - 1. `meridian_first_indices`: fine longitude x's stencil starts at coarse longitude (x // 4 - 1) or (x // 4), taken modulo 360.
All inputs are finite; a program needn't handle non-finite values.
Results may differ from a plain program's by a relative error of at most 0.0015.
Values may be sent and summed in bfloat16 or wider, within the bound.
No kernel may reach another device: no remote copies, remote signals or barrier semaphores. Data moves between devices by JAX's collectives and lax.ppermute only.
A program may use at most 64 MiB of HBM per device.

v0:
```python
import jax
import jax.numpy as jnp
from jax import lax
from jax.sharding import PartitionSpec as P


def padded(block, sides, width):
    for axis, dim in sides:
        count = lax.axis_size(axis)
        forward = [(i, i + 1) for i in range(count - 1)]
        backward = [(target, source) for source, target in forward]
        low = lax.ppermute(
            lax.slice_in_dim(block, block.shape[dim] - width, None, axis=dim), axis, forward
        )
        high = lax.ppermute(lax.slice_in_dim(block, 0, width, axis=dim), axis, backward)
        block = jnp.concatenate([low, block, high], axis=dim)
    return block


def lon_table(meridian_first_indices, meridian_blend_factors, sparse_easting_number):
    columns = jnp.arange(sparse_easting_number, dtype=jnp.int32)[:, None]
    weights = meridian_blend_factors.astype(jnp.float32)
    table = jnp.zeros((sparse_easting_number, meridian_first_indices.shape[0]), jnp.float32)
    for stencil in range(4):
        target = ((meridian_first_indices + stencil) % sparse_easting_number)[None, :]
        table = table + weights[stencil][None, :] * (columns == target).astype(jnp.float32)
    return table.astype(jnp.bfloat16)


def shards(
    model_prognosis,
    analysis_truth,
    expected_normal,
    parallel_first_indices,
    parallel_blend_factors,
    meridian_first_indices,
    meridian_blend_factors,
):
    init_date_count, lead_time_count, variable_count, coarse_row_count, sparse_easting_number = (
        model_prognosis.shape
    )
    fine_rows = analysis_truth.shape[3]
    dense_easting_extent = analysis_truth.shape[4]
    table = lon_table(meridian_first_indices, meridian_blend_factors, sparse_easting_number)
    enlarged_prognosis_arrays = padded(model_prognosis, (("band", 3),), 2)
    flattened_arrays = enlarged_prognosis_arrays.reshape(-1, sparse_easting_number)
    returned_pair = jnp.dot(flattened_arrays, table, preferred_element_type=jnp.float32)
    through_axis = returned_pair.reshape(
        enlarged_prognosis_arrays.shape[:-1] + (dense_easting_extent,)
    )
    first_row = lax.axis_index("band") * coarse_row_count - 2
    local_start = parallel_first_indices - first_row
    columns = jnp.arange(coarse_row_count + 4, dtype=jnp.int32)[None, :]
    lat_table = jnp.zeros((fine_rows, coarse_row_count + 4), jnp.float32)
    for stencil in range(4):
        lat_table = lat_table + parallel_blend_factors[:, stencil][:, None] * (
            columns == (local_start + stencil)[:, None]
        ).astype(jnp.float32)
    climate_all = expected_normal.astype(jnp.float32)
    fine = jnp.einsum("rc,dlvcx->dlvrx", lat_table, through_axis, precision=lax.Precision.HIGHEST)
    actual = analysis_truth.astype(jnp.float32)
    error_map = fine - actual
    fcst_anom = fine - climate_all
    true_anom = actual - climate_all
    terms = jnp.stack(
        [jnp.sum(error_map * error_map, axis=0), jnp.sum(fcst_anom * true_anom, axis=0)], axis=0
    )
    partial_maps = jnp.moveaxis(terms, 3, 0)
    total = lax.psum_scatter(partial_maps, "date", scatter_dimension=0, tiled=True)
    total = total / (init_date_count * lax.axis_size("date"))
    sq_error = jnp.transpose(total[:, 0], (1, 2, 0, 3))
    anom_product = jnp.transpose(total[:, 1], (1, 2, 0, 3))
    return (sq_error, anom_product)


def solution(mesh):
    in_specs = (
        P("date", None, None, "band", None),
        P("date", None, None, "band", None),
        P(None, None, "band", None),
        P("band"),
        P("band", None),
        P(),
        P(),
    )
    out_specs = (P(None, None, ("band", "date"), None), P(None, None, ("band", "date"), None))
    return jax.shard_map(shards, mesh=mesh, in_specs=in_specs, out_specs=out_specs, check_vma=False)
```

profile of v0, /device:TPU:0, one launch (start us, length us, event | category | flops | bytes accessed | tf_op | source)
XLA Modules:
  0.0 85.2 jit_solution(16726793916694669917)
XLA Ops:
  7.2 0.0 all-reduce.3.cloned.1.call-start
  7.2 1.0 %fusion.41 = (bf16[2,2,5,2,360]{4,3,2,1,0:T(2,128)(2,1)S(1)}, bf16[2,2,5,2,360]{4,3,2,1,0:T(2,128)(2,1)S(1)}) fusion(bf16[2,2,5,4,360]{4,3,2,1,0:T(4,128)(2,1)} %param.7), kind=kLoop, calls=%fused_computation.75 | loop fusion | bytes 115200 | tf_op jit(solution)/shard_map/slice | solution.py:13
  8.2 4.9 %collective-permute-start = (bf16[2,2,5,2,360]{4,3,2,1,0:T(2,128)(2,1)S(1)}, bf16[2,2,5,2,360]{4,3,2,1,0:T(2,128)(2,1)S(1)}, u32[]{:S(2)}, u32[]{:S(2)}) collective-permute-start(bf16[2,2,5,2,360]{4,3,2,1,0:T(2,128)(2,1)S(1)} %get-tuple-element.12), channel_id=1, source_target_pairs={{0,1},{1,2},{2,3},{3,4},{4,5},{5,6},{6,7},{8,9},{9,10},{10,11},{11... | collective-permute-start | bytes 86408 | tf_op jit(solution)/shard_map/ppermute | solution.py:12
  13.1 1.3 %collective-permute-start.1 = (bf16[2,2,5,2,360]{4,3,2,1,0:T(2,128)(2,1)S(1)}, bf16[2,2,5,2,360]{4,3,2,1,0:T(2,128)(2,1)S(1)}, u32[]{:S(2)}, u32[]{:S(2)}) collective-permute-start(bf16[2,2,5,2,360]{4,3,2,1,0:T(2,128)(2,1)S(1)} %get-tuple-element.13), channel_id=1, source_target_pairs={{1,0},{2,1},{3,2},{4,3},{5,4},{6,5},{7,6},{9,8},{10,9},{11,10},{12... | collective-permute-start | bytes 86408 | tf_op jit(solution)/shard_map/ppermute | solution.py:15
  14.4 0.7 convert_element_type.8
  15.1 0.7 add_select_fusion.3
  15.8 0.7 broadcast_add_fusion.2
  16.5 0.8 slice_bitcast_fusion.5
  17.3 0.1 slice_reduce_fusion.3
  17.4 1.1 %convert_element_type.11 = f32[2,5,16,1440]{3,2,1,0:T(8,128)S(1)} convert(bf16[2,5,16,1440]{3,2,1,0:T(8,128)(2,1)} %param.9) | non-fusion elementwise | flops 230400 | bytes 1382400 | tf_op jit(solution)/shard_map/convert_element_type | solution.py:59
  18.5 0.0 collective-permute-done
  18.5 0.3 collective-permute-done.1
  18.8 0.0 copy-start
  18.8 2.3 %fusion.5 = f32[2,2,5,8,1440]{4,3,2,1,0:T(8,128)S(1)} fusion(f32[1440]{0:T(1024)S(1)} %get-tuple-element.5, s32[1440]{0:T(1024)S(1)} %get-tuple-element.16, f32[1440]{0:T(1024)S(1)} %get-tuple-element.6, s32[1440]{0:T(1024)S(1)} %get-tuple-element.17, f32[1440]{0:T(1024)S(1)} %get-tuple-element.7, s32[1440]{0:T(1024)S(1)} %get-tuple-element.15, ...), kind=kOutput, calls=%fused_computation.14 | convolution fusion | flops 172454400 | bytes 1082880 | tf_op jit(solution)/shard_map/dot_general | solution.py:47
  21.1 0.0 copy-done
  21.1 2.2 %fusion.1 = (f32[2,5,16,1440]{3,2,1,0:T(8,128)S(1)}, f32[2,5,16,1440]{3,2,1,0:T(8,128)S(1)}) fusion(bf16[2,2,5,16,1440]{4,3,2,1,0:T(8,128)(2,1)S(1)} %copy-done, f32[2,5,16,1440]{3,2,1,0:T(8,128)S(1)} %convert_element_type.11, f32[2,2,5,8,1440]{4,3,2,1,0:T(8,128)S(1)} %fusion.5, f32[16]{0:T(128)S(1)} %get-tuple-element.20, s32[16]{0:T(128)S(1)} %get-tuple-element.23, ...), kind=kOutput, calls=%fused_computation.9 | convolution fusion | flops 47463808 | bytes 4608512 | tf_op jit(solution)/shard_map/rc,dlvcx->dlvrx/dot_general | solution.py:60
  23.3 1.4 %maximum_bitcast_fusion = f32[16,2,2,5,1440]{4,0,3,2,1:T(8,128)} fusion(f32[1,2,5,16,1440]{4,3,2,1,0:T(8,128)S(1)} %bitcast.37, f32[1,2,5,16,1440]{4,3,2,1,0:T(8,128)S(1)} %bitcast.36), kind=kLoop, calls=%fused_computation.12 | loop fusion | flops 460800 | bytes 3686400 | tf_op jit(solution)/shard_map/transpose | solution.py:68
  24.7 0.0 copy-start.1
  24.7 0.0 all-reduce.3.cloned.1.call-update
  24.8 0.6 copy-done.1
  25.4 0.6 dynamic-slice
  26.6 49.6 %all-reduce.3.cloned.1.call-done = f32[16,2,2,5,1440]{4,0,3,2,1:T(8,128)} async-done(((f32[16,2,2,5,1440]{4,0,3,2,1:T(8,128)}), f32[16,2,2,5,1440]{4,0,3,2,1:T(8,128)}) %all-reduce.3.cloned.1.call-update) | async-done | bytes 1843216
  76.2 1.3 %dynamic-slice_multiply_fusion = f32[4,2,2,5,1440]{4,0,3,2,1:T(4,128)S(1)} fusion(f32[16,2,2,5,1440]{4,0,3,2,1:T(8,128)} %all-reduce.3.cloned.1.call-done, u32[]{:T(128)S(6)} %multiply.2), kind=kLoop, calls=%fused_computation.24 | loop fusion | flops 115200 | bytes 921604 | tf_op jit(solution)/shard_map/div | solution.py:70
  77.5 0.8 slice_bitcast_fusion
  (1 shorter events, 0.0 us)
Async XLA Ops:
  7.2 69.1 %all-reduce.3.cloned.1.call-start = ((), (), s32[]{:S(2)}) async-start(), calls=%async_computation | async-start | bytes 3932160
  8.2 10.3 %collective-permute-start = (bf16[2,2,5,2,360]{4,3,2,1,0:T(2,128)(2,1)S(1)}, bf16[2,2,5,2,360]{4,3,2,1,0:T(2,128)(2,1)S(1)}, u32[]{:S(2)}, u32[]{:S(2)}) collective-permute-start(bf16[2,2,5,2,360]{4,3,2,1,0:T(2,128)(2,1)S(1)} %get-tuple-element.12), channel_id=1, source_target_pairs={{0,1},{1,2},{2,3},{3,4},{4,5},{5,6},{6,7},{8,9},{9,10},{10,11},{11... | collective-permute-start | bytes 86408 | tf_op jit(solution)/shard_map/ppermute | solution.py:12
  13.1 5.8 %collective-permute-start.1 = (bf16[2,2,5,2,360]{4,3,2,1,0:T(2,128)(2,1)S(1)}, bf16[2,2,5,2,360]{4,3,2,1,0:T(2,128)(2,1)S(1)}, u32[]{:S(2)}, u32[]{:S(2)}) collective-permute-start(bf16[2,2,5,2,360]{4,3,2,1,0:T(2,128)(2,1)S(1)} %get-tuple-element.13), channel_id=1, source_target_pairs={{1,0},{2,1},{3,2},{4,3},{5,4},{6,5},{7,6},{9,8},{10,9},{11,10},{12... | collective-permute-start | bytes 86408 | tf_op jit(solution)/shard_map/ppermute | solution.py:15
  18.8 2.3 %copy-start = (bf16[2,2,5,16,1440]{4,3,2,1,0:T(8,128)(2,1)S(1)}, bf16[2,2,5,16,1440]{4,3,2,1,0:T(8,128)(2,1)}, u32[]{:S(2)}) copy-start(bf16[2,2,5,16,1440]{4,3,2,1,0:T(8,128)(2,1)} %param.8) | copy-start | bytes 2764804
  24.7 0.7 copy-start.1
Sparse Core Ops, SparseCore 0:
  24.9 51.3 all-reduce.2
where the time goes:
time: 85.7 us; the launch traced here: 85.2 us
  waiting for transfers between devices  50 us (58%)
  between operations  14.8 us (17%)
  starting transfers between devices  6.2 us (7%)
  other arithmetic  5.95 us (7%)
  matrix products  4.45 us (5%)
  local copies, waits for them, and re-layouts  3.89 us (5%)
    unnamed x2, waiting for transfers between devices  49.6 us
    ppermute x1, starting transfers between devices, padded(): lax.ppermute(lax.slice_in_dim(block, block.shape[dim] - width, None, axis...  4.87 us
    dot_general x1, matrix products, shards(): jnp.dot(flattened_arrays, table, preferred_element_type=jnp.float32)  2.27 us
    dot_general x1, matrix products, shards(): jnp.einsum('rc,dlvcx->dlvrx', lat_table, through_axis, precision=lax.Prec...  2.18 us
  transfers between devices with their start and end apart: 3, of which 2 were waited for; matrix products, arithmetic and copies ran while one was open for 6% of the time, Pallas kernels for 0%

commit v1 on v0

v1 whole, which is shorter than its diff:
```python
import functools

import jax
import jax.numpy as jnp
from jax import lax
from jax.experimental import pallas as pl
from jax.experimental.pallas import tpu as pltpu
from jax.sharding import PartitionSpec as P

TAPS = 4
LANES = 128
WIDE = 256
CARRY_SCALE = 16.0


def edges_kernel(own_ref, kept_ref, cross_ref, pair_ref):
    even = lax.rem(lax.axis_index("band"), 2) == 0
    for index in range(own_ref.shape[0]):
        kept_ref[index] = own_ref[index]
        rows = own_ref[index].astype(jnp.float32)
        bottom, top = rows[:2], rows[rows.shape[0] - 2 :]
        pair_ref[index] = jnp.where(even, top, bottom).astype(jnp.bfloat16)
        cross_ref[index] = jnp.where(even, bottom, top).astype(jnp.bfloat16)


def taps_kernel(tap_ref):
    row = lax.broadcasted_iota(jnp.int32, tap_ref.shape, 0)
    tap_ref[...] = row - lax.broadcasted_iota(jnp.int32, tap_ref.shape, 1) // 4


def fill_tables(tap_ref, lon_ref, table_ref):
    dense = lon_ref.shape[1]
    for tile in range(pl.cdiv(dense, WIDE)):
        low_x = tile * WIDE
        width = min(WIDE, dense - low_x)
        base = low_x // 4 % LANES
        rows = width // 4 + 8
        depth_here = LANES if base + rows <= LANES else 2 * LANES
        columns = slice(low_x, low_x + width)
        offset = tap_ref[:rows, :width] - lon_ref[TAPS : TAPS + 1, columns].astype(jnp.int32)
        block = jnp.zeros((rows, width), jnp.float32)
        for tap in range(TAPS):
            block = jnp.where(offset == tap, lon_ref[tap : tap + 1, columns], block)
        parts = [block]
        if base:
            parts.insert(0, jnp.zeros((base, width), jnp.float32))
        if depth_here > base + rows:
            parts.append(jnp.zeros((depth_here - base - rows, width), jnp.float32))
        table_ref[tile, :depth_here, :width] = jnp.concatenate(parts, axis=0).astype(jnp.bfloat16)


def widened(lhs_ref, table_ref, tile, low_x, width):
    base = low_x // 4 % LANES
    begin = low_x // 4 - base
    depth = LANES if base + width // 4 + 8 <= LANES else 2 * LANES
    lhs = jnp.concatenate([lhs_ref[0, :, begin : begin + depth], lhs_ref[1, :, begin : begin + depth]], axis=1)
    table = table_ref[tile, :depth, :width]
    return jnp.dot(lhs, jnp.concatenate([table, table], axis=0), preferred_element_type=jnp.float32)


def wrapped_rows(rows, depth):
    sparse = rows.shape[1]
    filler = jnp.zeros((rows.shape[0], depth - sparse - 4), jnp.float32)
    return jnp.concatenate([rows[:, sparse - 1 :], rows, rows[:, :3], filler], axis=1)


def error_kernel(
    own_ref,
    cross_ref,
    pair_ref,
    truth_ref,
    tap_ref,
    lon_ref,
    lat_ref,
    out_ref,
    fine_ref,
    lhs_ref,
    table_ref,
):
    fields, coarse_rows, sparse = own_ref.shape
    _, fine_rows, dense = truth_ref.shape
    pairs = out_ref.shape[2]
    dates = fields // pairs
    ratio = fine_rows // coarse_rows
    span = 8 // ratio
    depth = lhs_ref.shape[2]
    tiles = pl.cdiv(dense, WIDE)
    band = lax.axis_index("band")
    even = lax.rem(band, 2) == 0
    lowest = band == 0
    highest = band == lax.axis_size("band") - 1

    fill_tables(tap_ref, lon_ref, table_ref)

    weights = lat_ref[...].T
    lat = [
        [
            jnp.broadcast_to(weights[8 * group : 8 * group + 8, tap : tap + 1], (8, LANES))
            for tap in range(TAPS + 1)
        ]
        for group in range(fine_rows // 8)
    ]
    lat = [[jnp.concatenate([w] * (depth // LANES), axis=1) for w in group] for group in lat]

    upper_half = lax.broadcasted_iota(jnp.int32, (8, depth), 0) < ratio
    for pair in range(pairs):
        for date in range(dates):
            index = date * pairs + pair
            paired = pair_ref[index].astype(jnp.float32)
            crossed = cross_ref[index].astype(jnp.float32)
            low = jnp.where(lowest, 0.0, jnp.where(even, crossed, paired))
            high = jnp.where(highest, 0.0, jnp.where(even, paired, crossed))
            rows8 = jnp.concatenate([low, own_ref[index].astype(jnp.float32), high], axis=0)
            wrapped = wrapped_rows(rows8, depth)
            spread = [jnp.broadcast_to(wrapped[i : i + 1], (8, depth)) for i in range(coarse_rows + 4)]
            mixed = [jnp.where(upper_half, spread[i], spread[i + 1]) for i in range(coarse_rows + 3)]
            both = []
            for group in range(fine_rows // 8):
                total = lat[group][0] * mixed[span * group]
                for tap in range(1, TAPS + 1):
                    total = total + lat[group][tap] * mixed[span * group + tap]
                both.append(total)
            both = jnp.concatenate(both, axis=0)
            upper = both.astype(jnp.bfloat16)
            rest = (both - upper.astype(jnp.float32)).astype(jnp.bfloat16)
            at = (pair * dates + date) * fine_rows
            lhs_ref[0, at : at + fine_rows, :] = upper
            lhs_ref[1, at : at + fine_rows, :] = rest

    for tile in range(tiles):
        low_x = tile * WIDE
        width = min(WIDE, dense - low_x)
        columns = slice(low_x, low_x + width)
        fine_ref[:, columns] = widened(lhs_ref, table_ref, tile, low_x, width)
        for pair in range(pairs):
            total = 0.0
            for date in range(dates):
                at = (pair * dates + date) * fine_rows
                actual = truth_ref[date * pairs + pair, :, columns].astype(jnp.float32)
                error = fine_ref[at : at + fine_rows, columns] - actual
                total = total + error * error
            store_by_owner(out_ref, pair, columns, total)


def store_by_owner(out_ref, pair, columns, values):
    _, halves, _, owned, _ = out_ref.shape
    for owner in range(2 * halves):
        out_ref[owner % 2, owner // 2, pair, :, columns] = values[owner * owned : (owner + 1) * owned]


def anomaly_kernel(fine_ref, truth_ref, normal_ref, out_ref):
    fields, fine_rows, dense = truth_ref.shape
    pairs = normal_ref.shape[0]
    dates = fields // pairs
    for low_x in range(0, dense, WIDE):
        columns = slice(low_x, min(low_x + WIDE, dense))
        for pair in range(pairs):
            normal = normal_ref[pair, :, columns].astype(jnp.float32)
            total = 0.0
            for date in range(dates):
                at = (pair * dates + date) * fine_rows
                actual = truth_ref[date * pairs + pair, :, columns].astype(jnp.float32)
                total = total + (fine_ref[at : at + fine_rows, columns] - normal) * (actual - normal)
            store_by_owner(out_ref, pair, columns, total)


def edge_rows(own):
    fields, _, sparse = own.shape
    vmem = pl.BlockSpec(memory_space=pltpu.VMEM)
    edges = jax.ShapeDtypeStruct((fields, 2, sparse), jnp.bfloat16)
    return pl.pallas_call(
        edges_kernel,
        out_shape=[jax.ShapeDtypeStruct(own.shape, own.dtype), edges, edges],
        in_specs=[vmem],
        out_specs=[vmem] * 3,
        compiler_params=pltpu.CompilerParams(vmem_limit_bytes=8 * 1024 * 1024),
        cost_estimate=pl.CostEstimate(flops=100_000_000, bytes_accessed=200_000, transcendentals=0),
    )(own)


def lat_tap_weights(starts, weights, first_coarse, ratio):
    rows = starts.shape[0]
    late = starts > first_coarse + lax.iota(jnp.int32, rows) // ratio - 2
    by_tap = weights.T
    early = jnp.pad(by_tap, ((0, 8 - TAPS), (0, LANES - rows)))
    shifted = jnp.pad(by_tap, ((1, 7 - TAPS), (0, LANES - rows)))
    return jnp.where(jnp.pad(late, (0, LANES - rows))[None], shifted, early)


def error_map(own, crossed, paired, truth, taps, lon, lat, pairs, owners):
    fields, _, sparse = own.shape
    _, fine_rows, dense = truth.shape
    depth = pl.cdiv(sparse + 4, LANES) * LANES
    vmem = pl.BlockSpec(memory_space=pltpu.VMEM)
    return pl.pallas_call(
        error_kernel,
        out_shape=[
            jax.ShapeDtypeStruct((2, owners // 2, pairs, fine_rows // owners, dense), jnp.float32),
            jax.ShapeDtypeStruct((fields * fine_rows, dense), jnp.float32),
        ],
        in_specs=[vmem] * 7,
        out_specs=[vmem] * 2,
        scratch_shapes=[
            pltpu.VMEM((2, fields * fine_rows, depth), jnp.bfloat16),
            pltpu.VMEM((pl.cdiv(dense, WIDE), 2 * LANES, WIDE), jnp.bfloat16),
        ],
        compiler_params=pltpu.CompilerParams(vmem_limit_bytes=24 * 1024 * 1024),
        cost_estimate=pl.CostEstimate(flops=1_000_000_000, bytes_accessed=4_000_000, transcendentals=0),
    )(own, crossed, paired, truth, taps, lon, lat)


def anomaly_map(fine, truth, normal, owners):
    pairs, fine_rows, dense = normal.shape
    vmem = pl.BlockSpec(memory_space=pltpu.VMEM)
    return pl.pallas_call(
        anomaly_kernel,
        out_shape=jax.ShapeDtypeStruct((2, owners // 2, pairs, fine_rows // owners, dense), jnp.float32),
        in_specs=[vmem] * 3,
        out_specs=vmem,
        compiler_params=pltpu.CompilerParams(vmem_limit_bytes=24 * 1024 * 1024),
        cost_estimate=pl.CostEstimate(flops=500_000_000, bytes_accessed=4_000_000, transcendentals=0),
    )(fine, truth, normal)


def first_core():
    return lax.rem(lax.axis_index("date"), 2) == 0


def lower_chip():
    return lax.axis_index("date") < lax.axis_size("date") // 2


def by_owner(ref, entries, lower):
    blocks = [ref[entry].astype(jnp.float32) for entry in entries]
    half = blocks[0].shape[0] // 2
    blocks = [jnp.where(lower, block[:half], block[half:]) for block in blocks]
    owned = half // 2
    return (
        jnp.concatenate([block[:owned] for block in blocks], axis=0),
        jnp.concatenate([block[owned:] for block in blocks], axis=0),
    )


def packed_tiles(entries, dense):
    full, tail = divmod(dense, LANES)
    return entries * full + (pl.cdiv(entries, LANES // tail) if tail else 0)


def pack_rows(blocks, out_ref):
    rows, dense = blocks[0].shape
    full, tail = divmod(dense, LANES)
    for at, block in enumerate(blocks):
        for tile in range(full):
            out_ref[at * full + tile] = block[:, tile * LANES : (tile + 1) * LANES].astype(out_ref.dtype)
    if tail:
        share = LANES // tail
        tails = [block[:, full * LANES :] for block in blocks]
        tails += [jnp.zeros((rows, tail), jnp.float32)] * (-len(tails) % share)
        filler = [jnp.zeros((rows, LANES - share * tail), jnp.float32)] if LANES % tail else []
        for at in range(0, len(tails), share):
            joined = jnp.concatenate(tails[at : at + share] + filler, axis=1)
            out_ref[len(blocks) * full + at // share] = joined.astype(out_ref.dtype)


def unpacked_rows(ref, at, entries, dense, low_x, width):
    full, tail = divmod(dense, LANES)
    parts = [
        ref[at * full + tile].astype(jnp.float32)
        for tile in range(low_x // LANES, min((low_x + width) // LANES, full))
    ]
    if low_x + width > full * LANES:
        share = LANES // tail
        start = at % share * tail
        parts.append(ref[entries * full + at // share].astype(jnp.float32)[:, start : start + tail])
    return jnp.concatenate(parts, axis=1)


def away_kernel(dates, truth_ref, _, straight_ref, crossed_ref):
    pairs = truth_ref.shape[0] // dates
    first = first_core()
    straight, crossed = [], []
    for pair in range(pairs):
        entries = [date * pairs + pair for date in range(dates)]
        one, two = by_owner(truth_ref, entries, jnp.logical_not(lower_chip()))
        straight.append(jnp.where(first, one, two))
        crossed.append(jnp.where(first, two, one))
    pack_rows(straight, straight_ref)
    pack_rows(crossed, crossed_ref)


def home_kernel(dates, truth_ref, normal_ref, mine_ref, sibling_ref, normals_ref):
    pairs = normal_ref.shape[0]
    first = first_core()
    lower = lower_chip()
    for pair in range(pairs):
        one, two = by_owner(truth_ref, [date * pairs + pair for date in range(dates)], lower)
        mine_ref[pair] = jnp.where(first, one, two).astype(mine_ref.dtype)
        sibling_ref[pair] = jnp.where(first, two, one).astype(sibling_ref.dtype)
        one, two = by_owner(normal_ref, [pair] * dates, lower)
        normals_ref[pair] = jnp.where(first, one, two)


def shift_rows_kernel(own_ref, peer_ref, both_ref, rows_ref):
    lower = lower_chip()
    fields, coarse_rows, _ = own_ref.shape
    for index in range(2 * fields):
        block = (own_ref if index < fields else peer_ref)[index % fields]
        both_ref[index] = block
        block = block.astype(jnp.float32)
        rows_ref[index] = jnp.where(lower, block[coarse_rows - 2 :], block[:2]).astype(jnp.bfloat16)


def latitude_step(pairs, coarse_ref, halo_ref, lat_ref, lhs_ref, stage_ref):
    fields = coarse_ref.shape[0] // 2
    dates = fields // pairs
    depth = lhs_ref.shape[2]
    rows = lhs_ref.shape[1] // (2 * pairs)
    owned = rows // dates
    band = lax.axis_index("band")
    lower = lower_chip()
    first = first_core()
    outside = jnp.logical_or(
        jnp.logical_and(lower, band == 0),
        jnp.logical_and(jnp.logical_not(lower), band == lax.axis_size("band") - 1),
    )
    weights = lat_ref[...].T
    weights = jnp.where(lower, weights[: 2 * owned], weights[2 * owned : 4 * owned])
    weights = jnp.where(first, weights[:owned], weights[owned:])
    weights = jnp.concatenate([weights] * dates, axis=0)
    lat = [jnp.broadcast_to(weights[:, tap : tap + 1], (rows, depth)) for tap in range(TAPS + 1)]
    date_of_row = lax.broadcasted_iota(jnp.int32, (rows, depth), 0) // owned
    for side in range(2):
        for pair in range(pairs):
            sources = []
            for date in range(dates):
                index = side * fields + date * pairs + pair
                inner = coarse_ref[index].astype(jnp.float32)
                edge = jnp.where(outside, 0.0, halo_ref[index].astype(jnp.float32))
                below = jnp.concatenate([edge, inner], axis=0)
                above = jnp.concatenate([inner, edge], axis=0)
                wrapped = wrapped_rows(jnp.where(lower, below, above), depth)
                sources.append(jnp.where(first, wrapped[: TAPS + 1], wrapped[1 : TAPS + 2]))
            total = 0.0
            for tap in range(TAPS + 1):
                mixed = jnp.broadcast_to(sources[0][tap : tap + 1], (rows, depth))
                for date in range(1, dates):
                    spread = jnp.broadcast_to(sources[date][tap : tap + 1], (rows, depth))
                    mixed = jnp.where(date_of_row == date, spread, mixed)
                total = total + lat[tap] * mixed
            upper = total.astype(jnp.bfloat16).astype(jnp.float32)
            at = (side * pairs + pair) * rows
            stage_ref[at : at + rows, :depth] = upper
            stage_ref[at : at + rows, depth:] = total - upper
    lhs_ref[0] = stage_ref[:, :depth].astype(jnp.bfloat16)
    lhs_ref[1] = stage_ref[:, depth:].astype(jnp.bfloat16)


def column_blocks(dense):
    for tile in range(pl.cdiv(dense, WIDE)):
        low_x = tile * WIDE
        width = min(WIDE, dense - low_x)
        yield tile, low_x, width, slice(low_x, low_x + width)


def added(sums, fine, actual, normal):
    error = fine - actual
    return sums[0] + error * error, sums[1] + (fine - normal) * (actual - normal)


def own_dates_kernel(
    coarse_ref,
    halo_ref,
    truth_ref,
    normals_ref,
    lat_ref,
    tap_ref,
    lon_ref,
    sums_ref,
    away_ref,
    table_ref,
    lhs_ref,
    stage_ref,
):
    pairs, rows, dense = truth_ref.shape
    fill_tables(tap_ref, lon_ref, table_ref)
    latitude_step(pairs, coarse_ref, halo_ref, lat_ref, lhs_ref, stage_ref)
    for tile, low_x, width, columns in column_blocks(dense):
        stage_ref[:, :width] = widened(lhs_ref, table_ref, tile, low_x, width)
        away_ref[:, columns] = stage_ref[pairs * rows :, :width]
        for pair in range(pairs):
            fine = stage_ref[pair * rows : (pair + 1) * rows, :width]
            actual = truth_ref[pair, :, columns].astype(jnp.float32)
            sums = added((0.0, 0.0), fine, actual, normals_ref[pair, :, columns])
            sums_ref[0, pair, :, columns], sums_ref[1, pair, :, columns] = sums


def sibling_dates_kernel(
    coarse_ref,
    halo_ref,
    truth_ref,
    normals_ref,
    lat_ref,
    table_ref,
    before_ref,
    straight_fine_ref,
    straight_ref,
    sums_ref,
    away_ref,
    lhs_ref,
    stage_ref,
):
    pairs, rows, dense = truth_ref.shape
    latitude_step(pairs, coarse_ref, halo_ref, lat_ref, lhs_ref, stage_ref)
    for tile, low_x, width, columns in column_blocks(dense):
        stage_ref[:, :width] = widened(lhs_ref, table_ref, tile, low_x, width)
        away_ref[:, columns] = stage_ref[pairs * rows :, :width]
        for pair in range(pairs):
            span = slice(pair * rows, (pair + 1) * rows)
            normal = normals_ref[pair, :, columns]
            sums = (before_ref[0, pair, :, columns], before_ref[1, pair, :, columns])
            actual = truth_ref[pair, :, columns].astype(jnp.float32)
            sums = added(sums, stage_ref[span, :width], actual, normal)
            actual = unpacked_rows(straight_ref, pair, pairs, dense, low_x, width)
            sums = added(sums, straight_fine_ref[span, columns], actual, normal)
            sums_ref[0, pair, :, columns], sums_ref[1, pair, :, columns] = sums


def mean_kernel(dates, count, before_ref, fine_ref, crossed_ref, normals_ref, *results):
    pairs, rows, dense = normals_ref.shape
    owned = rows // dates
    for _, low_x, width, columns in column_blocks(dense):
        for pair in range(pairs):
            sums = (before_ref[0, pair, :, columns], before_ref[1, pair, :, columns])
            actual = unpacked_rows(crossed_ref, pair, pairs, dense, low_x, width)
            fine = fine_ref[pair * rows : (pair + 1) * rows, columns]
            sums = added(sums, fine, actual, normals_ref[pair, :, columns])
            for total, out_ref in zip(sums, results):
                parts = [total[date * owned : (date + 1) * owned] for date in range(dates)]
                out_ref[pair, :, columns] = sum(parts[1:], parts[0]) / count


def kernel_call(kernel, out_shape, scratch, megabytes, flops, *operands):
    vmem = pl.BlockSpec(memory_space=pltpu.VMEM)
    return pl.pallas_call(
        kernel,
        out_shape=out_shape,
        in_specs=[vmem] * len(operands),
        out_specs=[vmem] * len(out_shape),
        scratch_shapes=scratch,
        compiler_params=pltpu.CompilerParams(vmem_limit_bytes=megabytes * 1024 * 1024),
        cost_estimate=pl.CostEstimate(flops=flops, bytes_accessed=0, transcendentals=0),
    )(*operands)


def two_chip_maps(model_prognosis, analysis_truth, expected_normal, taps, lon_weights, lat_weights):
    bands = lax.axis_size("band")
    groups = lax.axis_size("date")
    dates, leads, variables, coarse_rows, sparse = model_prognosis.shape
    fine_rows, dense = analysis_truth.shape[3:]
    owned = fine_rows // groups
    rows = dates * owned
    pairs = leads * variables
    fields = dates * pairs
    depth = pl.cdiv(sparse + 4, LANES) * LANES
    float32, bfloat16 = jnp.float32, jnp.bfloat16
    straight_way = [(i, (i + 2) % groups) for i in range(groups)]
    crossed_way = [(i, (i + 2) % groups ^ 1) for i in range(groups)]
    sibling_way = [(i, i ^ 1) for i in range(groups)]

    own = model_prognosis.reshape(fields, coarse_rows, sparse)
    truth = analysis_truth.reshape(fields, fine_rows, dense)
    normal = expected_normal.reshape(pairs, fine_rows, dense)
    peer = lax.ppermute(model_prognosis, "date", straight_way).reshape(own.shape)

    packed = jax.ShapeDtypeStruct((packed_tiles(pairs, dense), rows, LANES), bfloat16)
    straight, crossed = kernel_call(
        functools.partial(away_kernel, dates), [packed, packed], [], 8, 100_000_000, truth, taps
    )
    straight = lax.ppermute(straight, "date", straight_way)
    crossed = lax.ppermute(crossed, "date", crossed_way)
    plain = jax.ShapeDtypeStruct((pairs, rows, dense), bfloat16)
    mine, sibling, normals = kernel_call(
        functools.partial(home_kernel, dates),
        [plain, plain, jax.ShapeDtypeStruct((pairs, rows, dense), float32)],
        [],
        12,
        100_000_000,
        truth,
        normal,
    )
    sibling = lax.ppermute(sibling, "date", sibling_way)

    chain = []
    for group in range(groups):
        for band in range(bands):
            to = band + (1 if group < groups // 2 else -1)
            if 0 <= to < bands:
                chain.append((group * bands + band, group * bands + to))
    coarse, edges = kernel_call(
        shift_rows_kernel,
        [
            jax.ShapeDtypeStruct((2 * fields, coarse_rows, sparse), bfloat16),
            jax.ShapeDtypeStruct((2 * fields, 2, sparse), bfloat16),
        ],
        [],
        8,
        100_000_000,
        own,
        peer,
    )
    halo = lax.ppermute(edges, ("date", "band"), chain)
    sibling_coarse = lax.ppermute(coarse, "date", sibling_way)
    sibling_halo = lax.ppermute(halo, "date", sibling_way)

    sums = jax.ShapeDtypeStruct((2, pairs, rows, dense), float32)
    away = jax.ShapeDtypeStruct((pairs * rows, dense), float32)
    table = jax.ShapeDtypeStruct((pl.cdiv(dense, WIDE), 2 * LANES, WIDE), bfloat16)
    scratch = [
        pltpu.VMEM((2, 2 * pairs * rows, depth), bfloat16),
        pltpu.VMEM((2 * pairs * rows, 2 * depth), float32),
    ]
    own_sums, straight_fine, table = kernel_call(
        own_dates_kernel,
        [sums, away, table],
        scratch,
        20,
        0,
        coarse,
        halo,
        mine,
        normals,
        lat_weights,
        taps,
        lon_weights,
    )
    chip_sums, crossed_fine = kernel_call(
        sibling_dates_kernel,
        [sums, away],
        scratch,
        20,
        0,
        sibling_coarse,
        sibling_halo,
        sibling,
        normals,
        lat_weights,
        table,
        own_sums,
        straight_fine,
        straight,
    )
    out = jax.ShapeDtypeStruct((pairs, owned, dense), float32)
    results = kernel_call(
        functools.partial(mean_kernel, dates, dates * groups),
        [out, out],
        [],
        16,
        0,
        chip_sums,
        crossed_fine,
        crossed,
        normals,
    )
    return tuple(result.reshape(leads, variables, owned, dense) for result in results)


def shards(
    model_prognosis,
    analysis_truth,
    expected_normal,
    parallel_first_indices,
    parallel_blend_factors,
    meridian_first_indices,
    meridian_blend_factors,
):
    bands = lax.axis_size("band")
    groups = lax.axis_size("date")
    halves = groups // 2
    dates = model_prognosis.shape[0]
    group = lax.axis_index("date")
    core = lax.rem(group, 2)
    half = lax.div(group, 2)

    coarse_rows = model_prognosis.shape[3]
    lat_weights = lat_tap_weights(
        parallel_first_indices,
        parallel_blend_factors,
        lax.axis_index("band") * coarse_rows,
        analysis_truth.shape[3] // coarse_rows,
    )
    dense = meridian_first_indices.shape[0]
    late = meridian_first_indices == lax.iota(jnp.int32, dense) // 4
    lon_weights = jnp.where(
        lax.broadcasted_iota(jnp.int32, (8, dense), 0) < TAPS,
        jnp.pad(meridian_blend_factors, ((0, 8 - TAPS), (0, 0))).astype(jnp.float32),
        late.astype(jnp.float32)[None],
    )
    (taps,) = kernel_call(
        taps_kernel, [jax.ShapeDtypeStruct((WIDE // 4 + 8, WIDE), jnp.int32)], [], 8, 2_000_000_000
    )
    if halves == 2 and dates * analysis_truth.shape[3] == 8 * groups:
        return two_chip_maps(model_prognosis, analysis_truth, expected_normal, taps, lon_weights, lat_weights)

    own = model_prognosis.reshape((-1,) + model_prognosis.shape[3:])
    own, to_cross, to_pair = edge_rows(own)
    across = [(i, min(max(i + (1 if i % 2 else -1), 0), bands - 1)) for i in range(bands)]
    paired = lax.ppermute(to_pair, "band", [(i, i ^ 1) for i in range(bands)])
    crossed = lax.ppermute(to_cross, "band", across)
    truth = analysis_truth.reshape((-1,) + analysis_truth.shape[3:])
    normal = expected_normal.reshape((-1,) + expected_normal.shape[2:])
    error, fine = error_map(own, crossed, paired, truth, taps, lon_weights, lat_weights, normal.shape[0], groups)
    anomaly = anomaly_map(fine, truth, normal, groups)

    def packed(values):
        return (values * CARRY_SCALE).astype(jnp.float16)

    def unpacked(values):
        return values.astype(jnp.float32) / CARRY_SCALE

    def row_block(values, index):
        return lax.dynamic_index_in_dim(values, index, 0, keepdims=False)

    def mean_over_dates(maps):
        swapped = lax.ppermute(packed(row_block(maps, 1 - core)), "date", [(i, i ^ 1) for i in range(groups)])

        def chip_sum(index):
            mine = lax.dynamic_slice(maps, (core, index, 0, 0, 0), (1, 1) + maps.shape[2:])[0, 0]
            return mine + unpacked(row_block(swapped, index))

        pieces = []
        for step in range(1, halves):
            piece = packed(chip_sum(lax.rem(half + step, halves)))
            ring = [(i, (i + 2 * step) % groups) for i in range(groups)]
            pieces.append(lax.ppermute(piece, "date", ring))
        total = chip_sum(half)
        for piece in pieces:
            total = total + unpacked(piece)
        total = total / (dates * groups)
        return total.reshape(expected_normal.shape[:2] + total.shape[1:])

    return (mean_over_dates(error), mean_over_dates(anomaly))


def solution(mesh):
    in_specs = (
        P("date", None, None, "band", None),
        P("date", None, None, "band", None),
        P(None, None, "band", None),
        P("band"),
        P("band", None),
        P(),
        P(),
    )
    out_specs = (P(None, None, ("band", "date"), None), P(None, None, ("band", "date"), None))
    return jax.shard_map(shards, mesh=mesh, in_specs=in_specs, out_specs=out_specs, check_vma=False)
```

time: 85.7 us -> 16.8 us (0.20)
  waiting for transfers between devices: 50 us -> 3.09 us
  between operations: 14.8 us -> 0.78 us
  other arithmetic: 5.95 us -> 0.11 us
  matrix products: 4.45 us -> 0 us
  local copies, waits for them, and re-layouts: 3.89 us -> 0.04 us
  Pallas kernels: 0 us -> 3.39 us
  starting transfers between devices: 6.2 us -> 9.14 us
    unnamed x2 -> x0, waiting for transfers between devices: 49.6 us -> none
    dot_general x2 -> x0, matrix products: 4.45 us -> none  [the longest x1 2.27 us: shards(): jnp.dot(flattened_arrays, table, preferred_element_type=jnp.float32)]
    pallas_call x0 -> x7, Pallas kernels: none -> 3.39 us  [kernel_call(): pl.pallas_call(kernel, out_shape=out_shape, in_specs=[vmem] * len(operand...]
    ppermute x2 -> x7, starting transfers between devices: 6.16 us -> 9.14 us  [the longest x1 3.81 us: two_chip_maps(): halo = lax.ppermute(edges, ('date', 'band'), chain)]
    ppermute x2 -> x7, waiting for transfers between devices: 0.33 us -> 3.09 us  [the longest x1 1.71 us: two_chip_maps(): halo = lax.ppermute(edges, ('date', 'band'), chain)]
    convert_element_type x2 -> x1, other arithmetic: 1.84 us -> 0.01 us  [shards(): late.astype(jnp.float32)[None]]
    transpose x1 -> x0, other arithmetic: 1.41 us -> none  [shards(): partial_maps = jnp.moveaxis(terms, 3, 0)]
    div x1 -> x0, other arithmetic: 1.31 us -> none  [shards(): total = total / (init_date_count * lax.axis_size('date'))]
  transfers between devices with their start and end apart: 3 -> 7, of which waited for: 2 -> 3; matrix products, arithmetic and copies ran while one was open for 6% -> 1% of each run, Pallas kernels for 0% -> 14%
where the time goes in v1:
time: 16.8 us; the launch traced here: 16.6 us
  starting transfers between devices  9.14 us (54%)
  Pallas kernels  3.39 us (20%)
  waiting for transfers between devices  3.09 us (18%)
  between operations  0.78 us (5%)
    ppermute x1, starting transfers between devices, two_chip_maps(): halo = lax.ppermute(edges, ('date', 'band'), chain)  3.81 us
    pallas_call x7, Pallas kernels, kernel_call(): pl.pallas_call(kernel, out_shape=out_shape, in_specs=[vmem] * len(operand...  3.39 us
    ppermute x1, starting transfers between devices, two_chip_maps(): lax.ppermute(model_prognosis, 'date', straight_way).reshape(own.shape)  3 us
    ppermute x1, waiting for transfers between devices, two_chip_maps(): halo = lax.ppermute(edges, ('date', 'band'), chain)  1.71 us
    ppermute x1, starting transfers between devices, two_chip_maps(): straight = lax.ppermute(straight, 'date', straight_way)  1.15 us
    ppermute x1, starting transfers between devices, two_chip_maps(): sibling = lax.ppermute(sibling, 'date', sibling_way)  1.1 us
    ppermute x1, waiting for transfers between devices, two_chip_maps(): crossed = lax.ppermute(crossed, 'date', crossed_way)  1 us
    ppermute x1, waiting for transfers between devices, two_chip_maps(): sibling_halo = lax.ppermute(halo, 'date', sibling_way)  0.36 us
  transfers between devices with their start and end apart: 7, of which 3 were waited for; matrix products, arithmetic and copies ran while one was open for 1% of the time, Pallas kernels for 14%

profile of v1, /device:TPU:0, one launch (start us, length us, event | category | flops | bytes accessed | tf_op | source)
XLA Modules:
  0.0 16.6 jit_solution(4639643474286665869)
XLA Ops:
  0.6 0.0 copy-start
  0.6 3.0 %collective-permute-start = (bf16[2,2,5,4,360]{4,3,2,1,0:T(4,128)(2,1)}, bf16[2,2,5,4,360]{4,3,2,1,0:T(4,128)(2,1)S(1)}, u32[]{:S(2)}, u32[]{:S(2)}) collective-permute-start(bf16[2,2,5,4,360]{4,3,2,1,0:T(4,128)(2,1)} %param.7), channel_id=1, source_target_pairs={{0,16},{8,24},{16,0},{24,8},{1,17},{9,25},{17,1},{25,9},{2,18},{10... | collective-permute-start | bytes 172808 | tf_op jit(solution)/shard_map/ppermute | solution.py:473
  3.7 0.0 copy-done
  3.7 0.0 copy-start.1
  3.7 0.2 %shard_map.90 = (bf16[113,8,128]{2,1,0:T(8,128)(2,1)S(1)}, bf16[113,8,128]{2,1,0:T(8,128)(2,1)S(1)}) custom-call(bf16[20,16,1440]{2,1,0:T(8,128)(2,1)S(1)} %bitcast.7, s32[72,256]{1,0:T(8,128)S(1)} %shard_map.88.tap_ref._), custom_call_target="tpu_custom_call" | custom-call | flops 100000000 | tf_op jit(solution)/shard_map/pallas_call | solution.py:444
  3.9 1.2 %collective-permute-start.5 = (bf16[113,8,128]{2,1,0:T(8,128)(2,1)S(1)}, bf16[113,8,128]{2,1,0:T(8,128)(2,1)S(1)}, u32[]{:S(2)}, u32[]{:S(2)}) collective-permute-start(bf16[113,8,128]{2,1,0:T(8,128)(2,1)S(1)} %get-tuple-element.24), channel_id=1, source_target_pairs={{0,16},{8,24},{16,0},{24,8},{1,17},{9,25},{17,1},{25,9},{2,18},{10... | collective-permute-start | bytes 694280 | tf_op jit(solution)/shard_map/ppermute | solution.py:479
  5.1 0.0 collective-permute-start.6
  5.1 0.0 copy-done.1
  5.1 0.0 copy-start.4
  5.1 0.0 copy-start.3
  5.1 0.3 %shard_map.87 = (bf16[10,8,1440]{2,1,0:T(8,128)(2,1)S(1)}, bf16[10,8,1440]{2,1,0:T(8,128)(2,1)S(1)}, f32[10,8,1440]{2,1,0:T(8,128)S(1)}) custom-call(bf16[20,16,1440]{2,1,0:T(8,128)(2,1)S(1)} %bitcast.8, bf16[10,16,1440]{2,1,0:T(8,128)(2,1)S(1)} %bitcast.9), custom_call_target="tpu_custom_call" | custom-call | flops 100000000 | tf_op jit(solution)/shard_map/pallas_call | solution.py:444
  5.4 0.0 copy-start.2
  5.4 1.1 %collective-permute-start.4 = (bf16[10,8,1440]{2,1,0:T(8,128)(2,1)S(1)}, bf16[10,8,1440]{2,1,0:T(8,128)(2,1)S(1)}, u32[]{:S(2)}, u32[]{:S(2)}) collective-permute-start(bf16[10,8,1440]{2,1,0:T(8,128)(2,1)S(1)} %get-tuple-element.18), channel_id=1, source_target_pairs={{0,8},{8,0},{16,24},{24,16},{1,9},{9,1},{17,25},{25,17},{2,10},{10... | collective-permute-start | bytes 691208 | tf_op jit(solution)/shard_map/ppermute | solution.py:491
  6.5 0.0 copy-done.4
  6.6 0.0 copy-done.3
  6.6 0.1 convert_select_fusion.lon_ref
  6.6 0.0 collective-permute-done
  6.6 0.0 copy-done.2
  6.7 0.1 shard_map.86
  6.8 0.0 copy-start.6
  6.8 3.8 %collective-permute-start.2 = (bf16[40,2,360]{2,1,0:T(2,128)(2,1)S(1)}, bf16[40,2,360]{2,1,0:T(2,128)(2,1)S(1)}, u32[]{:S(2)}, u32[]{:S(2)}) collective-permute-start(bf16[40,2,360]{2,1,0:T(2,128)(2,1)S(1)} %get-tuple-element.17), channel_id=1, source_target_pairs={{0,1},{1,2},{2,3},{3,4},{4,5},{5,6},{6,7},{8,9},{9,10},{10,11},{11... | collective-permute-start | bytes 172808 | tf_op jit(solution)/shard_map/ppermute | solution.py:511
  10.6 0.0 copy-done.6
  10.6 0.0 copy-start.5
  10.6 0.1 collective-permute-start.1
  10.7 1.7 %collective-permute-done.2.halo_ref = bf16[40,2,360]{2,1,0:T(2,128)(2,1)S(1)} collective-permute-done((bf16[40,2,360]{2,1,0:T(2,128)(2,1)S(1)}, bf16[40,2,360]{2,1,0:T(2,128)(2,1)S(1)}, u32[]{:S(2)}, u32[]{:S(2)}) %collective-permute-start.2) | collective-permute-done | bytes 57632 | tf_op jit(solution)/shard_map/ppermute | solution.py:511
  12.4 0.0 collective-permute-start.3
  12.4 0.0 copy-done.5
  12.4 0.9 %shard_map.89 = (f32[2,10,8,1440]{3,2,1,0:T(8,128)S(1)}, f32[80,1440]{1,0:T(8,128)S(1)}, bf16[6,256,256]{2,1,0:T(8,128)(2,1)S(1)}) custom-call(bf16[40,4,360]{2,1,0:T(4,128)(2,1)S(1)} %get-tuple-element.16.coarse_ref, bf16[40,2,360]{2,1,0:T(2,128)(2,1)S(1)} %collective-permute-done.2.halo_ref, bf16[10,8,1440]{2,1,0:T(8,128)(2,1)S(1)} %get-tuple-element.20.truth_ref, ...), custom_call_target="tpu_custom_call" | custom-call | tf_op jit(solution)/shard_map/pallas_call | solution.py:444
  13.3 0.4 %collective-permute-done.3.halo_ref = bf16[40,2,360]{2,1,0:T(2,128)(2,1)S(1)} collective-permute-done((bf16[40,2,360]{2,1,0:T(2,128)(2,1)S(1)}, bf16[40,2,360]{2,1,0:T(2,128)(2,1)S(1)}, u32[]{:S(2)}, u32[]{:S(2)}) %collective-permute-start.3) | collective-permute-done | bytes 57632 | tf_op jit(solution)/shard_map/ppermute | solution.py:513
  13.7 0.0 collective-permute-done.1.coarse_ref
  13.7 0.0 collective-permute-done.4.truth_ref
  13.7 0.0 collective-permute-done.5.straight_ref
  13.7 0.8 %shard_map.91 = (f32[2,10,8,1440]{3,2,1,0:T(8,128)S(1)}, f32[80,1440]{1,0:T(8,128)S(1)}) custom-call(bf16[40,4,360]{2,1,0:T(4,128)(2,1)S(1)} %collective-permute-done.1.coarse_ref, bf16[40,2,360]{2,1,0:T(2,128)(2,1)S(1)} %collective-permute-done.3.halo_ref, bf16[10,8,1440]{2,1,0:T(8,128)(2,1)S(1)} %collective-permute-done.4.truth_ref, ...), custom_call_target="tpu_custom_call" | custom-call | tf_op jit(solution)/shard_map/pallas_call | solution.py:444
  14.5 1.0 %collective-permute-done.6.crossed_ref = bf16[113,8,128]{2,1,0:T(8,128)(2,1)S(1)} collective-permute-done((bf16[113,8,128]{2,1,0:T(8,128)(2,1)S(1)}, bf16[113,8,128]{2,1,0:T(8,128)(2,1)S(1)}, u32[]{:S(2)}, u32[]{:S(2)}) %collective-permute-start.6) | collective-permute-done | bytes 231456 | tf_op jit(solution)/shard_map/ppermute | solution.py:480
  15.5 1.0 %shard_map.92 = (f32[10,4,1440]{2,1,0:T(4,128)}, f32[10,4,1440]{2,1,0:T(4,128)}) custom-call(f32[2,10,8,1440]{3,2,1,0:T(8,128)S(1)} %get-tuple-element.25.before_ref, f32[80,1440]{1,0:T(8,128)S(1)} %get-tuple-element.26.fine_ref, bf16[113,8,128]{2,1,0:T(8,128)(2,1)S(1)} %collective-permute-done.6.crossed_ref, f32[10,8,1440]{2,1,0:T(8,128)S(1)} %get-tuple-element.19.normals_ref), custom_call_target="tpu_custom_call" | custom-call | tf_op jit(solution)/shard_map/pallas_call | solution.py:444
  (6 shorter events, 0.0 us)
Async XLA Ops:
  0.6 3.0 %copy-start = (bf16[2,2,5,16,1440]{4,3,2,1,0:T(8,128)(2,1)S(1)}, bf16[2,2,5,16,1440]{4,3,2,1,0:T(8,128)(2,1)}, u32[]{:S(2)}) copy-start(bf16[2,2,5,16,1440]{4,3,2,1,0:T(8,128)(2,1)} %param.8) | copy-start | bytes 2764804
  0.6 6.0 %collective-permute-start = (bf16[2,2,5,4,360]{4,3,2,1,0:T(4,128)(2,1)}, bf16[2,2,5,4,360]{4,3,2,1,0:T(4,128)(2,1)S(1)}, u32[]{:S(2)}, u32[]{:S(2)}) collective-permute-start(bf16[2,2,5,4,360]{4,3,2,1,0:T(4,128)(2,1)} %param.7), channel_id=1, source_target_pairs={{0,16},{8,24},{16,0},{24,8},{1,17},{9,25},{17,1},{25,9},{2,18},{10... | collective-permute-start | bytes 172808 | tf_op jit(solution)/shard_map/ppermute | solution.py:473
  3.7 1.4 %copy-start.1 = (bf16[2,5,16,1440]{3,2,1,0:T(8,128)(2,1)S(1)}, bf16[2,5,16,1440]{3,2,1,0:T(8,128)(2,1)}, u32[]{:S(2)}) copy-start(bf16[2,5,16,1440]{3,2,1,0:T(8,128)(2,1)} %param.9) | copy-start | bytes 1382404
  3.9 9.8 %collective-permute-start.5 = (bf16[113,8,128]{2,1,0:T(8,128)(2,1)S(1)}, bf16[113,8,128]{2,1,0:T(8,128)(2,1)S(1)}, u32[]{:S(2)}, u32[]{:S(2)}) collective-permute-start(bf16[113,8,128]{2,1,0:T(8,128)(2,1)S(1)} %get-tuple-element.24), channel_id=1, source_target_pairs={{0,16},{8,24},{16,0},{24,8},{1,17},{9,25},{17,1},{25,9},{2,18},{10... | collective-permute-start | bytes 694280 | tf_op jit(solution)/shard_map/ppermute | solution.py:479
  5.1 10.4 %collective-permute-start.6 = (bf16[113,8,128]{2,1,0:T(8,128)(2,1)S(1)}, bf16[113,8,128]{2,1,0:T(8,128)(2,1)S(1)}, u32[]{:S(2)}, u32[]{:S(2)}) collective-permute-start(bf16[113,8,128]{2,1,0:T(8,128)(2,1)S(1)} %get-tuple-element.27), channel_id=1, source_target_pairs={{0,24},{8,16},{16,8},{24,0},{1,25},{9,17},{17,9},{25,1},{2,26},{10... | collective-permute-start | bytes 694280 | tf_op jit(solution)/shard_map/ppermute | solution.py:480
  5.1 1.5 %copy-start.4 = (s32[1440]{0:T(1024)S(1)}, s32[1440]{0:T(1024)}, u32[]{:S(2)}) copy-start(s32[1440]{0:T(1024)} %param.12) | copy-start | bytes 17284
  5.1 1.5 %copy-start.3 = (bf16[4,1440]{1,0:T(4,128)(2,1)S(1)}, bf16[4,1440]{1,0:T(4,128)(2,1)}, u32[]{:S(2)}) copy-start(bf16[4,1440]{1,0:T(4,128)(2,1)} %param.13) | copy-start | bytes 34564
  5.4 1.2 %copy-start.2 = (bf16[2,2,5,4,360]{4,3,2,1,0:T(4,128)(2,1)S(1)}, bf16[2,2,5,4,360]{4,3,2,1,0:T(4,128)(2,1)}, u32[]{:S(2)}) copy-start(bf16[2,2,5,4,360]{4,3,2,1,0:T(4,128)(2,1)} %param.7) | copy-start | bytes 172804
  5.4 8.2 %collective-permute-start.4 = (bf16[10,8,1440]{2,1,0:T(8,128)(2,1)S(1)}, bf16[10,8,1440]{2,1,0:T(8,128)(2,1)S(1)}, u32[]{:S(2)}, u32[]{:S(2)}) collective-permute-start(bf16[10,8,1440]{2,1,0:T(8,128)(2,1)S(1)} %get-tuple-element.18), channel_id=1, source_target_pairs={{0,8},{8,0},{16,24},{24,16},{1,9},{9,1},{17,25},{25,17},{2,10},{10... | collective-permute-start | bytes 691208 | tf_op jit(solution)/shard_map/ppermute | solution.py:491
  6.8 3.8 %copy-start.6 = (s32[16]{0:T(128)S(1)}, s32[16]{0:T(128)}, u32[]{:S(2)}) copy-start(s32[16]{0:T(128)} %param.10) | copy-start | bytes 196
  6.8 5.7 %collective-permute-start.2 = (bf16[40,2,360]{2,1,0:T(2,128)(2,1)S(1)}, bf16[40,2,360]{2,1,0:T(2,128)(2,1)S(1)}, u32[]{:S(2)}, u32[]{:S(2)}) collective-permute-start(bf16[40,2,360]{2,1,0:T(2,128)(2,1)S(1)} %get-tuple-element.17), channel_id=1, source_target_pairs={{0,1},{1,2},{2,3},{3,4},{4,5},{5,6},{6,7},{8,9},{9,10},{10,11},{11... | collective-permute-start | bytes 172808 | tf_op jit(solution)/shard_map/ppermute | solution.py:511
  10.6 1.8 %copy-start.5 = (f32[16,4]{0,1:T(4,128)S(1)}, f32[16,4]{0,1:T(4,128)}, u32[]{:S(2)}) copy-start(f32[16,4]{0,1:T(4,128)} %param.11) | copy-start | bytes 772
  10.6 3.0 %collective-permute-start.1 = (bf16[40,4,360]{2,1,0:T(4,128)(2,1)S(1)}, bf16[40,4,360]{2,1,0:T(4,128)(2,1)S(1)}, u32[]{:S(2)}, u32[]{:S(2)}) collective-permute-start(bf16[40,4,360]{2,1,0:T(4,128)(2,1)S(1)} %get-tuple-element.16.coarse_ref), channel_id=1, source_target_pairs={{0,8},{8,0},{16,24},{24,16},{1,9},{9,1},{17,25},{25,17},{2,10},{10... | collective-permute-start | bytes 345608 | tf_op jit(solution)/shard_map/ppermute | solution.py:512
  12.4 1.2 %collective-permute-start.3 = (bf16[40,2,360]{2,1,0:T(2,128)(2,1)S(1)}, bf16[40,2,360]{2,1,0:T(2,128)(2,1)S(1)}, u32[]{:S(2)}, u32[]{:S(2)}) collective-permute-start(bf16[40,2,360]{2,1,0:T(2,128)(2,1)S(1)} %collective-permute-done.2.halo_ref), channel_id=1, source_target_pairs={{0,8},{8,0},{16,24},{24,16},{1,9},{9,1},{17,25},{25,17},{2,10},{10... | collective-permute-start | bytes 172808 | tf_op jit(solution)/shard_map/ppermute | solution.py:513

commit v2 on v1

--- a/solution.py
+++ b/solution.py
@@ -275,29 +275,36 @@
     return jnp.concatenate(parts, axis=1)
 
 
-def away_kernel(dates, truth_ref, _, straight_ref, crossed_ref):
-    pairs = truth_ref.shape[0] // dates
+def tile_entries(pairs, dates):
+    return [[date * pairs + pair, date * pairs + pair + 1] for pair in range(0, pairs, 2) for date in range(dates)]
+
+
+def straight_kernel(dates, truth_ref, own_ref, _, out_ref, kept_ref):
     first = first_core()
-    straight, crossed = [], []
-    for pair in range(pairs):
-        entries = [date * pairs + pair for date in range(dates)]
+    blocks = []
+    for entries in tile_entries(truth_ref.shape[0] // dates, dates):
         one, two = by_owner(truth_ref, entries, jnp.logical_not(lower_chip()))
-        straight.append(jnp.where(first, one, two))
-        crossed.append(jnp.where(first, two, one))
-    pack_rows(straight, straight_ref)
-    pack_rows(crossed, crossed_ref)
-
-
-def home_kernel(dates, truth_ref, normal_ref, mine_ref, sibling_ref, normals_ref):
+        blocks.append(jnp.where(first, one, two))
+    pack_rows(blocks, out_ref)
+    for index in range(own_ref.shape[0]):
+        kept_ref[index] = own_ref[index]
+
+
+def home_kernel(dates, truth_ref, normal_ref, _, crossed_ref, mine_ref, sibling_ref, normals_ref):
     pairs = normal_ref.shape[0]
     first = first_core()
     lower = lower_chip()
-    for pair in range(pairs):
-        one, two = by_owner(truth_ref, [date * pairs + pair for date in range(dates)], lower)
-        mine_ref[pair] = jnp.where(first, one, two).astype(mine_ref.dtype)
-        sibling_ref[pair] = jnp.where(first, two, one).astype(sibling_ref.dtype)
-        one, two = by_owner(normal_ref, [pair] * dates, lower)
-        normals_ref[pair] = jnp.where(first, one, two)
+    crossed = []
+    for at, entries in enumerate(tile_entries(pairs, dates)):
+        one, two = by_owner(truth_ref, entries, jnp.logical_not(lower))
+        crossed.append(jnp.where(first, two, one))
+        one, two = by_owner(truth_ref, entries, lower)
+        mine_ref[at] = jnp.where(first, one, two).astype(mine_ref.dtype)
+        sibling_ref[at] = jnp.where(first, two, one).astype(sibling_ref.dtype)
+    pack_rows(crossed, crossed_ref)
+    for pair in range(0, pairs, 2):
+        one, two = by_owner(normal_ref, [pair, pair + 1], lower)
+        normals_ref[pair // 2] = jnp.where(first, one, two)
 
 
 def shift_rows_kernel(own_ref, peer_ref, both_ref, rows_ref):
@@ -310,12 +317,12 @@
         rows_ref[index] = jnp.where(lower, block[coarse_rows - 2 :], block[:2]).astype(jnp.bfloat16)
 
 
-def latitude_step(pairs, coarse_ref, halo_ref, lat_ref, lhs_ref, stage_ref):
+def latitude_step(dates, coarse_ref, halo_ref, lat_ref, lhs_ref):
     fields = coarse_ref.shape[0] // 2
-    dates = fields // pairs
+    pairs = fields // dates
     depth = lhs_ref.shape[2]
-    rows = lhs_ref.shape[1] // (2 * pairs)
-    owned = rows // dates
+    rows = 2 * lhs_ref.shape[1] // (2 * fields)
+    owned = rows // 2
     band = lax.axis_index("band")
     lower = lower_chip()
     first = first_core()
@@ -326,14 +333,16 @@
     weights = lat_ref[...].T
     weights = jnp.where(lower, weights[: 2 * owned], weights[2 * owned : 4 * owned])
     weights = jnp.where(first, weights[:owned], weights[owned:])
-    weights = jnp.concatenate([weights] * dates, axis=0)
+    weights = jnp.concatenate([weights, weights], axis=0)
     lat = [jnp.broadcast_to(weights[:, tap : tap + 1], (rows, depth)) for tap in range(TAPS + 1)]
-    date_of_row = lax.broadcasted_iota(jnp.int32, (rows, depth), 0) // owned
+    first_pair = lax.broadcasted_iota(jnp.int32, (rows, depth), 0) < owned
+    pending = []
+    at = 0
     for side in range(2):
-        for pair in range(pairs):
+        for entries in tile_entries(pairs, dates):
             sources = []
-            for date in range(dates):
-                index = side * fields + date * pairs + pair
+            for entry in entries:
+                index = side * fields + entry
                 inner = coarse_ref[index].astype(jnp.float32)
                 edge = jnp.where(outside, 0.0, halo_ref[index].astype(jnp.float32))
                 below = jnp.concatenate([edge, inner], axis=0)
@@ -342,17 +351,16 @@
                 sources.append(jnp.where(first, wrapped[: TAPS + 1], wrapped[1 : TAPS + 2]))
             total = 0.0
             for tap in range(TAPS + 1):
-                mixed = jnp.broadcast_to(sources[0][tap : tap + 1], (rows, depth))
-                for date in range(1, dates):
-                    spread = jnp.broadcast_to(sources[date][tap : tap + 1], (rows, depth))
-                    mixed = jnp.where(date_of_row == date, spread, mixed)
-                total = total + lat[tap] * mixed
-            upper = total.astype(jnp.bfloat16).astype(jnp.float32)
-            at = (side * pairs + pair) * rows
-            stage_ref[at : at + rows, :depth] = upper
-            stage_ref[at : at + rows, depth:] = total - upper
-    lhs_ref[0] = stage_ref[:, :depth].astype(jnp.bfloat16)
-    lhs_ref[1] = stage_ref[:, depth:].astype(jnp.bfloat16)
+                one, two = [jnp.broadcast_to(source[tap : tap + 1], (rows, depth)) for source in sources]
+                total = total + lat[tap] * jnp.where(first_pair, one, two)
+            pending.append(total)
+            at += rows
+            if len(pending) * rows == 16:
+                block = jnp.concatenate(pending, axis=0)
+                upper = block.astype(jnp.bfloat16)
+                lhs_ref[0, at - 16 : at] = upper
+                lhs_ref[1, at - 16 : at] = (block - upper.astype(jnp.float32)).astype(jnp.bfloat16)
+                pending = []
 
 
 def column_blocks(dense):
@@ -373,24 +381,24 @@
     truth_ref,
     normals_ref,
     lat_ref,
-    tap_ref,
-    lon_ref,
+    table_ref,
     sums_ref,
     away_ref,
-    table_ref,
     lhs_ref,
-    stage_ref,
+    fine_ref,
 ):
-    pairs, rows, dense = truth_ref.shape
-    fill_tables(tap_ref, lon_ref, table_ref)
-    latitude_step(pairs, coarse_ref, halo_ref, lat_ref, lhs_ref, stage_ref)
+    tiles, rows, dense = truth_ref.shape
+    dates = tiles // normals_ref.shape[0]
+    latitude_step(dates, coarse_ref, halo_ref, lat_ref, lhs_ref)
     for tile, low_x, width, columns in column_blocks(dense):
-        stage_ref[:, :width] = widened(lhs_ref, table_ref, tile, low_x, width)
-        away_ref[:, columns] = stage_ref[pairs * rows :, :width]
-        for pair in range(pairs):
-            fine = stage_ref[pair * rows : (pair + 1) * rows, :width]
-            actual = truth_ref[pair, :, columns].astype(jnp.float32)
-            sums = added((0.0, 0.0), fine, actual, normals_ref[pair, :, columns])
+        fine_ref[:, :width] = widened(lhs_ref, table_ref, tile, low_x, width)
+        away_ref[:, columns] = fine_ref[tiles * rows :, :width]
+        for pair in range(normals_ref.shape[0]):
+            normal = normals_ref[pair, :, columns]
+            sums = (0.0, 0.0)
+            for at in range(pair * dates, (pair + 1) * dates):
+                actual = truth_ref[at, :, columns].astype(jnp.float32)
+                sums = added(sums, fine_ref[at * rows : (at + 1) * rows, :width], actual, normal)
             sums_ref[0, pair, :, columns], sums_ref[1, pair, :, columns] = sums
 
 
@@ -407,45 +415,58 @@
     sums_ref,
     away_ref,
     lhs_ref,
-    stage_ref,
+    fine_ref,
 ):
-    pairs, rows, dense = truth_ref.shape
-    latitude_step(pairs, coarse_ref, halo_ref, lat_ref, lhs_ref, stage_ref)
+    tiles, rows, dense = truth_ref.shape
+    dates = tiles // normals_ref.shape[0]
+    latitude_step(dates, coarse_ref, halo_ref, lat_ref, lhs_ref)
     for tile, low_x, width, columns in column_blocks(dense):
-        stage_ref[:, :width] = widened(lhs_ref, table_ref, tile, low_x, width)
-        away_ref[:, columns] = stage_ref[pairs * rows :, :width]
-        for pair in range(pairs):
-            span = slice(pair * rows, (pair + 1) * rows)
+        fine_ref[:, :width] = widened(lhs_ref, table_ref, tile, low_x, width)
+        away_ref[:, columns] = fine_ref[tiles * rows :, :width]
+        for pair in range(normals_ref.shape[0]):
             normal = normals_ref[pair, :, columns]
             sums = (before_ref[0, pair, :, columns], before_ref[1, pair, :, columns])
-            actual = truth_ref[pair, :, columns].astype(jnp.float32)
-            sums = added(sums, stage_ref[span, :width], actual, normal)
-            actual = unpacked_rows(straight_ref, pair, pairs, dense, low_x, width)
-            sums = added(sums, straight_fine_ref[span, columns], actual, normal)
+            for at in range(pair * dates, (pair + 1) * dates):
+                span = slice(at * rows, (at + 1) * rows)
+                actual = truth_ref[at, :, columns].astype(jnp.float32)
+                sums = added(sums, fine_ref[span, :width], actual, normal)
+                actual = unpacked_rows(straight_ref, at, tiles, dense, low_x, width)
+                sums = added(sums, straight_fine_ref[span, columns], actual, normal)
             sums_ref[0, pair, :, columns], sums_ref[1, pair, :, columns] = sums
 
 
-def mean_kernel(dates, count, before_ref, fine_ref, crossed_ref, normals_ref, *results):
-    pairs, rows, dense = normals_ref.shape
-    owned = rows // dates
-    for _, low_x, width, columns in column_blocks(dense):
-        for pair in range(pairs):
+def mean_kernel(dates, count, before_ref, fine_ref, crossed_ref, normals_ref, *refs):
+    *results, held_ref, sems = refs
+    tiles, rows, dense = normals_ref.shape
+    owned = rows // 2
+    copies = []
+    for pair in range(tiles):
+        for _, low_x, width, columns in column_blocks(dense):
+            normal = normals_ref[pair, :, columns]
             sums = (before_ref[0, pair, :, columns], before_ref[1, pair, :, columns])
-            actual = unpacked_rows(crossed_ref, pair, pairs, dense, low_x, width)
-            fine = fine_ref[pair * rows : (pair + 1) * rows, columns]
-            sums = added(sums, fine, actual, normals_ref[pair, :, columns])
-            for total, out_ref in zip(sums, results):
-                parts = [total[date * owned : (date + 1) * owned] for date in range(dates)]
-                out_ref[pair, :, columns] = sum(parts[1:], parts[0]) / count
-
-
-def kernel_call(kernel, out_shape, scratch, megabytes, flops, *operands):
+            for at in range(pair * dates, (pair + 1) * dates):
+                actual = unpacked_rows(crossed_ref, at, tiles * dates, dense, low_x, width)
+                sums = added(sums, fine_ref[at * rows : (at + 1) * rows, columns], actual, normal)
+            for kind, total in enumerate(sums):
+                total = total * (1.0 / count)
+                held_ref[kind, 2 * pair, :, columns] = total[:owned]
+                held_ref[kind, 2 * pair + 1, :, columns] = total[owned:]
+        done = pl.ds(2 * pair, 2)
+        for kind, out_ref in enumerate(results):
+            copy = pltpu.make_async_copy(held_ref.at[kind, done], out_ref.at[done], sems.at[len(copies)])
+            copy.start()
+            copies.append(copy)
+    for copy in copies:
+        copy.wait()
+
+
+def kernel_call(kernel, out_shape, scratch, megabytes, flops, *operands, out_space=pltpu.VMEM):
     vmem = pl.BlockSpec(memory_space=pltpu.VMEM)
     return pl.pallas_call(
         kernel,
         out_shape=out_shape,
         in_specs=[vmem] * len(operands),
-        out_specs=[vmem] * len(out_shape),
+        out_specs=[pl.BlockSpec(memory_space=out_space)] * len(out_shape),
         scratch_shapes=scratch,
         compiler_params=pltpu.CompilerParams(vmem_limit_bytes=megabytes * 1024 * 1024),
         cost_estimate=pl.CostEstimate(flops=flops, bytes_accessed=0, transcendentals=0),
@@ -458,9 +479,10 @@
     dates, leads, variables, coarse_rows, sparse = model_prognosis.shape
     fine_rows, dense = analysis_truth.shape[3:]
     owned = fine_rows // groups
-    rows = dates * owned
+    rows = 2 * owned
     pairs = leads * variables
     fields = dates * pairs
+    tiles = fields // 2
     depth = pl.cdiv(sparse + 4, LANES) * LANES
     float32, bfloat16 = jnp.float32, jnp.bfloat16
     straight_way = [(i, (i + 2) % groups) for i in range(groups)]
@@ -472,22 +494,30 @@
     normal = expected_normal.reshape(pairs, fine_rows, dense)
     peer = lax.ppermute(model_prognosis, "date", straight_way).reshape(own.shape)
 
-    packed = jax.ShapeDtypeStruct((packed_tiles(pairs, dense), rows, LANES), bfloat16)
-    straight, crossed = kernel_call(
-        functools.partial(away_kernel, dates), [packed, packed], [], 8, 100_000_000, truth, taps
+    packed = jax.ShapeDtypeStruct((packed_tiles(tiles, dense), rows, LANES), bfloat16)
+    straight, own = kernel_call(
+        functools.partial(straight_kernel, dates),
+        [packed, jax.ShapeDtypeStruct(own.shape, own.dtype)],
+        [],
+        8,
+        100_000_000,
+        truth,
+        own,
+        taps,
     )
     straight = lax.ppermute(straight, "date", straight_way)
-    crossed = lax.ppermute(crossed, "date", crossed_way)
-    plain = jax.ShapeDtypeStruct((pairs, rows, dense), bfloat16)
-    mine, sibling, normals = kernel_call(
+    plain = jax.ShapeDtypeStruct((tiles, rows, dense), bfloat16)
+    crossed, mine, sibling, normals = kernel_call(
         functools.partial(home_kernel, dates),
-        [plain, plain, jax.ShapeDtypeStruct((pairs, rows, dense), float32)],
+        [packed, plain, plain, jax.ShapeDtypeStruct((pairs // 2, rows, dense), float32)],
         [],
         12,
         100_000_000,
         truth,
         normal,
-    )
+        own,
+    )
+    crossed = lax.ppermute(crossed, "date", crossed_way)
     sibling = lax.ppermute(sibling, "date", sibling_way)
 
     chain = []
@@ -512,16 +542,17 @@
     sibling_coarse = lax.ppermute(coarse, "date", sibling_way)
     sibling_halo = lax.ppermute(halo, "date", sibling_way)
 
-    sums = jax.ShapeDtypeStruct((2, pairs, rows, dense), float32)
-    away = jax.ShapeDtypeStruct((pairs * rows, dense), float32)
+    sums = jax.ShapeDtypeStruct((2, pairs // 2, rows, dense), float32)
+    away = jax.ShapeDtypeStruct((tiles * rows, dense), float32)
     table = jax.ShapeDtypeStruct((pl.cdiv(dense, WIDE), 2 * LANES, WIDE), bfloat16)
     scratch = [
-        pltpu.VMEM((2, 2 * pairs * rows, depth), bfloat16),
-        pltpu.VMEM((2 * pairs * rows, 2 * depth), float32),
+        pltpu.VMEM((2, 2 * tiles * rows, depth), bfloat16),
+        pltpu.VMEM((2 * tiles * rows, WIDE), float32),
     ]
-    own_sums, straight_fine, table = kernel_call(
+    (table,) = kernel_call(fill_tables, [table], [], 8, 4_000_000_000, taps, lon_weights)
+    own_sums, straight_fine = kernel_call(
         own_dates_kernel,
-        [sums, away, table],
+        [sums, away],
         scratch,
         20,
         0,
@@ -530,8 +561,7 @@
         mine,
         normals,
         lat_weights,
-        taps,
-        lon_weights,
+        table,
     )
     chip_sums, crossed_fine = kernel_call(
         sibling_dates_kernel,
@@ -553,13 +583,14 @@
     results = kernel_call(
         functools.partial(mean_kernel, dates, dates * groups),
         [out, out],
-        [],
+        [pltpu.VMEM((2,) + out.shape, float32), pltpu.SemaphoreType.DMA((pairs,))],
         16,
         0,
         chip_sums,
         crossed_fine,
         crossed,
         normals,
+        out_space=pl.ANY,
     )
     return tuple(result.reshape(leads, variables, owned, dense) for result in results)
 
@@ -598,7 +629,8 @@
     (taps,) = kernel_call(
         taps_kernel, [jax.ShapeDtypeStruct((WIDE // 4 + 8, WIDE), jnp.int32)], [], 8, 2_000_000_000
     )
-    if halves == 2 and dates * analysis_truth.shape[3] == 8 * groups:
+    tall = 2 * analysis_truth.shape[3] == 8 * groups
+    if halves == 2 and tall and expected_normal.shape[0] * expected_normal.shape[1] % 2 == 0:
         return two_chip_maps(model_prognosis, analysis_truth, expected_normal, taps, lon_weights, lat_weights)
 
     own = model_prognosis.reshape((-1,) + model_prognosis.shape[3:])

time: 16.8 us -> 16.6 us (0.988)
  starting transfers between devices: 9.14 us -> 8.86 us
  waiting for transfers between devices: 3.09 us -> 3.33 us
    ppermute x1, starting transfers between devices: 3.81 us -> 3.51 us  [two_chip_maps(): halo = lax.ppermute(edges, ('date', 'band'), chain)]
    ppermute x1, starting transfers between devices: 1.1 us -> 0.85 us  [two_chip_maps(): sibling = lax.ppermute(sibling, 'date', sibling_way)]
    ppermute x1, starting transfers between devices: 0.01 us -> 0.25 us  [two_chip_maps(): crossed = lax.ppermute(crossed, 'date', crossed_way)]
    ppermute x1, waiting for transfers between devices: 0.36 us -> 0.56 us  [two_chip_maps(): sibling_halo = lax.ppermute(halo, 'date', sibling_way)]
    pallas_call x7 -> x8, Pallas kernels: 3.39 us -> 3.31 us  [kernel_call(): pl.pallas_call(kernel, out_shape=out_shape, in_specs=[vmem] * len(operand...]
where the time goes in v2:
time: 16.6 us; the launch traced here: 16.5 us
  starting transfers between devices  8.86 us (53%)
  waiting for transfers between devices  3.33 us (20%)
  Pallas kernels  3.31 us (20%)
  between operations  0.8 us (5%)
    ppermute x1, starting transfers between devices, two_chip_maps(): halo = lax.ppermute(edges, ('date', 'band'), chain)  3.51 us
    pallas_call x8, Pallas kernels, kernel_call(): pl.pallas_call(kernel, out_shape=out_shape, in_specs=[vmem] * len(operand...  3.31 us
    ppermute x1, starting transfers between devices, two_chip_maps(): lax.ppermute(model_prognosis, 'date', straight_way).reshape(own.shape)  3 us
    ppermute x1, waiting for transfers between devices, two_chip_maps(): halo = lax.ppermute(edges, ('date', 'band'), chain)  1.71 us
    ppermute x1, starting transfers between devices, two_chip_maps(): straight = lax.ppermute(straight, 'date', straight_way)  1.17 us
    ppermute x1, waiting for transfers between devices, two_chip_maps(): crossed = lax.ppermute(crossed, 'date', crossed_way)  1.05 us
    ppermute x1, starting transfers between devices, two_chip_maps(): sibling = lax.ppermute(sibling, 'date', sibling_way)  0.85 us
    ppermute x1, waiting for transfers between devices, two_chip_maps(): sibling_halo = lax.ppermute(halo, 'date', sibling_way)  0.56 us
  transfers between devices with their start and end apart: 7, of which 3 were waited for; matrix products, arithmetic and copies ran while one was open for 1% of the time, Pallas kernels for 14%

profile of v2, /device:TPU:0, one launch (start us, length us, event | category | flops | bytes accessed | tf_op | source)
XLA Modules:
  0.0 16.5 jit_solution(15999699185216217075)
XLA Ops:
  0.6 0.0 copy-start.2
  0.6 0.0 copy-start
  0.6 3.0 %collective-permute-start = (bf16[2,2,5,4,360]{4,3,2,1,0:T(4,128)(2,1)}, bf16[2,2,5,4,360]{4,3,2,1,0:T(4,128)(2,1)S(1)}, u32[]{:S(2)}, u32[]{:S(2)}) collective-permute-start(bf16[2,2,5,4,360]{4,3,2,1,0:T(4,128)(2,1)} %param.7), channel_id=1, source_target_pairs={{0,16},{8,24},{16,0},{24,8},{1,17},{9,25},{17,1},{25,9},{2,18},{10... | collective-permute-start | bytes 172808 | tf_op jit(solution)/shard_map/ppermute | solution.py:495
  3.7 0.0 copy-done.2
  3.7 0.0 copy-done
  3.7 0.0 copy-start.1
  3.7 0.2 %shard_map.87 = (bf16[113,8,128]{2,1,0:T(8,128)(2,1)S(1)}, bf16[20,4,360]{2,1,0:T(4,128)(2,1)S(1)}) custom-call(bf16[20,16,1440]{2,1,0:T(8,128)(2,1)S(1)} %bitcast.7, bf16[20,4,360]{2,1,0:T(4,128)(2,1)S(1)} %bitcast.10, s32[72,256]{1,0:T(8,128)S(1)} %shard_map.86._.tap_ref), custom_call_target="tpu_custom_call" | custom-call | flops 100000000 | tf_op jit(solution)/shard_map/pallas_call | solution.py:465
  3.9 1.2 %collective-permute-start.5 = (bf16[113,8,128]{2,1,0:T(8,128)(2,1)S(1)}, bf16[113,8,128]{2,1,0:T(8,128)(2,1)S(1)}, u32[]{:S(2)}, u32[]{:S(2)}) collective-permute-start(bf16[113,8,128]{2,1,0:T(8,128)(2,1)S(1)} %get-tuple-element.24), channel_id=1, source_target_pairs={{0,16},{8,24},{16,0},{24,8},{1,17},{9,25},{17,1},{25,9},{2,18},{10... | collective-permute-start | bytes 694280 | tf_op jit(solution)/shard_map/ppermute | solution.py:508
  5.1 0.0 copy-done.1
  5.1 0.0 copy-start.4
  5.1 0.5 %shard_map.89 = (bf16[113,8,128]{2,1,0:T(8,128)(2,1)S(1)}, bf16[10,8,1440]{2,1,0:T(8,128)(2,1)S(1)}, bf16[10,8,1440]{2,1,0:T(8,128)(2,1)S(1)}, f32[5,8,1440]{2,1,0:T(8,128)S(1)}) custom-call(bf16[20,16,1440]{2,1,0:T(8,128)(2,1)S(1)} %bitcast.8, bf16[10,16,1440]{2,1,0:T(8,128)(2,1)S(1)} %bitcast.9, bf16[20,4,360]{2,1,0:T(4,128)(2,1)S(1)} %get-tuple-element.16.own_ref._), custom_call_target="tpu_custom_call" | custom-call | flops 100000000 | tf_op jit(solution)/shard_map/pallas_call | solution.py:465
  5.6 0.0 copy-start.3
  5.6 0.3 %collective-permute-start.6 = (bf16[113,8,128]{2,1,0:T(8,128)(2,1)S(1)}, bf16[113,8,128]{2,1,0:T(8,128)(2,1)S(1)}, u32[]{:S(2)}, u32[]{:S(2)}) collective-permute-start(bf16[113,8,128]{2,1,0:T(8,128)(2,1)S(1)} %get-tuple-element.27), channel_id=1, source_target_pairs={{0,24},{8,16},{16,8},{24,0},{1,25},{9,17},{17,9},{25,1},{2,26},{10... | collective-permute-start | bytes 694280 | tf_op jit(solution)/shard_map/ppermute | solution.py:520
  5.9 0.9 %collective-permute-start.4 = (bf16[10,8,1440]{2,1,0:T(8,128)(2,1)S(1)}, bf16[10,8,1440]{2,1,0:T(8,128)(2,1)S(1)}, u32[]{:S(2)}, u32[]{:S(2)}) collective-permute-start(bf16[10,8,1440]{2,1,0:T(8,128)(2,1)S(1)} %get-tuple-element.19), channel_id=1, source_target_pairs={{0,8},{8,0},{16,24},{24,16},{1,9},{9,1},{17,25},{25,17},{2,10},{10... | collective-permute-start | bytes 691208 | tf_op jit(solution)/shard_map/ppermute | solution.py:521
  6.7 0.0 copy-done.4
  6.7 0.0 copy-done.3
  6.7 0.1 convert_select_fusion.lon_ref
  6.8 0.1 shard_map.90.table_ref
  7.0 0.0 collective-permute-done
  7.0 0.1 shard_map.88
  7.1 0.0 copy-start.6
  7.1 3.5 %collective-permute-start.2 = (bf16[40,2,360]{2,1,0:T(2,128)(2,1)S(1)}, bf16[40,2,360]{2,1,0:T(2,128)(2,1)S(1)}, u32[]{:S(2)}, u32[]{:S(2)}) collective-permute-start(bf16[40,2,360]{2,1,0:T(2,128)(2,1)S(1)} %get-tuple-element.18), channel_id=1, source_target_pairs={{0,1},{1,2},{2,3},{3,4},{4,5},{5,6},{6,7},{8,9},{9,10},{10,11},{11... | collective-permute-start | bytes 172808 | tf_op jit(solution)/shard_map/ppermute | solution.py:541
  10.6 0.0 copy-done.6
  10.6 0.0 copy-start.5
  10.7 0.1 collective-permute-start.1
  10.7 1.7 %collective-permute-done.2.halo_ref = bf16[40,2,360]{2,1,0:T(2,128)(2,1)S(1)} collective-permute-done((bf16[40,2,360]{2,1,0:T(2,128)(2,1)S(1)}, bf16[40,2,360]{2,1,0:T(2,128)(2,1)S(1)}, u32[]{:S(2)}, u32[]{:S(2)}) %collective-permute-start.2) | collective-permute-done | bytes 57632 | tf_op jit(solution)/shard_map/ppermute | solution.py:541
  12.4 0.0 collective-permute-start.3
  12.4 0.0 copy-done.5
  12.5 0.7 %shard_map.91 = (f32[2,5,8,1440]{3,2,1,0:T(8,128)S(1)}, f32[80,1440]{1,0:T(8,128)S(1)}) custom-call(bf16[40,4,360]{2,1,0:T(4,128)(2,1)S(1)} %get-tuple-element.17.coarse_ref, bf16[40,2,360]{2,1,0:T(2,128)(2,1)S(1)} %collective-permute-done.2.halo_ref, bf16[10,8,1440]{2,1,0:T(8,128)(2,1)S(1)} %get-tuple-element.21.truth_ref, ...), custom_call_target="tpu_custom_call" | custom-call | tf_op jit(solution)/shard_map/pallas_call | solution.py:465
  13.1 0.6 %collective-permute-done.3.halo_ref = bf16[40,2,360]{2,1,0:T(2,128)(2,1)S(1)} collective-permute-done((bf16[40,2,360]{2,1,0:T(2,128)(2,1)S(1)}, bf16[40,2,360]{2,1,0:T(2,128)(2,1)S(1)}, u32[]{:S(2)}, u32[]{:S(2)}) %collective-permute-start.3) | collective-permute-done | bytes 57632 | tf_op jit(solution)/shard_map/ppermute | solution.py:543
  13.7 0.0 collective-permute-done.1.coarse_ref
  13.7 0.0 collective-permute-done.4.truth_ref
  13.7 0.0 collective-permute-done.5.straight_ref
  13.7 0.8 %shard_map.92 = (f32[2,5,8,1440]{3,2,1,0:T(8,128)S(1)}, f32[80,1440]{1,0:T(8,128)S(1)}) custom-call(bf16[40,4,360]{2,1,0:T(4,128)(2,1)S(1)} %collective-permute-done.1.coarse_ref, bf16[40,2,360]{2,1,0:T(2,128)(2,1)S(1)} %collective-permute-done.3.halo_ref, bf16[10,8,1440]{2,1,0:T(8,128)(2,1)S(1)} %collective-permute-done.4.truth_ref, ...), custom_call_target="tpu_custom_call" | custom-call | tf_op jit(solution)/shard_map/pallas_call | solution.py:465
  14.5 1.0 %collective-permute-done.6.crossed_ref = bf16[113,8,128]{2,1,0:T(8,128)(2,1)S(1)} collective-permute-done((bf16[113,8,128]{2,1,0:T(8,128)(2,1)S(1)}, bf16[113,8,128]{2,1,0:T(8,128)(2,1)S(1)}, u32[]{:S(2)}, u32[]{:S(2)}) %collective-permute-start.6) | collective-permute-done | bytes 231456 | tf_op jit(solution)/shard_map/ppermute | solution.py:520
  15.5 0.9 %shard_map.93 = (f32[10,4,1440]{2,1,0:T(4,128)}, f32[10,4,1440]{2,1,0:T(4,128)}) custom-call(f32[2,5,8,1440]{3,2,1,0:T(8,128)S(1)} %get-tuple-element.25.before_ref, f32[80,1440]{1,0:T(8,128)S(1)} %get-tuple-element.26.fine_ref, bf16[113,8,128]{2,1,0:T(8,128)(2,1)S(1)} %collective-permute-done.6.crossed_ref, f32[5,8,1440]{2,1,0:T(8,128)S(1)} %get-tuple-element.20.normals_ref), custom_call_target="tpu_custom_call" | custom-call | tf_op jit(solution)/shard_map/pallas_call | solution.py:465
  (6 shorter events, 0.0 us)
Async XLA Ops:
  0.6 3.0 %copy-start.2 = (bf16[2,2,5,4,360]{4,3,2,1,0:T(4,128)(2,1)S(1)}, bf16[2,2,5,4,360]{4,3,2,1,0:T(4,128)(2,1)}, u32[]{:S(2)}) copy-start(bf16[2,2,5,4,360]{4,3,2,1,0:T(4,128)(2,1)} %param.7) | copy-start | bytes 172804
  0.6 3.0 %copy-start = (bf16[2,2,5,16,1440]{4,3,2,1,0:T(8,128)(2,1)S(1)}, bf16[2,2,5,16,1440]{4,3,2,1,0:T(8,128)(2,1)}, u32[]{:S(2)}) copy-start(bf16[2,2,5,16,1440]{4,3,2,1,0:T(8,128)(2,1)} %param.8) | copy-start | bytes 2764804
  0.6 6.3 %collective-permute-start = (bf16[2,2,5,4,360]{4,3,2,1,0:T(4,128)(2,1)}, bf16[2,2,5,4,360]{4,3,2,1,0:T(4,128)(2,1)S(1)}, u32[]{:S(2)}, u32[]{:S(2)}) collective-permute-start(bf16[2,2,5,4,360]{4,3,2,1,0:T(4,128)(2,1)} %param.7), channel_id=1, source_target_pairs={{0,16},{8,24},{16,0},{24,8},{1,17},{9,25},{17,1},{25,9},{2,18},{10... | collective-permute-start | bytes 172808 | tf_op jit(solution)/shard_map/ppermute | solution.py:495
  3.7 1.4 %copy-start.1 = (bf16[2,5,16,1440]{3,2,1,0:T(8,128)(2,1)S(1)}, bf16[2,5,16,1440]{3,2,1,0:T(8,128)(2,1)}, u32[]{:S(2)}) copy-start(bf16[2,5,16,1440]{3,2,1,0:T(8,128)(2,1)} %param.9) | copy-start | bytes 1382404
  3.9 9.8 %collective-permute-start.5 = (bf16[113,8,128]{2,1,0:T(8,128)(2,1)S(1)}, bf16[113,8,128]{2,1,0:T(8,128)(2,1)S(1)}, u32[]{:S(2)}, u32[]{:S(2)}) collective-permute-start(bf16[113,8,128]{2,1,0:T(8,128)(2,1)S(1)} %get-tuple-element.24), channel_id=1, source_target_pairs={{0,16},{8,24},{16,0},{24,8},{1,17},{9,25},{17,1},{25,9},{2,18},{10... | collective-permute-start | bytes 694280 | tf_op jit(solution)/shard_map/ppermute | solution.py:508
  5.1 1.6 %copy-start.4 = (s32[1440]{0:T(1024)S(1)}, s32[1440]{0:T(1024)}, u32[]{:S(2)}) copy-start(s32[1440]{0:T(1024)} %param.12) | copy-start | bytes 17284
  5.6 1.1 %copy-start.3 = (bf16[4,1440]{1,0:T(4,128)(2,1)S(1)}, bf16[4,1440]{1,0:T(4,128)(2,1)}, u32[]{:S(2)}) copy-start(bf16[4,1440]{1,0:T(4,128)(2,1)} %param.13) | copy-start | bytes 34564
  5.6 9.9 %collective-permute-start.6 = (bf16[113,8,128]{2,1,0:T(8,128)(2,1)S(1)}, bf16[113,8,128]{2,1,0:T(8,128)(2,1)S(1)}, u32[]{:S(2)}, u32[]{:S(2)}) collective-permute-start(bf16[113,8,128]{2,1,0:T(8,128)(2,1)S(1)} %get-tuple-element.27), channel_id=1, source_target_pairs={{0,24},{8,16},{16,8},{24,0},{1,25},{9,17},{17,9},{25,1},{2,26},{10... | collective-permute-start | bytes 694280 | tf_op jit(solution)/shard_map/ppermute | solution.py:520
  5.9 7.8 %collective-permute-start.4 = (bf16[10,8,1440]{2,1,0:T(8,128)(2,1)S(1)}, bf16[10,8,1440]{2,1,0:T(8,128)(2,1)S(1)}, u32[]{:S(2)}, u32[]{:S(2)}) collective-permute-start(bf16[10,8,1440]{2,1,0:T(8,128)(2,1)S(1)} %get-tuple-element.19), channel_id=1, source_target_pairs={{0,8},{8,0},{16,24},{24,16},{1,9},{9,1},{17,25},{25,17},{2,10},{10... | collective-permute-start | bytes 691208 | tf_op jit(solution)/shard_map/ppermute | solution.py:521
  7.1 3.5 %copy-start.6 = (s32[16]{0:T(128)S(1)}, s32[16]{0:T(128)}, u32[]{:S(2)}) copy-start(s32[16]{0:T(128)} %param.10) | copy-start | bytes 196
  7.1 5.4 %collective-permute-start.2 = (bf16[40,2,360]{2,1,0:T(2,128)(2,1)S(1)}, bf16[40,2,360]{2,1,0:T(2,128)(2,1)S(1)}, u32[]{:S(2)}, u32[]{:S(2)}) collective-permute-start(bf16[40,2,360]{2,1,0:T(2,128)(2,1)S(1)} %get-tuple-element.18), channel_id=1, source_target_pairs={{0,1},{1,2},{2,3},{3,4},{4,5},{5,6},{6,7},{8,9},{9,10},{10,11},{11... | collective-permute-start | bytes 172808 | tf_op jit(solution)/shard_map/ppermute | solution.py:541
  10.6 1.8 %copy-start.5 = (f32[16,4]{0,1:T(4,128)S(1)}, f32[16,4]{0,1:T(4,128)}, u32[]{:S(2)}) copy-start(f32[16,4]{0,1:T(4,128)} %param.11) | copy-start | bytes 772
  10.7 3.0 %collective-permute-start.1 = (bf16[40,4,360]{2,1,0:T(4,128)(2,1)S(1)}, bf16[40,4,360]{2,1,0:T(4,128)(2,1)S(1)}, u32[]{:S(2)}, u32[]{:S(2)}) collective-permute-start(bf16[40,4,360]{2,1,0:T(4,128)(2,1)S(1)} %get-tuple-element.17.coarse_ref), channel_id=1, source_target_pairs={{0,8},{8,0},{16,24},{24,16},{1,9},{9,1},{17,25},{25,17},{2,10},{10... | collective-permute-start | bytes 345608 | tf_op jit(solution)/shard_map/ppermute | solution.py:542
  12.4 1.2 %collective-permute-start.3 = (bf16[40,2,360]{2,1,0:T(2,128)(2,1)S(1)}, bf16[40,2,360]{2,1,0:T(2,128)(2,1)S(1)}, u32[]{:S(2)}, u32[]{:S(2)}) collective-permute-start(bf16[40,2,360]{2,1,0:T(2,128)(2,1)S(1)} %collective-permute-done.2.halo_ref), channel_id=1, source_target_pairs={{0,8},{8,0},{16,24},{24,16},{1,9},{9,1},{17,25},{25,17},{2,10},{10... | collective-permute-start | bytes 172808 | tf_op jit(solution)/shard_map/ppermute | solution.py:543

commit v3 on v2

--- a/solution.py
+++ b/solution.py
@@ -279,29 +279,27 @@
     return [[date * pairs + pair, date * pairs + pair + 1] for pair in range(0, pairs, 2) for date in range(dates)]
 
 
-def straight_kernel(dates, truth_ref, own_ref, _, out_ref, kept_ref):
+def away_kernel(dates, truth_ref, own_ref, _, straight_ref, crossed_ref, kept_ref):
     first = first_core()
-    blocks = []
+    straight, crossed = [], []
     for entries in tile_entries(truth_ref.shape[0] // dates, dates):
         one, two = by_owner(truth_ref, entries, jnp.logical_not(lower_chip()))
-        blocks.append(jnp.where(first, one, two))
-    pack_rows(blocks, out_ref)
+        straight.append(jnp.where(first, one, two))
+        crossed.append(jnp.where(first, two, one))
+    pack_rows(straight, straight_ref)
+    pack_rows(crossed, crossed_ref)
     for index in range(own_ref.shape[0]):
         kept_ref[index] = own_ref[index]
 
 
-def home_kernel(dates, truth_ref, normal_ref, _, crossed_ref, mine_ref, sibling_ref, normals_ref):
+def home_kernel(dates, truth_ref, normal_ref, mine_ref, sibling_ref, normals_ref):
     pairs = normal_ref.shape[0]
     first = first_core()
     lower = lower_chip()
-    crossed = []
     for at, entries in enumerate(tile_entries(pairs, dates)):
-        one, two = by_owner(truth_ref, entries, jnp.logical_not(lower))
-        crossed.append(jnp.where(first, two, one))
         one, two = by_owner(truth_ref, entries, lower)
         mine_ref[at] = jnp.where(first, one, two).astype(mine_ref.dtype)
         sibling_ref[at] = jnp.where(first, two, one).astype(sibling_ref.dtype)
-    pack_rows(crossed, crossed_ref)
     for pair in range(0, pairs, 2):
         one, two = by_owner(normal_ref, [pair, pair + 1], lower)
         normals_ref[pair // 2] = jnp.where(first, one, two)
@@ -439,23 +437,42 @@
     *results, held_ref, sems = refs
     tiles, rows, dense = normals_ref.shape
     owned = rows // 2
-    copies = []
-    for pair in range(tiles):
-        for _, low_x, width, columns in column_blocks(dense):
-            normal = normals_ref[pair, :, columns]
-            sums = (before_ref[0, pair, :, columns], before_ref[1, pair, :, columns])
-            for at in range(pair * dates, (pair + 1) * dates):
-                actual = unpacked_rows(crossed_ref, at, tiles * dates, dense, low_x, width)
-                sums = added(sums, fine_ref[at * rows : (at + 1) * rows, columns], actual, normal)
-            for kind, total in enumerate(sums):
-                total = total * (1.0 / count)
-                held_ref[kind, 2 * pair, :, columns] = total[:owned]
-                held_ref[kind, 2 * pair + 1, :, columns] = total[owned:]
-        done = pl.ds(2 * pair, 2)
-        for kind, out_ref in enumerate(results):
-            copy = pltpu.make_async_copy(held_ref.at[kind, done], out_ref.at[done], sems.at[len(copies)])
-            copy.start()
-            copies.append(copy)
+    full = dense // LANES
+
+    def add_columns(pair, columns, actuals):
+        normal = normals_ref[pair, :, columns]
+        sums = (before_ref[0, pair, :, columns], before_ref[1, pair, :, columns])
+        for date, actual in enumerate(actuals):
+            at = (pair * dates + date) * rows
+            at = at if isinstance(at, int) else pl.multiple_of(at, rows)
+            sums = added(sums, fine_ref[pl.ds(at, rows), columns], actual, normal)
+        for kind, total in enumerate(sums):
+            total = total * (1.0 / count)
+            held_ref[kind, 2 * pair, :, columns] = total[:owned]
+            held_ref[kind, 2 * pair + 1, :, columns] = total[owned:]
+
+    def whole_tiles(pair, carry):
+        for tile in range(full):
+            actuals = [
+                crossed_ref[(pair * dates + date) * full + tile].astype(jnp.float32) for date in range(dates)
+            ]
+            add_columns(pair, slice(tile * LANES, (tile + 1) * LANES), actuals)
+        return carry
+
+    lax.fori_loop(0, tiles, whole_tiles, 0)
+    if dense % LANES:
+        low_x = full * LANES
+        for pair in range(tiles):
+            actuals = [
+                unpacked_rows(crossed_ref, pair * dates + date, tiles * dates, dense, low_x, dense - low_x)
+                for date in range(dates)
+            ]
+            add_columns(pair, slice(low_x, dense), actuals)
+    copies = [
+        pltpu.make_async_copy(held_ref.at[kind], out_ref, sems.at[kind]) for kind, out_ref in enumerate(results)
+    ]
+    for copy in copies:
+        copy.start()
     for copy in copies:
         copy.wait()
 
@@ -495,9 +512,9 @@
     peer = lax.ppermute(model_prognosis, "date", straight_way).reshape(own.shape)
 
     packed = jax.ShapeDtypeStruct((packed_tiles(tiles, dense), rows, LANES), bfloat16)
-    straight, own = kernel_call(
-        functools.partial(straight_kernel, dates),
-        [packed, jax.ShapeDtypeStruct(own.shape, own.dtype)],
+    straight, crossed, own = kernel_call(
+        functools.partial(away_kernel, dates),
+        [packed, packed, jax.ShapeDtypeStruct(own.shape, own.dtype)],
         [],
         8,
         100_000_000,
@@ -506,18 +523,17 @@
         taps,
     )
     straight = lax.ppermute(straight, "date", straight_way)
+    crossed = lax.ppermute(crossed, "date", crossed_way)
     plain = jax.ShapeDtypeStruct((tiles, rows, dense), bfloat16)
-    crossed, mine, sibling, normals = kernel_call(
+    mine, sibling, normals = kernel_call(
         functools.partial(home_kernel, dates),
-        [packed, plain, plain, jax.ShapeDtypeStruct((pairs // 2, rows, dense), float32)],
+        [plain, plain, jax.ShapeDtypeStruct((pairs // 2, rows, dense), float32)],
         [],
         12,
         100_000_000,
         truth,
         normal,
-        own,
-    )
-    crossed = lax.ppermute(crossed, "date", crossed_way)
+    )
     sibling = lax.ppermute(sibling, "date", sibling_way)
 
     chain = []
@@ -583,7 +599,7 @@
     results = kernel_call(
         functools.partial(mean_kernel, dates, dates * groups),
         [out, out],
-        [pltpu.VMEM((2,) + out.shape, float32), pltpu.SemaphoreType.DMA((pairs,))],
+        [pltpu.VMEM((2,) + out.shape, float32), pltpu.SemaphoreType.DMA((2,))],
         16,
         0,
         chip_sums,

time: 16.6 us -> 16.9 us (1.018)
  starting transfers between devices: 8.86 us -> 9.1 us
    ppermute x1, starting transfers between devices: 0.25 us -> 0.01 us  [two_chip_maps(): crossed = lax.ppermute(crossed, 'date', crossed_way)]
    ppermute x1, starting transfers between devices: 0.85 us -> 1.1 us  [two_chip_maps(): sibling = lax.ppermute(sibling, 'date', sibling_way)]
  transfers between devices with their start and end apart: 7 -> 7, of which waited for: 3 -> 3; matrix products, arithmetic and copies ran while one was open for 1% -> 1% of each run, Pallas kernels for 14% -> 13%
where the time goes in v3:
time: 16.9 us; the launch traced here: 16.6 us
  starting transfers between devices  9.1 us (54%)
  Pallas kernels  3.32 us (20%)
  waiting for transfers between devices  3.27 us (19%)
  between operations  0.79 us (5%)
    ppermute x1, starting transfers between devices, two_chip_maps(): halo = lax.ppermute(edges, ('date', 'band'), chain)  3.67 us
    pallas_call x8, Pallas kernels, kernel_call(): pl.pallas_call(kernel, out_shape=out_shape, in_specs=[vmem] * len(operand...  3.32 us
    ppermute x1, starting transfers between devices, two_chip_maps(): lax.ppermute(model_prognosis, 'date', straight_way).reshape(own.shape)  3 us
    ppermute x1, waiting for transfers between devices, two_chip_maps(): halo = lax.ppermute(edges, ('date', 'band'), chain)  1.65 us
    ppermute x1, starting transfers between devices, two_chip_maps(): straight = lax.ppermute(straight, 'date', straight_way)  1.17 us
    ppermute x1, starting transfers between devices, two_chip_maps(): sibling = lax.ppermute(sibling, 'date', sibling_way)  1.1 us
    ppermute x1, waiting for transfers between devices, two_chip_maps(): crossed = lax.ppermute(crossed, 'date', crossed_way)  1.05 us
    ppermute x1, waiting for transfers between devices, two_chip_maps(): sibling_halo = lax.ppermute(halo, 'date', sibling_way)  0.56 us
  transfers between devices with their start and end apart: 7, of which 3 were waited for; matrix products, arithmetic and copies ran while one was open for 1% of the time, Pallas kernels for 13%

profile of v3, /device:TPU:0, one launch (start us, length us, event | category | flops | bytes accessed | tf_op | source)
XLA Modules:
  0.0 16.6 jit_solution(3111186043610542136)
XLA Ops:
  0.6 0.0 copy-start.2
  0.6 0.0 copy-start
  0.6 3.0 %collective-permute-start = (bf16[2,2,5,4,360]{4,3,2,1,0:T(4,128)(2,1)}, bf16[2,2,5,4,360]{4,3,2,1,0:T(4,128)(2,1)S(1)}, u32[]{:S(2)}, u32[]{:S(2)}) collective-permute-start(bf16[2,2,5,4,360]{4,3,2,1,0:T(4,128)(2,1)} %param.7), channel_id=1, source_target_pairs={{0,16},{8,24},{16,0},{24,8},{1,17},{9,25},{17,1},{25,9},{2,18},{10... | collective-permute-start | bytes 172808 | tf_op jit(solution)/shard_map/ppermute | solution.py:512
  3.7 0.0 copy-done.2
  3.7 0.0 copy-done
  3.7 0.0 copy-start.1
  3.7 0.2 %shard_map.87 = (bf16[113,8,128]{2,1,0:T(8,128)(2,1)S(1)}, bf16[113,8,128]{2,1,0:T(8,128)(2,1)S(1)}, bf16[20,4,360]{2,1,0:T(4,128)(2,1)S(1)}) custom-call(bf16[20,16,1440]{2,1,0:T(8,128)(2,1)S(1)} %bitcast.7, bf16[20,4,360]{2,1,0:T(4,128)(2,1)S(1)} %bitcast.10, s32[72,256]{1,0:T(8,128)S(1)} %shard_map.86._.tap_ref), custom_call_target="tpu_custom_call" | custom-call | flops 100000000 | tf_op jit(solution)/shard_map/pallas_call | solution.py:482
  3.9 1.2 %collective-permute-start.5 = (bf16[113,8,128]{2,1,0:T(8,128)(2,1)S(1)}, bf16[113,8,128]{2,1,0:T(8,128)(2,1)S(1)}, u32[]{:S(2)}, u32[]{:S(2)}) collective-permute-start(bf16[113,8,128]{2,1,0:T(8,128)(2,1)S(1)} %get-tuple-element.24), channel_id=1, source_target_pairs={{0,16},{8,24},{16,0},{24,8},{1,17},{9,25},{17,1},{25,9},{2,18},{10... | collective-permute-start | bytes 694280 | tf_op jit(solution)/shard_map/ppermute | solution.py:525
  5.1 0.0 collective-permute-start.6
  5.1 0.0 copy-done.1
  5.1 0.0 copy-start.4
  5.1 0.3 %shard_map.89 = (bf16[10,8,1440]{2,1,0:T(8,128)(2,1)S(1)}, bf16[10,8,1440]{2,1,0:T(8,128)(2,1)S(1)}, f32[5,8,1440]{2,1,0:T(8,128)S(1)}) custom-call(bf16[20,16,1440]{2,1,0:T(8,128)(2,1)S(1)} %bitcast.8, bf16[10,16,1440]{2,1,0:T(8,128)(2,1)S(1)} %bitcast.9), custom_call_target="tpu_custom_call" | custom-call | flops 100000000 | tf_op jit(solution)/shard_map/pallas_call | solution.py:482
  5.4 0.0 copy-start.3
  5.4 1.1 %collective-permute-start.4 = (bf16[10,8,1440]{2,1,0:T(8,128)(2,1)S(1)}, bf16[10,8,1440]{2,1,0:T(8,128)(2,1)S(1)}, u32[]{:S(2)}, u32[]{:S(2)}) collective-permute-start(bf16[10,8,1440]{2,1,0:T(8,128)(2,1)S(1)} %get-tuple-element.19), channel_id=1, source_target_pairs={{0,8},{8,0},{16,24},{24,16},{1,9},{9,1},{17,25},{25,17},{2,10},{10... | collective-permute-start | bytes 691208 | tf_op jit(solution)/shard_map/ppermute | solution.py:537
  6.5 0.0 copy-done.4
  6.6 0.0 copy-done.3
  6.6 0.1 convert_select_fusion.lon_ref
  6.6 0.1 shard_map.90.table_ref
  6.8 0.0 collective-permute-done
  6.8 0.1 shard_map.88
  6.9 0.0 copy-start.6
  6.9 3.7 %collective-permute-start.2 = (bf16[40,2,360]{2,1,0:T(2,128)(2,1)S(1)}, bf16[40,2,360]{2,1,0:T(2,128)(2,1)S(1)}, u32[]{:S(2)}, u32[]{:S(2)}) collective-permute-start(bf16[40,2,360]{2,1,0:T(2,128)(2,1)S(1)} %get-tuple-element.18), channel_id=1, source_target_pairs={{0,1},{1,2},{2,3},{3,4},{4,5},{5,6},{6,7},{8,9},{9,10},{10,11},{11... | collective-permute-start | bytes 172808 | tf_op jit(solution)/shard_map/ppermute | solution.py:557
  10.6 0.0 copy-done.6
  10.6 0.0 copy-start.5
  10.6 0.1 collective-permute-start.1
  10.8 1.6 %collective-permute-done.2.halo_ref = bf16[40,2,360]{2,1,0:T(2,128)(2,1)S(1)} collective-permute-done((bf16[40,2,360]{2,1,0:T(2,128)(2,1)S(1)}, bf16[40,2,360]{2,1,0:T(2,128)(2,1)S(1)}, u32[]{:S(2)}, u32[]{:S(2)}) %collective-permute-start.2) | collective-permute-done | bytes 57632 | tf_op jit(solution)/shard_map/ppermute | solution.py:557
  12.4 0.0 collective-permute-start.3
  12.4 0.0 copy-done.5
  12.5 0.7 %shard_map.91 = (f32[2,5,8,1440]{3,2,1,0:T(8,128)S(1)}, f32[80,1440]{1,0:T(8,128)S(1)}) custom-call(bf16[40,4,360]{2,1,0:T(4,128)(2,1)S(1)} %get-tuple-element.17.coarse_ref, bf16[40,2,360]{2,1,0:T(2,128)(2,1)S(1)} %collective-permute-done.2.halo_ref, bf16[10,8,1440]{2,1,0:T(8,128)(2,1)S(1)} %get-tuple-element.21.truth_ref, ...), custom_call_target="tpu_custom_call" | custom-call | tf_op jit(solution)/shard_map/pallas_call | solution.py:482
  13.1 0.6 %collective-permute-done.3.halo_ref = bf16[40,2,360]{2,1,0:T(2,128)(2,1)S(1)} collective-permute-done((bf16[40,2,360]{2,1,0:T(2,128)(2,1)S(1)}, bf16[40,2,360]{2,1,0:T(2,128)(2,1)S(1)}, u32[]{:S(2)}, u32[]{:S(2)}) %collective-permute-start.3) | collective-permute-done | bytes 57632 | tf_op jit(solution)/shard_map/ppermute | solution.py:559
  13.7 0.0 collective-permute-done.1.coarse_ref
  13.7 0.0 collective-permute-done.4.truth_ref
  13.7 0.0 collective-permute-done.5.straight_ref
  13.7 0.8 %shard_map.92 = (f32[2,5,8,1440]{3,2,1,0:T(8,128)S(1)}, f32[80,1440]{1,0:T(8,128)S(1)}) custom-call(bf16[40,4,360]{2,1,0:T(4,128)(2,1)S(1)} %collective-permute-done.1.coarse_ref, bf16[40,2,360]{2,1,0:T(2,128)(2,1)S(1)} %collective-permute-done.3.halo_ref, bf16[10,8,1440]{2,1,0:T(8,128)(2,1)S(1)} %collective-permute-done.4.truth_ref, ...), custom_call_target="tpu_custom_call" | custom-call | tf_op jit(solution)/shard_map/pallas_call | solution.py:482
  14.5 1.0 %collective-permute-done.6.crossed_ref = bf16[113,8,128]{2,1,0:T(8,128)(2,1)S(1)} collective-permute-done((bf16[113,8,128]{2,1,0:T(8,128)(2,1)S(1)}, bf16[113,8,128]{2,1,0:T(8,128)(2,1)S(1)}, u32[]{:S(2)}, u32[]{:S(2)}) %collective-permute-start.6) | collective-permute-done | bytes 231456 | tf_op jit(solution)/shard_map/ppermute | solution.py:526
  15.5 1.1 %shard_map.93 = (f32[10,4,1440]{2,1,0:T(4,128)}, f32[10,4,1440]{2,1,0:T(4,128)}) custom-call(f32[2,5,8,1440]{3,2,1,0:T(8,128)S(1)} %get-tuple-element.25.before_ref, f32[80,1440]{1,0:T(8,128)S(1)} %get-tuple-element.26.fine_ref, bf16[113,8,128]{2,1,0:T(8,128)(2,1)S(1)} %collective-permute-done.6.crossed_ref, f32[5,8,1440]{2,1,0:T(8,128)S(1)} %get-tuple-element.20.normals_ref), custom_call_target="tpu_custom_call" | custom-call | tf_op jit(solution)/shard_map/pallas_call | solution.py:482
  (6 shorter events, 0.0 us)
Async XLA Ops:
  0.6 3.0 %copy-start.2 = (bf16[2,2,5,4,360]{4,3,2,1,0:T(4,128)(2,1)S(1)}, bf16[2,2,5,4,360]{4,3,2,1,0:T(4,128)(2,1)}, u32[]{:S(2)}) copy-start(bf16[2,2,5,4,360]{4,3,2,1,0:T(4,128)(2,1)} %param.7) | copy-start | bytes 172804
  0.6 3.0 %copy-start = (bf16[2,2,5,16,1440]{4,3,2,1,0:T(8,128)(2,1)S(1)}, bf16[2,2,5,16,1440]{4,3,2,1,0:T(8,128)(2,1)}, u32[]{:S(2)}) copy-start(bf16[2,2,5,16,1440]{4,3,2,1,0:T(8,128)(2,1)} %param.8) | copy-start | bytes 2764804
  0.6 6.1 %collective-permute-start = (bf16[2,2,5,4,360]{4,3,2,1,0:T(4,128)(2,1)}, bf16[2,2,5,4,360]{4,3,2,1,0:T(4,128)(2,1)S(1)}, u32[]{:S(2)}, u32[]{:S(2)}) collective-permute-start(bf16[2,2,5,4,360]{4,3,2,1,0:T(4,128)(2,1)} %param.7), channel_id=1, source_target_pairs={{0,16},{8,24},{16,0},{24,8},{1,17},{9,25},{17,1},{25,9},{2,18},{10... | collective-permute-start | bytes 172808 | tf_op jit(solution)/shard_map/ppermute | solution.py:512
  3.7 1.4 %copy-start.1 = (bf16[2,5,16,1440]{3,2,1,0:T(8,128)(2,1)S(1)}, bf16[2,5,16,1440]{3,2,1,0:T(8,128)(2,1)}, u32[]{:S(2)}) copy-start(bf16[2,5,16,1440]{3,2,1,0:T(8,128)(2,1)} %param.9) | copy-start | bytes 1382404
  3.9 9.8 %collective-permute-start.5 = (bf16[113,8,128]{2,1,0:T(8,128)(2,1)S(1)}, bf16[113,8,128]{2,1,0:T(8,128)(2,1)S(1)}, u32[]{:S(2)}, u32[]{:S(2)}) collective-permute-start(bf16[113,8,128]{2,1,0:T(8,128)(2,1)S(1)} %get-tuple-element.24), channel_id=1, source_target_pairs={{0,16},{8,24},{16,0},{24,8},{1,17},{9,25},{17,1},{25,9},{2,18},{10... | collective-permute-start | bytes 694280 | tf_op jit(solution)/shard_map/ppermute | solution.py:525
  5.1 10.4 %collective-permute-start.6 = (bf16[113,8,128]{2,1,0:T(8,128)(2,1)S(1)}, bf16[113,8,128]{2,1,0:T(8,128)(2,1)S(1)}, u32[]{:S(2)}, u32[]{:S(2)}) collective-permute-start(bf16[113,8,128]{2,1,0:T(8,128)(2,1)S(1)} %get-tuple-element.27), channel_id=1, source_target_pairs={{0,24},{8,16},{16,8},{24,0},{1,25},{9,17},{17,9},{25,1},{2,26},{10... | collective-permute-start | bytes 694280 | tf_op jit(solution)/shard_map/ppermute | solution.py:526
  5.1 1.4 %copy-start.4 = (s32[1440]{0:T(1024)S(1)}, s32[1440]{0:T(1024)}, u32[]{:S(2)}) copy-start(s32[1440]{0:T(1024)} %param.12) | copy-start | bytes 17284
  5.4 1.1 %copy-start.3 = (bf16[4,1440]{1,0:T(4,128)(2,1)S(1)}, bf16[4,1440]{1,0:T(4,128)(2,1)}, u32[]{:S(2)}) copy-start(bf16[4,1440]{1,0:T(4,128)(2,1)} %param.13) | copy-start | bytes 34564
  5.4 8.3 %collective-permute-start.4 = (bf16[10,8,1440]{2,1,0:T(8,128)(2,1)S(1)}, bf16[10,8,1440]{2,1,0:T(8,128)(2,1)S(1)}, u32[]{:S(2)}, u32[]{:S(2)}) collective-permute-start(bf16[10,8,1440]{2,1,0:T(8,128)(2,1)S(1)} %get-tuple-element.19), channel_id=1, source_target_pairs={{0,8},{8,0},{16,24},{24,16},{1,9},{9,1},{17,25},{25,17},{2,10},{10... | collective-permute-start | bytes 691208 | tf_op jit(solution)/shard_map/ppermute | solution.py:537
  6.9 3.7 %copy-start.6 = (s32[16]{0:T(128)S(1)}, s32[16]{0:T(128)}, u32[]{:S(2)}) copy-start(s32[16]{0:T(128)} %param.10) | copy-start | bytes 196
  6.9 5.5 %collective-permute-start.2 = (bf16[40,2,360]{2,1,0:T(2,128)(2,1)S(1)}, bf16[40,2,360]{2,1,0:T(2,128)(2,1)S(1)}, u32[]{:S(2)}, u32[]{:S(2)}) collective-permute-start(bf16[40,2,360]{2,1,0:T(2,128)(2,1)S(1)} %get-tuple-element.18), channel_id=1, source_target_pairs={{0,1},{1,2},{2,3},{3,4},{4,5},{5,6},{6,7},{8,9},{9,10},{10,11},{11... | collective-permute-start | bytes 172808 | tf_op jit(solution)/shard_map/ppermute | solution.py:557
  10.6 1.8 %copy-start.5 = (f32[16,4]{0,1:T(4,128)S(1)}, f32[16,4]{0,1:T(4,128)}, u32[]{:S(2)}) copy-start(f32[16,4]{0,1:T(4,128)} %param.11) | copy-start | bytes 772
  10.6 3.0 %collective-permute-start.1 = (bf16[40,4,360]{2,1,0:T(4,128)(2,1)S(1)}, bf16[40,4,360]{2,1,0:T(4,128)(2,1)S(1)}, u32[]{:S(2)}, u32[]{:S(2)}) collective-permute-start(bf16[40,4,360]{2,1,0:T(4,128)(2,1)S(1)} %get-tuple-element.17.coarse_ref), channel_id=1, source_target_pairs={{0,8},{8,0},{16,24},{24,16},{1,9},{9,1},{17,25},{25,17},{2,10},{10... | collective-permute-start | bytes 345608 | tf_op jit(solution)/shard_map/ppermute | solution.py:558
  12.4 1.2 %collective-permute-start.3 = (bf16[40,2,360]{2,1,0:T(2,128)(2,1)S(1)}, bf16[40,2,360]{2,1,0:T(2,128)(2,1)S(1)}, u32[]{:S(2)}, u32[]{:S(2)}) collective-permute-start(bf16[40,2,360]{2,1,0:T(2,128)(2,1)S(1)} %collective-permute-done.2.halo_ref), channel_id=1, source_target_pairs={{0,8},{8,0},{16,24},{24,16},{1,9},{9,1},{17,25},{25,17},{2,10},{10... | collective-permute-start | bytes 172808 | tf_op jit(solution)/shard_map/ppermute | solution.py:559

commit v4 on v2

--- a/solution.py
+++ b/solution.py
@@ -279,29 +279,27 @@
     return [[date * pairs + pair, date * pairs + pair + 1] for pair in range(0, pairs, 2) for date in range(dates)]
 
 
-def straight_kernel(dates, truth_ref, own_ref, _, out_ref, kept_ref):
+def away_kernel(dates, truth_ref, own_ref, _, straight_ref, crossed_ref, kept_ref):
     first = first_core()
-    blocks = []
+    straight, crossed = [], []
     for entries in tile_entries(truth_ref.shape[0] // dates, dates):
         one, two = by_owner(truth_ref, entries, jnp.logical_not(lower_chip()))
-        blocks.append(jnp.where(first, one, two))
-    pack_rows(blocks, out_ref)
+        straight.append(jnp.where(first, one, two))
+        crossed.append(jnp.where(first, two, one))
+    pack_rows(straight, straight_ref)
+    pack_rows(crossed, crossed_ref)
     for index in range(own_ref.shape[0]):
         kept_ref[index] = own_ref[index]
 
 
-def home_kernel(dates, truth_ref, normal_ref, _, crossed_ref, mine_ref, sibling_ref, normals_ref):
+def home_kernel(dates, truth_ref, normal_ref, mine_ref, sibling_ref, normals_ref):
     pairs = normal_ref.shape[0]
     first = first_core()
     lower = lower_chip()
-    crossed = []
     for at, entries in enumerate(tile_entries(pairs, dates)):
-        one, two = by_owner(truth_ref, entries, jnp.logical_not(lower))
-        crossed.append(jnp.where(first, two, one))
         one, two = by_owner(truth_ref, entries, lower)
         mine_ref[at] = jnp.where(first, one, two).astype(mine_ref.dtype)
         sibling_ref[at] = jnp.where(first, two, one).astype(sibling_ref.dtype)
-    pack_rows(crossed, crossed_ref)
     for pair in range(0, pairs, 2):
         one, two = by_owner(normal_ref, [pair, pair + 1], lower)
         normals_ref[pair // 2] = jnp.where(first, one, two)
@@ -315,6 +313,15 @@
         both_ref[index] = block
         block = block.astype(jnp.float32)
         rows_ref[index] = jnp.where(lower, block[coarse_rows - 2 :], block[:2]).astype(jnp.bfloat16)
+
+
+def pick_halo_kernel(paired_ref, crossed_ref, halo_ref):
+    odd = lax.rem(lax.axis_index("band"), 2) == 1
+    from_pair = jnp.logical_not(jnp.logical_xor(odd, lower_chip()))
+    for index in range(halo_ref.shape[0]):
+        paired = paired_ref[index].astype(jnp.float32)
+        crossed = crossed_ref[index].astype(jnp.float32)
+        halo_ref[index] = jnp.where(from_pair, paired, crossed).astype(halo_ref.dtype)
 
 
 def latitude_step(dates, coarse_ref, halo_ref, lat_ref, lhs_ref):
@@ -495,9 +502,9 @@
     peer = lax.ppermute(model_prognosis, "date", straight_way).reshape(own.shape)
 
     packed = jax.ShapeDtypeStruct((packed_tiles(tiles, dense), rows, LANES), bfloat16)
-    straight, own = kernel_call(
-        functools.partial(straight_kernel, dates),
-        [packed, jax.ShapeDtypeStruct(own.shape, own.dtype)],
+    straight, crossed, own = kernel_call(
+        functools.partial(away_kernel, dates),
+        [packed, packed, jax.ShapeDtypeStruct(own.shape, own.dtype)],
         [],
         8,
         100_000_000,
@@ -506,26 +513,19 @@
         taps,
     )
     straight = lax.ppermute(straight, "date", straight_way)
+    crossed = lax.ppermute(crossed, "date", crossed_way)
     plain = jax.ShapeDtypeStruct((tiles, rows, dense), bfloat16)
-    crossed, mine, sibling, normals = kernel_call(
+    mine, sibling, normals = kernel_call(
         functools.partial(home_kernel, dates),
-        [packed, plain, plain, jax.ShapeDtypeStruct((pairs // 2, rows, dense), float32)],
+        [plain, plain, jax.ShapeDtypeStruct((pairs // 2, rows, dense), float32)],
         [],
         12,
         100_000_000,
         truth,
         normal,
-        own,
-    )
-    crossed = lax.ppermute(crossed, "date", crossed_way)
+    )
     sibling = lax.ppermute(sibling, "date", sibling_way)
 
-    chain = []
-    for group in range(groups):
-        for band in range(bands):
-            to = band + (1 if group < groups // 2 else -1)
-            if 0 <= to < bands:
-                chain.append((group * bands + band, group * bands + to))
     coarse, edges = kernel_call(
         shift_rows_kernel,
         [
@@ -538,7 +538,12 @@
         own,
         peer,
     )
-    halo = lax.ppermute(edges, ("date", "band"), chain)
+    across = [(i, min(max(i + (1 if i % 2 else -1), 0), bands - 1)) for i in range(bands)]
+    crossed_rows = lax.ppermute(edges, "band", across)
+    paired_rows = lax.ppermute(edges, "band", [(i, i ^ 1) for i in range(bands)])
+    (halo,) = kernel_call(
+        pick_halo_kernel, [jax.ShapeDtypeStruct(edges.shape, bfloat16)], [], 8, 0, paired_rows, crossed_rows
+    )
     sibling_coarse = lax.ppermute(coarse, "date", sibling_way)
     sibling_halo = lax.ppermute(halo, "date", sibling_way)
 

time: 16.6 us -> 18 us (1.084)
  starting transfers between devices: 8.86 us -> 10.7 us
  waiting for transfers between devices: 3.33 us -> 2.36 us
  local copies, waits for them, and re-layouts: 0.04 us -> 0.53 us
    ppermute x1 -> x2, starting transfers between devices: 3.51 us -> 5.26 us  [the longest x1 4.59 us: two_chip_maps(): lax.ppermute(edges, 'band', [(i, i ^ 1) for i in range(bands)])]
    ppermute x1, waiting for transfers between devices: 1.05 us -> 0.01 us  [two_chip_maps(): crossed = lax.ppermute(crossed, 'date', crossed_way)]
    ppermute x1 -> x2, waiting for transfers between devices: 1.71 us -> 2.29 us  [the longest x1 2.28 us: two_chip_maps(): lax.ppermute(edges, 'band', [(i, i ^ 1) for i in range(bands)])]
    ppermute x1, waiting for transfers between devices: 0.56 us -> 0.06 us  [two_chip_maps(): sibling_halo = lax.ppermute(halo, 'date', sibling_way)]
    unnamed x14, local copies, waits for them, and re-layouts: 0.04 us -> 0.52 us
    ppermute x1, starting transfers between devices: 0.25 us -> 0.01 us  [two_chip_maps(): crossed = lax.ppermute(crossed, 'date', crossed_way)]
    ppermute x1, starting transfers between devices: 0.85 us -> 1.1 us  [two_chip_maps(): sibling = lax.ppermute(sibling, 'date', sibling_way)]
    pallas_call x8 -> x9, Pallas kernels: 3.31 us -> 3.25 us  [kernel_call(): pl.pallas_call(kernel, out_shape=out_shape, in_specs=[vmem] * len(operand...]
  transfers between devices with their start and end apart: 7 -> 8, of which waited for: 3 -> 2; matrix products, arithmetic and copies ran while one was open for 1% -> 1% of each run, Pallas kernels for 14% -> 13%
where the time goes in v4:
time: 18 us; the launch traced here: 17.7 us
  starting transfers between devices  10.7 us (59%)
  Pallas kernels  3.25 us (18%)
  waiting for transfers between devices  2.36 us (13%)
  between operations  0.8 us (4%)
  local copies, waits for them, and re-layouts  0.53 us (3%)
    ppermute x1, starting transfers between devices, two_chip_maps(): lax.ppermute(edges, 'band', [(i, i ^ 1) for i in range(bands)])  4.59 us
    pallas_call x9, Pallas kernels, kernel_call(): pl.pallas_call(kernel, out_shape=out_shape, in_specs=[vmem] * len(operand...  3.25 us
    ppermute x1, starting transfers between devices, two_chip_maps(): lax.ppermute(model_prognosis, 'date', straight_way).reshape(own.shape)  3 us
    ppermute x1, waiting for transfers between devices, two_chip_maps(): lax.ppermute(edges, 'band', [(i, i ^ 1) for i in range(bands)])  2.28 us
    ppermute x1, starting transfers between devices, two_chip_maps(): straight = lax.ppermute(straight, 'date', straight_way)  1.17 us
    ppermute x1, starting transfers between devices, two_chip_maps(): sibling = lax.ppermute(sibling, 'date', sibling_way)  1.1 us
    ppermute x1, starting transfers between devices, two_chip_maps(): crossed_rows = lax.ppermute(edges, 'band', across)  0.66 us
    unnamed x14, local copies, waits for them, and re-layouts  0.52 us
  transfers between devices with their start and end apart: 8, of which 2 were waited for; matrix products, arithmetic and copies ran while one was open for 1% of the time, Pallas kernels for 13%

profile of v4, /device:TPU:0, one launch (start us, length us, event | category | flops | bytes accessed | tf_op | source)
XLA Modules:
  0.0 17.7 jit_solution(12801754782225228820)
XLA Ops:
  0.6 0.0 copy-start.2
  0.6 0.0 copy-start
  0.6 3.0 %collective-permute-start = (bf16[2,2,5,4,360]{4,3,2,1,0:T(4,128)(2,1)}, bf16[2,2,5,4,360]{4,3,2,1,0:T(4,128)(2,1)S(1)}, u32[]{:S(2)}, u32[]{:S(2)}) collective-permute-start(bf16[2,2,5,4,360]{4,3,2,1,0:T(4,128)(2,1)} %param.7), channel_id=1, source_target_pairs={{0,16},{8,24},{16,0},{24,8},{1,17},{9,25},{17,1},{25,9},{2,18},{10... | collective-permute-start | bytes 172808 | tf_op jit(solution)/shard_map/ppermute | solution.py:502
  3.7 0.0 copy-done.2
  3.7 0.0 copy-done
  3.7 0.0 copy-start.1
  3.7 0.2 %shard_map.87 = (bf16[113,8,128]{2,1,0:T(8,128)(2,1)S(1)}, bf16[113,8,128]{2,1,0:T(8,128)(2,1)S(1)}, bf16[20,4,360]{2,1,0:T(4,128)(2,1)S(1)}) custom-call(bf16[20,16,1440]{2,1,0:T(8,128)(2,1)S(1)} %bitcast.7, bf16[20,4,360]{2,1,0:T(4,128)(2,1)S(1)} %bitcast.10, s32[72,256]{1,0:T(8,128)S(1)} %shard_map.86._.tap_ref), custom_call_target="tpu_custom_call" | custom-call | flops 100000000 | tf_op jit(solution)/shard_map/pallas_call | solution.py:472
  3.9 1.2 %collective-permute-start.6 = (bf16[113,8,128]{2,1,0:T(8,128)(2,1)S(1)}, bf16[113,8,128]{2,1,0:T(8,128)(2,1)S(1)}, u32[]{:S(2)}, u32[]{:S(2)}) collective-permute-start(bf16[113,8,128]{2,1,0:T(8,128)(2,1)S(1)} %get-tuple-element.24), channel_id=1, source_target_pairs={{0,16},{8,24},{16,0},{24,8},{1,17},{9,25},{17,1},{25,9},{2,18},{10... | collective-permute-start | bytes 694280 | tf_op jit(solution)/shard_map/ppermute | solution.py:515
  5.1 0.0 collective-permute-start.7
  5.1 0.0 copy-done.1
  5.1 0.0 copy-start.4
  5.1 0.3 %shard_map.90 = (bf16[10,8,1440]{2,1,0:T(8,128)(2,1)S(1)}, bf16[10,8,1440]{2,1,0:T(8,128)(2,1)S(1)}, f32[5,8,1440]{2,1,0:T(8,128)S(1)}) custom-call(bf16[20,16,1440]{2,1,0:T(8,128)(2,1)S(1)} %bitcast.8, bf16[10,16,1440]{2,1,0:T(8,128)(2,1)S(1)} %bitcast.9), custom_call_target="tpu_custom_call" | custom-call | flops 100000000 | tf_op jit(solution)/shard_map/pallas_call | solution.py:472
  5.4 0.0 copy-start.3
  5.4 1.1 %collective-permute-start.5 = (bf16[10,8,1440]{2,1,0:T(8,128)(2,1)S(1)}, bf16[10,8,1440]{2,1,0:T(8,128)(2,1)S(1)}, u32[]{:S(2)}, u32[]{:S(2)}) collective-permute-start(bf16[10,8,1440]{2,1,0:T(8,128)(2,1)S(1)} %get-tuple-element.19), channel_id=1, source_target_pairs={{0,8},{8,0},{16,24},{24,16},{1,9},{9,1},{17,25},{25,17},{2,10},{10... | collective-permute-start | bytes 691208 | tf_op jit(solution)/shard_map/ppermute | solution.py:527
  6.5 0.0 copy-done.4
  6.6 0.0 copy-done.3
  6.6 0.1 convert_select_fusion.lon_ref
  6.6 0.1 shard_map.91.table_ref
  6.8 0.0 collective-permute-done
  6.8 0.1 shard_map.88
  6.9 0.0 copy-start.6
  6.9 0.7 %collective-permute-start.3 = (bf16[40,2,360]{2,1,0:T(2,128)(2,1)S(1)}, bf16[40,2,360]{2,1,0:T(2,128)(2,1)S(1)}, u32[]{:S(2)}, u32[]{:S(2)}) collective-permute-start(bf16[40,2,360]{2,1,0:T(2,128)(2,1)S(1)} %get-tuple-element.18), channel_id=1, source_target_pairs={{0,0},{1,2},{2,1},{3,4},{4,3},{5,6},{6,5},{7,7},{8,8},{9,10},{10,9... | collective-permute-start | bytes 172808 | tf_op jit(solution)/shard_map/ppermute | solution.py:542
  7.6 4.6 %collective-permute-start.2 = (bf16[40,2,360]{2,1,0:T(2,128)(2,1)S(1)}, bf16[40,2,360]{2,1,0:T(2,128)(2,1)S(1)}, u32[]{:S(2)}, u32[]{:S(2)}) collective-permute-start(bf16[40,2,360]{2,1,0:T(2,128)(2,1)S(1)} %get-tuple-element.18), channel_id=1, source_target_pairs={{0,1},{1,0},{2,3},{3,2},{4,5},{5,4},{6,7},{7,6},{8,9},{9,8},{10,11... | collective-permute-start | bytes 172808 | tf_op jit(solution)/shard_map/ppermute | solution.py:543
  12.2 0.0 copy-done.6
  12.2 0.0 collective-permute-done.3.crossed_ref
  12.2 0.1 collective-permute-start.1
  12.3 2.3 %collective-permute-done.2.paired_ref = bf16[40,2,360]{2,1,0:T(2,128)(2,1)S(1)} collective-permute-done((bf16[40,2,360]{2,1,0:T(2,128)(2,1)S(1)}, bf16[40,2,360]{2,1,0:T(2,128)(2,1)S(1)}, u32[]{:S(2)}, u32[]{:S(2)}) %collective-permute-start.2) | collective-permute-done | bytes 57632 | tf_op jit(solution)/shard_map/ppermute | solution.py:543
  14.6 0.0 copy-start.5
  14.6 0.1 shard_map.89.halo_ref
  14.7 0.1 collective-permute-start.4
  14.8 0.5 %copy-done.5 = f32[16,4]{0,1:T(4,128)S(1)} copy-done((f32[16,4]{0,1:T(4,128)S(1)}, f32[16,4]{0,1:T(4,128)}, u32[]{:S(2)}) %copy-start.5) | copy-done | bytes 280
  15.3 0.7 %shard_map.92 = (f32[2,5,8,1440]{3,2,1,0:T(8,128)S(1)}, f32[80,1440]{1,0:T(8,128)S(1)}) custom-call(bf16[40,4,360]{2,1,0:T(4,128)(2,1)S(1)} %get-tuple-element.17.coarse_ref, bf16[40,2,360]{2,1,0:T(2,128)(2,1)S(1)} %shard_map.89.halo_ref, bf16[10,8,1440]{2,1,0:T(8,128)(2,1)S(1)} %get-tuple-element.21.truth_ref, ...), custom_call_target="tpu_custom_call" | custom-call | tf_op jit(solution)/shard_map/pallas_call | solution.py:472
  15.9 0.1 collective-permute-done.4.halo_ref
  16.0 0.0 collective-permute-done.1.coarse_ref
  16.0 0.0 collective-permute-done.5.truth_ref
  16.0 0.0 collective-permute-done.6.straight_ref
  16.0 0.8 %shard_map.93 = (f32[2,5,8,1440]{3,2,1,0:T(8,128)S(1)}, f32[80,1440]{1,0:T(8,128)S(1)}) custom-call(bf16[40,4,360]{2,1,0:T(4,128)(2,1)S(1)} %collective-permute-done.1.coarse_ref, bf16[40,2,360]{2,1,0:T(2,128)(2,1)S(1)} %collective-permute-done.4.halo_ref, bf16[10,8,1440]{2,1,0:T(8,128)(2,1)S(1)} %collective-permute-done.5.truth_ref, ...), custom_call_target="tpu_custom_call" | custom-call | tf_op jit(solution)/shard_map/pallas_call | solution.py:472
  16.8 0.0 collective-permute-done.7.crossed_ref
  16.8 0.9 %shard_map.94 = (f32[10,4,1440]{2,1,0:T(4,128)}, f32[10,4,1440]{2,1,0:T(4,128)}) custom-call(f32[2,5,8,1440]{3,2,1,0:T(8,128)S(1)} %get-tuple-element.25.before_ref, f32[80,1440]{1,0:T(8,128)S(1)} %get-tuple-element.26.fine_ref, bf16[113,8,128]{2,1,0:T(8,128)(2,1)S(1)} %collective-permute-done.7.crossed_ref, f32[5,8,1440]{2,1,0:T(8,128)S(1)} %get-tuple-element.20.normals_ref), custom_call_target="tpu_custom_call" | custom-call | tf_op jit(solution)/shard_map/pallas_call | solution.py:472
  (6 shorter events, 0.0 us)
Async XLA Ops:
  0.6 3.0 %copy-start.2 = (bf16[2,2,5,4,360]{4,3,2,1,0:T(4,128)(2,1)S(1)}, bf16[2,2,5,4,360]{4,3,2,1,0:T(4,128)(2,1)}, u32[]{:S(2)}) copy-start(bf16[2,2,5,4,360]{4,3,2,1,0:T(4,128)(2,1)} %param.7) | copy-start | bytes 172804
  0.6 3.0 %copy-start = (bf16[2,2,5,16,1440]{4,3,2,1,0:T(8,128)(2,1)S(1)}, bf16[2,2,5,16,1440]{4,3,2,1,0:T(8,128)(2,1)}, u32[]{:S(2)}) copy-start(bf16[2,2,5,16,1440]{4,3,2,1,0:T(8,128)(2,1)} %param.8) | copy-start | bytes 2764804
  0.6 6.1 %collective-permute-start = (bf16[2,2,5,4,360]{4,3,2,1,0:T(4,128)(2,1)}, bf16[2,2,5,4,360]{4,3,2,1,0:T(4,128)(2,1)S(1)}, u32[]{:S(2)}, u32[]{:S(2)}) collective-permute-start(bf16[2,2,5,4,360]{4,3,2,1,0:T(4,128)(2,1)} %param.7), channel_id=1, source_target_pairs={{0,16},{8,24},{16,0},{24,8},{1,17},{9,25},{17,1},{25,9},{2,18},{10... | collective-permute-start | bytes 172808 | tf_op jit(solution)/shard_map/ppermute | solution.py:502
  3.7 1.4 %copy-start.1 = (bf16[2,5,16,1440]{3,2,1,0:T(8,128)(2,1)S(1)}, bf16[2,5,16,1440]{3,2,1,0:T(8,128)(2,1)}, u32[]{:S(2)}) copy-start(bf16[2,5,16,1440]{3,2,1,0:T(8,128)(2,1)} %param.9) | copy-start | bytes 1382404
  3.9 12.1 %collective-permute-start.6 = (bf16[113,8,128]{2,1,0:T(8,128)(2,1)S(1)}, bf16[113,8,128]{2,1,0:T(8,128)(2,1)S(1)}, u32[]{:S(2)}, u32[]{:S(2)}) collective-permute-start(bf16[113,8,128]{2,1,0:T(8,128)(2,1)S(1)} %get-tuple-element.24), channel_id=1, source_target_pairs={{0,16},{8,24},{16,0},{24,8},{1,17},{9,25},{17,1},{25,9},{2,18},{10... | collective-permute-start | bytes 694280 | tf_op jit(solution)/shard_map/ppermute | solution.py:515
  5.1 11.7 %collective-permute-start.7 = (bf16[113,8,128]{2,1,0:T(8,128)(2,1)S(1)}, bf16[113,8,128]{2,1,0:T(8,128)(2,1)S(1)}, u32[]{:S(2)}, u32[]{:S(2)}) collective-permute-start(bf16[113,8,128]{2,1,0:T(8,128)(2,1)S(1)} %get-tuple-element.27), channel_id=1, source_target_pairs={{0,24},{8,16},{16,8},{24,0},{1,25},{9,17},{17,9},{25,1},{2,26},{10... | collective-permute-start | bytes 694280 | tf_op jit(solution)/shard_map/ppermute | solution.py:516
  5.1 1.4 %copy-start.4 = (s32[1440]{0:T(1024)S(1)}, s32[1440]{0:T(1024)}, u32[]{:S(2)}) copy-start(s32[1440]{0:T(1024)} %param.12) | copy-start | bytes 17284
  5.4 1.1 %copy-start.3 = (bf16[4,1440]{1,0:T(4,128)(2,1)S(1)}, bf16[4,1440]{1,0:T(4,128)(2,1)}, u32[]{:S(2)}) copy-start(bf16[4,1440]{1,0:T(4,128)(2,1)} %param.13) | copy-start | bytes 34564
  5.4 10.6 %collective-permute-start.5 = (bf16[10,8,1440]{2,1,0:T(8,128)(2,1)S(1)}, bf16[10,8,1440]{2,1,0:T(8,128)(2,1)S(1)}, u32[]{:S(2)}, u32[]{:S(2)}) collective-permute-start(bf16[10,8,1440]{2,1,0:T(8,128)(2,1)S(1)} %get-tuple-element.19), channel_id=1, source_target_pairs={{0,8},{8,0},{16,24},{24,16},{1,9},{9,1},{17,25},{25,17},{2,10},{10... | collective-permute-start | bytes 691208 | tf_op jit(solution)/shard_map/ppermute | solution.py:527
  6.9 5.3 %copy-start.6 = (s32[16]{0:T(128)S(1)}, s32[16]{0:T(128)}, u32[]{:S(2)}) copy-start(s32[16]{0:T(128)} %param.10) | copy-start | bytes 196
  6.9 5.3 %collective-permute-start.3 = (bf16[40,2,360]{2,1,0:T(2,128)(2,1)S(1)}, bf16[40,2,360]{2,1,0:T(2,128)(2,1)S(1)}, u32[]{:S(2)}, u32[]{:S(2)}) collective-permute-start(bf16[40,2,360]{2,1,0:T(2,128)(2,1)S(1)} %get-tuple-element.18), channel_id=1, source_target_pairs={{0,0},{1,2},{2,1},{3,4},{4,3},{5,6},{6,5},{7,7},{8,8},{9,10},{10,9... | collective-permute-start | bytes 172808 | tf_op jit(solution)/shard_map/ppermute | solution.py:542
  7.6 7.0 %collective-permute-start.2 = (bf16[40,2,360]{2,1,0:T(2,128)(2,1)S(1)}, bf16[40,2,360]{2,1,0:T(2,128)(2,1)S(1)}, u32[]{:S(2)}, u32[]{:S(2)}) collective-permute-start(bf16[40,2,360]{2,1,0:T(2,128)(2,1)S(1)} %get-tuple-element.18), channel_id=1, source_target_pairs={{0,1},{1,0},{2,3},{3,2},{4,5},{5,4},{6,7},{7,6},{8,9},{9,8},{10,11... | collective-permute-start | bytes 172808 | tf_op jit(solution)/shard_map/ppermute | solution.py:543
  12.2 3.8 %collective-permute-start.1 = (bf16[40,4,360]{2,1,0:T(4,128)(2,1)S(1)}, bf16[40,4,360]{2,1,0:T(4,128)(2,1)S(1)}, u32[]{:S(2)}, u32[]{:S(2)}) collective-permute-start(bf16[40,4,360]{2,1,0:T(4,128)(2,1)S(1)} %get-tuple-element.17.coarse_ref), channel_id=1, source_target_pairs={{0,8},{8,0},{16,24},{24,16},{1,9},{9,1},{17,25},{25,17},{2,10},{10... | collective-permute-start | bytes 345608 | tf_op jit(solution)/shard_map/ppermute | solution.py:547
  14.6 0.7 %copy-start.5 = (f32[16,4]{0,1:T(4,128)S(1)}, f32[16,4]{0,1:T(4,128)}, u32[]{:S(2)}) copy-start(f32[16,4]{0,1:T(4,128)} %param.11) | copy-start | bytes 772
  14.7 1.3 %collective-permute-start.4 = (bf16[40,2,360]{2,1,0:T(2,128)(2,1)S(1)}, bf16[40,2,360]{2,1,0:T(2,128)(2,1)S(1)}, u32[]{:S(2)}, u32[]{:S(2)}) collective-permute-start(bf16[40,2,360]{2,1,0:T(2,128)(2,1)S(1)} %shard_map.89.halo_ref), channel_id=1, source_target_pairs={{0,8},{8,0},{16,24},{24,16},{1,9},{9,1},{17,25},{25,17},{2,10},{10... | collective-permute-start | bytes 172808 | tf_op jit(solution)/shard_map/ppermute | solution.py:548

commit v5 on v4

--- a/solution.py
+++ b/solution.py
@@ -231,9 +231,9 @@
 
 
 def by_owner(ref, entries, lower):
-    blocks = [ref[entry].astype(jnp.float32) for entry in entries]
+    blocks = [ref[entry] for entry in entries]
     half = blocks[0].shape[0] // 2
-    blocks = [jnp.where(lower, block[:half], block[half:]) for block in blocks]
+    blocks = [jnp.where(lower, block[:half], block[half:]).astype(jnp.float32) for block in blocks]
     owned = half // 2
     return (
         jnp.concatenate([block[:owned] for block in blocks], axis=0),
@@ -313,15 +313,6 @@
         both_ref[index] = block
         block = block.astype(jnp.float32)
         rows_ref[index] = jnp.where(lower, block[coarse_rows - 2 :], block[:2]).astype(jnp.bfloat16)
-
-
-def pick_halo_kernel(paired_ref, crossed_ref, halo_ref):
-    odd = lax.rem(lax.axis_index("band"), 2) == 1
-    from_pair = jnp.logical_not(jnp.logical_xor(odd, lower_chip()))
-    for index in range(halo_ref.shape[0]):
-        paired = paired_ref[index].astype(jnp.float32)
-        crossed = crossed_ref[index].astype(jnp.float32)
-        halo_ref[index] = jnp.where(from_pair, paired, crossed).astype(halo_ref.dtype)
 
 
 def latitude_step(dates, coarse_ref, halo_ref, lat_ref, lhs_ref):
@@ -526,6 +517,12 @@
     )
     sibling = lax.ppermute(sibling, "date", sibling_way)
 
+    chain = []
+    for group in range(groups):
+        for band in range(bands):
+            to = band + (1 if group < groups // 2 else -1)
+            if 0 <= to < bands:
+                chain.append((group * bands + band, group * bands + to))
     coarse, edges = kernel_call(
         shift_rows_kernel,
         [
@@ -538,12 +535,7 @@
         own,
         peer,
     )
-    across = [(i, min(max(i + (1 if i % 2 else -1), 0), bands - 1)) for i in range(bands)]
-    crossed_rows = lax.ppermute(edges, "band", across)
-    paired_rows = lax.ppermute(edges, "band", [(i, i ^ 1) for i in range(bands)])
-    (halo,) = kernel_call(
-        pick_halo_kernel, [jax.ShapeDtypeStruct(edges.shape, bfloat16)], [], 8, 0, paired_rows, crossed_rows
-    )
+    halo = lax.ppermute(edges, ("date", "band"), chain)
     sibling_coarse = lax.ppermute(coarse, "date", sibling_way)
     sibling_halo = lax.ppermute(halo, "date", sibling_way)
 

time: 18 us -> 16.7 us (0.928)
  starting transfers between devices: 10.7 us -> 9.14 us
  waiting for transfers between devices: 2.36 us -> 3.32 us
  local copies, waits for them, and re-layouts: 0.53 us -> 0.04 us
  Pallas kernels: 3.25 us -> 3.04 us
    ppermute x2 -> x1, starting transfers between devices: 5.26 us -> 3.79 us  [two_chip_maps(): halo = lax.ppermute(edges, ('date', 'band'), chain)]
    ppermute x1, waiting for transfers between devices: 0.01 us -> 1.03 us  [two_chip_maps(): crossed = lax.ppermute(crossed, 'date', crossed_way)]
    ppermute x2 -> x1, waiting for transfers between devices: 2.29 us -> 1.71 us  [two_chip_maps(): halo = lax.ppermute(edges, ('date', 'band'), chain)]
    ppermute x1, waiting for transfers between devices: 0.06 us -> 0.56 us  [two_chip_maps(): sibling_halo = lax.ppermute(halo, 'date', sibling_way)]
    unnamed x14, local copies, waits for them, and re-layouts: 0.52 us -> 0.04 us
    pallas_call x9 -> x8, Pallas kernels: 3.25 us -> 3.04 us  [kernel_call(): pl.pallas_call(kernel, out_shape=out_shape, in_specs=[vmem] * len(operand...]
  transfers between devices with their start and end apart: 8 -> 7, of which waited for: 2 -> 3; matrix products, arithmetic and copies ran while one was open for 1% -> 1% of each run, Pallas kernels for 13% -> 13%
where the time goes in v5:
time: 16.7 us; the launch traced here: 16.5 us
  starting transfers between devices  9.14 us (55%)
  waiting for transfers between devices  3.32 us (20%)
  Pallas kernels  3.04 us (18%)
  between operations  0.8 us (5%)
    ppermute x1, starting transfers between devices, two_chip_maps(): halo = lax.ppermute(edges, ('date', 'band'), chain)  3.79 us
    pallas_call x8, Pallas kernels, kernel_call(): pl.pallas_call(kernel, out_shape=out_shape, in_specs=[vmem] * len(operand...  3.04 us
    ppermute x1, starting transfers between devices, two_chip_maps(): lax.ppermute(model_prognosis, 'date', straight_way).reshape(own.shape)  3 us
    ppermute x1, waiting for transfers between devices, two_chip_maps(): halo = lax.ppermute(edges, ('date', 'band'), chain)  1.71 us
    ppermute x1, starting transfers between devices, two_chip_maps(): straight = lax.ppermute(straight, 'date', straight_way)  1.17 us
    ppermute x1, starting transfers between devices, two_chip_maps(): sibling = lax.ppermute(sibling, 'date', sibling_way)  1.1 us
    ppermute x1, waiting for transfers between devices, two_chip_maps(): crossed = lax.ppermute(crossed, 'date', crossed_way)  1.03 us
    ppermute x1, waiting for transfers between devices, two_chip_maps(): sibling_halo = lax.ppermute(halo, 'date', sibling_way)  0.56 us
  transfers between devices with their start and end apart: 7, of which 3 were waited for; matrix products, arithmetic and copies ran while one was open for 1% of the time, Pallas kernels for 13%

profile of v5, /device:TPU:0, one launch (start us, length us, event | category | flops | bytes accessed | tf_op | source)
XLA Modules:
  0.0 16.5 jit_solution(6086069199068419342)
XLA Ops:
  0.6 0.0 copy-start.2
  0.6 0.0 copy-start
  0.6 3.0 %collective-permute-start = (bf16[2,2,5,4,360]{4,3,2,1,0:T(4,128)(2,1)}, bf16[2,2,5,4,360]{4,3,2,1,0:T(4,128)(2,1)S(1)}, u32[]{:S(2)}, u32[]{:S(2)}) collective-permute-start(bf16[2,2,5,4,360]{4,3,2,1,0:T(4,128)(2,1)} %param.7), channel_id=1, source_target_pairs={{0,16},{8,24},{16,0},{24,8},{1,17},{9,25},{17,1},{25,9},{2,18},{10... | collective-permute-start | bytes 172808 | tf_op jit(solution)/shard_map/ppermute | solution.py:493
  3.7 0.0 copy-done.2
  3.7 0.0 copy-done
  3.7 0.0 copy-start.1
  3.7 0.2 %shard_map.87 = (bf16[113,8,128]{2,1,0:T(8,128)(2,1)S(1)}, bf16[113,8,128]{2,1,0:T(8,128)(2,1)S(1)}, bf16[20,4,360]{2,1,0:T(4,128)(2,1)S(1)}) custom-call(bf16[20,16,1440]{2,1,0:T(8,128)(2,1)S(1)} %bitcast.7, bf16[20,4,360]{2,1,0:T(4,128)(2,1)S(1)} %bitcast.10, s32[72,256]{1,0:T(8,128)S(1)} %shard_map.86._.tap_ref), custom_call_target="tpu_custom_call" | custom-call | flops 100000000 | tf_op jit(solution)/shard_map/pallas_call | solution.py:463
  3.9 1.2 %collective-permute-start.5 = (bf16[113,8,128]{2,1,0:T(8,128)(2,1)S(1)}, bf16[113,8,128]{2,1,0:T(8,128)(2,1)S(1)}, u32[]{:S(2)}, u32[]{:S(2)}) collective-permute-start(bf16[113,8,128]{2,1,0:T(8,128)(2,1)S(1)} %get-tuple-element.24), channel_id=1, source_target_pairs={{0,16},{8,24},{16,0},{24,8},{1,17},{9,25},{17,1},{25,9},{2,18},{10... | collective-permute-start | bytes 694280 | tf_op jit(solution)/shard_map/ppermute | solution.py:506
  5.1 0.0 collective-permute-start.6
  5.1 0.0 copy-done.1
  5.1 0.0 copy-start.4
  5.1 0.2 %shard_map.89 = (bf16[10,8,1440]{2,1,0:T(8,128)(2,1)S(1)}, bf16[10,8,1440]{2,1,0:T(8,128)(2,1)S(1)}, f32[5,8,1440]{2,1,0:T(8,128)S(1)}) custom-call(bf16[20,16,1440]{2,1,0:T(8,128)(2,1)S(1)} %bitcast.8, bf16[10,16,1440]{2,1,0:T(8,128)(2,1)S(1)} %bitcast.9), custom_call_target="tpu_custom_call" | custom-call | flops 100000000 | tf_op jit(solution)/shard_map/pallas_call | solution.py:463
  5.3 0.0 copy-start.3
  5.3 1.1 %collective-permute-start.4 = (bf16[10,8,1440]{2,1,0:T(8,128)(2,1)S(1)}, bf16[10,8,1440]{2,1,0:T(8,128)(2,1)S(1)}, u32[]{:S(2)}, u32[]{:S(2)}) collective-permute-start(bf16[10,8,1440]{2,1,0:T(8,128)(2,1)S(1)} %get-tuple-element.19), channel_id=1, source_target_pairs={{0,8},{8,0},{16,24},{24,16},{1,9},{9,1},{17,25},{25,17},{2,10},{10... | collective-permute-start | bytes 691208 | tf_op jit(solution)/shard_map/ppermute | solution.py:518
  6.4 0.0 copy-done.4
  6.5 0.0 copy-done.3
  6.5 0.1 convert_select_fusion.lon_ref
  6.5 0.1 shard_map.90.table_ref
  6.7 0.0 collective-permute-done
  6.7 0.1 shard_map.88
  6.8 0.0 copy-start.6
  6.8 3.8 %collective-permute-start.2 = (bf16[40,2,360]{2,1,0:T(2,128)(2,1)S(1)}, bf16[40,2,360]{2,1,0:T(2,128)(2,1)S(1)}, u32[]{:S(2)}, u32[]{:S(2)}) collective-permute-start(bf16[40,2,360]{2,1,0:T(2,128)(2,1)S(1)} %get-tuple-element.18), channel_id=1, source_target_pairs={{0,1},{1,2},{2,3},{3,4},{4,5},{5,6},{6,7},{8,9},{9,10},{10,11},{11... | collective-permute-start | bytes 172808 | tf_op jit(solution)/shard_map/ppermute | solution.py:538
  10.6 0.0 copy-done.6
  10.6 0.0 copy-start.5
  10.7 0.1 collective-permute-start.1
  10.7 1.7 %collective-permute-done.2.halo_ref = bf16[40,2,360]{2,1,0:T(2,128)(2,1)S(1)} collective-permute-done((bf16[40,2,360]{2,1,0:T(2,128)(2,1)S(1)}, bf16[40,2,360]{2,1,0:T(2,128)(2,1)S(1)}, u32[]{:S(2)}, u32[]{:S(2)}) %collective-permute-start.2) | collective-permute-done | bytes 57632 | tf_op jit(solution)/shard_map/ppermute | solution.py:538
  12.5 0.0 collective-permute-start.3
  12.5 0.0 copy-done.5
  12.5 0.7 %shard_map.91 = (f32[2,5,8,1440]{3,2,1,0:T(8,128)S(1)}, f32[80,1440]{1,0:T(8,128)S(1)}) custom-call(bf16[40,4,360]{2,1,0:T(4,128)(2,1)S(1)} %get-tuple-element.17.coarse_ref, bf16[40,2,360]{2,1,0:T(2,128)(2,1)S(1)} %collective-permute-done.2.halo_ref, bf16[10,8,1440]{2,1,0:T(8,128)(2,1)S(1)} %get-tuple-element.21.truth_ref, ...), custom_call_target="tpu_custom_call" | custom-call | tf_op jit(solution)/shard_map/pallas_call | solution.py:463
  13.1 0.6 %collective-permute-done.3.halo_ref = bf16[40,2,360]{2,1,0:T(2,128)(2,1)S(1)} collective-permute-done((bf16[40,2,360]{2,1,0:T(2,128)(2,1)S(1)}, bf16[40,2,360]{2,1,0:T(2,128)(2,1)S(1)}, u32[]{:S(2)}, u32[]{:S(2)}) %collective-permute-start.3) | collective-permute-done | bytes 57632 | tf_op jit(solution)/shard_map/ppermute | solution.py:540
  13.7 0.0 collective-permute-done.1.coarse_ref
  13.7 0.0 collective-permute-done.4.truth_ref
  13.7 0.0 collective-permute-done.5.straight_ref
  13.7 0.8 %shard_map.92 = (f32[2,5,8,1440]{3,2,1,0:T(8,128)S(1)}, f32[80,1440]{1,0:T(8,128)S(1)}) custom-call(bf16[40,4,360]{2,1,0:T(4,128)(2,1)S(1)} %collective-permute-done.1.coarse_ref, bf16[40,2,360]{2,1,0:T(2,128)(2,1)S(1)} %collective-permute-done.3.halo_ref, bf16[10,8,1440]{2,1,0:T(8,128)(2,1)S(1)} %collective-permute-done.4.truth_ref, ...), custom_call_target="tpu_custom_call" | custom-call | tf_op jit(solution)/shard_map/pallas_call | solution.py:463
  14.5 1.0 %collective-permute-done.6.crossed_ref = bf16[113,8,128]{2,1,0:T(8,128)(2,1)S(1)} collective-permute-done((bf16[113,8,128]{2,1,0:T(8,128)(2,1)S(1)}, bf16[113,8,128]{2,1,0:T(8,128)(2,1)S(1)}, u32[]{:S(2)}, u32[]{:S(2)}) %collective-permute-start.6) | collective-permute-done | bytes 231456 | tf_op jit(solution)/shard_map/ppermute | solution.py:507
  15.5 0.9 %shard_map.93 = (f32[10,4,1440]{2,1,0:T(4,128)}, f32[10,4,1440]{2,1,0:T(4,128)}) custom-call(f32[2,5,8,1440]{3,2,1,0:T(8,128)S(1)} %get-tuple-element.25.before_ref, f32[80,1440]{1,0:T(8,128)S(1)} %get-tuple-element.26.fine_ref, bf16[113,8,128]{2,1,0:T(8,128)(2,1)S(1)} %collective-permute-done.6.crossed_ref, f32[5,8,1440]{2,1,0:T(8,128)S(1)} %get-tuple-element.20.normals_ref), custom_call_target="tpu_custom_call" | custom-call | tf_op jit(solution)/shard_map/pallas_call | solution.py:463
  (6 shorter events, 0.0 us)
Async XLA Ops:
  0.6 3.0 %copy-start.2 = (bf16[2,2,5,4,360]{4,3,2,1,0:T(4,128)(2,1)S(1)}, bf16[2,2,5,4,360]{4,3,2,1,0:T(4,128)(2,1)}, u32[]{:S(2)}) copy-start(bf16[2,2,5,4,360]{4,3,2,1,0:T(4,128)(2,1)} %param.7) | copy-start | bytes 172804
  0.6 3.0 %copy-start = (bf16[2,2,5,16,1440]{4,3,2,1,0:T(8,128)(2,1)S(1)}, bf16[2,2,5,16,1440]{4,3,2,1,0:T(8,128)(2,1)}, u32[]{:S(2)}) copy-start(bf16[2,2,5,16,1440]{4,3,2,1,0:T(8,128)(2,1)} %param.8) | copy-start | bytes 2764804
  0.6 6.0 %collective-permute-start = (bf16[2,2,5,4,360]{4,3,2,1,0:T(4,128)(2,1)}, bf16[2,2,5,4,360]{4,3,2,1,0:T(4,128)(2,1)S(1)}, u32[]{:S(2)}, u32[]{:S(2)}) collective-permute-start(bf16[2,2,5,4,360]{4,3,2,1,0:T(4,128)(2,1)} %param.7), channel_id=1, source_target_pairs={{0,16},{8,24},{16,0},{24,8},{1,17},{9,25},{17,1},{25,9},{2,18},{10... | collective-permute-start | bytes 172808 | tf_op jit(solution)/shard_map/ppermute | solution.py:493
  3.7 1.4 %copy-start.1 = (bf16[2,5,16,1440]{3,2,1,0:T(8,128)(2,1)S(1)}, bf16[2,5,16,1440]{3,2,1,0:T(8,128)(2,1)}, u32[]{:S(2)}) copy-start(bf16[2,5,16,1440]{3,2,1,0:T(8,128)(2,1)} %param.9) | copy-start | bytes 1382404
  3.9 9.8 %collective-permute-start.5 = (bf16[113,8,128]{2,1,0:T(8,128)(2,1)S(1)}, bf16[113,8,128]{2,1,0:T(8,128)(2,1)S(1)}, u32[]{:S(2)}, u32[]{:S(2)}) collective-permute-start(bf16[113,8,128]{2,1,0:T(8,128)(2,1)S(1)} %get-tuple-element.24), channel_id=1, source_target_pairs={{0,16},{8,24},{16,0},{24,8},{1,17},{9,25},{17,1},{25,9},{2,18},{10... | collective-permute-start | bytes 694280 | tf_op jit(solution)/shard_map/ppermute | solution.py:506
  5.1 10.4 %collective-permute-start.6 = (bf16[113,8,128]{2,1,0:T(8,128)(2,1)S(1)}, bf16[113,8,128]{2,1,0:T(8,128)(2,1)S(1)}, u32[]{:S(2)}, u32[]{:S(2)}) collective-permute-start(bf16[113,8,128]{2,1,0:T(8,128)(2,1)S(1)} %get-tuple-element.27), channel_id=1, source_target_pairs={{0,24},{8,16},{16,8},{24,0},{1,25},{9,17},{17,9},{25,1},{2,26},{10... | collective-permute-start | bytes 694280 | tf_op jit(solution)/shard_map/ppermute | solution.py:507
  5.1 1.4 %copy-start.4 = (s32[1440]{0:T(1024)S(1)}, s32[1440]{0:T(1024)}, u32[]{:S(2)}) copy-start(s32[1440]{0:T(1024)} %param.12) | copy-start | bytes 17284
  5.3 1.1 %copy-start.3 = (bf16[4,1440]{1,0:T(4,128)(2,1)S(1)}, bf16[4,1440]{1,0:T(4,128)(2,1)}, u32[]{:S(2)}) copy-start(bf16[4,1440]{1,0:T(4,128)(2,1)} %param.13) | copy-start | bytes 34564
  5.3 8.4 %collective-permute-start.4 = (bf16[10,8,1440]{2,1,0:T(8,128)(2,1)S(1)}, bf16[10,8,1440]{2,1,0:T(8,128)(2,1)S(1)}, u32[]{:S(2)}, u32[]{:S(2)}) collective-permute-start(bf16[10,8,1440]{2,1,0:T(8,128)(2,1)S(1)} %get-tuple-element.19), channel_id=1, source_target_pairs={{0,8},{8,0},{16,24},{24,16},{1,9},{9,1},{17,25},{25,17},{2,10},{10... | collective-permute-start | bytes 691208 | tf_op jit(solution)/shard_map/ppermute | solution.py:518
  6.8 3.8 %copy-start.6 = (s32[16]{0:T(128)S(1)}, s32[16]{0:T(128)}, u32[]{:S(2)}) copy-start(s32[16]{0:T(128)} %param.10) | copy-start | bytes 196
  6.8 5.6 %collective-permute-start.2 = (bf16[40,2,360]{2,1,0:T(2,128)(2,1)S(1)}, bf16[40,2,360]{2,1,0:T(2,128)(2,1)S(1)}, u32[]{:S(2)}, u32[]{:S(2)}) collective-permute-start(bf16[40,2,360]{2,1,0:T(2,128)(2,1)S(1)} %get-tuple-element.18), channel_id=1, source_target_pairs={{0,1},{1,2},{2,3},{3,4},{4,5},{5,6},{6,7},{8,9},{9,10},{10,11},{11... | collective-permute-start | bytes 172808 | tf_op jit(solution)/shard_map/ppermute | solution.py:538
  10.6 1.8 %copy-start.5 = (f32[16,4]{0,1:T(4,128)S(1)}, f32[16,4]{0,1:T(4,128)}, u32[]{:S(2)}) copy-start(f32[16,4]{0,1:T(4,128)} %param.11) | copy-start | bytes 772
  10.7 3.0 %collective-permute-start.1 = (bf16[40,4,360]{2,1,0:T(4,128)(2,1)S(1)}, bf16[40,4,360]{2,1,0:T(4,128)(2,1)S(1)}, u32[]{:S(2)}, u32[]{:S(2)}) collective-permute-start(bf16[40,4,360]{2,1,0:T(4,128)(2,1)S(1)} %get-tuple-element.17.coarse_ref), channel_id=1, source_target_pairs={{0,8},{8,0},{16,24},{24,16},{1,9},{9,1},{17,25},{25,17},{2,10},{10... | collective-permute-start | bytes 345608 | tf_op jit(solution)/shard_map/ppermute | solution.py:539
  12.5 1.2 %collective-permute-start.3 = (bf16[40,2,360]{2,1,0:T(2,128)(2,1)S(1)}, bf16[40,2,360]{2,1,0:T(2,128)(2,1)S(1)}, u32[]{:S(2)}, u32[]{:S(2)}) collective-permute-start(bf16[40,2,360]{2,1,0:T(2,128)(2,1)S(1)} %collective-permute-done.2.halo_ref), channel_id=1, source_target_pairs={{0,8},{8,0},{16,24},{24,16},{1,9},{9,1},{17,25},{25,17},{2,10},{10... | collective-permute-start | bytes 172808 | tf_op jit(solution)/shard_map/ppermute | solution.py:540

commit v6 on v2

--- a/solution.py
+++ b/solution.py
@@ -231,7 +231,7 @@
 
 
 def by_owner(ref, entries, lower):
-    blocks = [ref[entry].astype(jnp.float32) for entry in entries]
+    blocks = [ref[entry] for entry in entries]
     half = blocks[0].shape[0] // 2
     blocks = [jnp.where(lower, block[:half], block[half:]) for block in blocks]
     owned = half // 2
@@ -255,8 +255,8 @@
     if tail:
         share = LANES // tail
         tails = [block[:, full * LANES :] for block in blocks]
-        tails += [jnp.zeros((rows, tail), jnp.float32)] * (-len(tails) % share)
-        filler = [jnp.zeros((rows, LANES - share * tail), jnp.float32)] if LANES % tail else []
+        tails += [jnp.zeros((rows, tail), blocks[0].dtype)] * (-len(tails) % share)
+        filler = [jnp.zeros((rows, LANES - share * tail), blocks[0].dtype)] if LANES % tail else []
         for at in range(0, len(tails), share):
             joined = jnp.concatenate(tails[at : at + share] + filler, axis=1)
             out_ref[len(blocks) * full + at // share] = joined.astype(out_ref.dtype)
@@ -304,7 +304,7 @@
     pack_rows(crossed, crossed_ref)
     for pair in range(0, pairs, 2):
         one, two = by_owner(normal_ref, [pair, pair + 1], lower)
-        normals_ref[pair // 2] = jnp.where(first, one, two)
+        normals_ref[pair // 2] = jnp.where(first, one, two).astype(jnp.float32)
 
 
 def shift_rows_kernel(own_ref, peer_ref, both_ref, rows_ref):

time: 16.6 us -> 16.6 us (level)
  starting transfers between devices: 8.86 us -> 9.07 us
    ppermute x1, starting transfers between devices: 3.51 us -> 3.72 us  [two_chip_maps(): halo = lax.ppermute(edges, ('date', 'band'), chain)]
  transfers between devices with their start and end apart: 7 -> 7, of which waited for: 3 -> 3; matrix products, arithmetic and copies ran while one was open for 1% -> 1% of each run, Pallas kernels for 14% -> 13%
where the time goes in v6:
time: 16.6 us; the launch traced here: 16.5 us
  starting transfers between devices  9.07 us (55%)
  waiting for transfers between devices  3.28 us (20%)
  Pallas kernels  3.15 us (19%)
  between operations  0.8 us (5%)
    ppermute x1, starting transfers between devices, two_chip_maps(): halo = lax.ppermute(edges, ('date', 'band'), chain)  3.72 us
    pallas_call x8, Pallas kernels, kernel_call(): pl.pallas_call(kernel, out_shape=out_shape, in_specs=[vmem] * len(operand...  3.15 us
    ppermute x1, starting transfers between devices, two_chip_maps(): lax.ppermute(model_prognosis, 'date', straight_way).reshape(own.shape)  3 us
    ppermute x1, waiting for transfers between devices, two_chip_maps(): halo = lax.ppermute(edges, ('date', 'band'), chain)  1.71 us
    ppermute x1, starting transfers between devices, two_chip_maps(): straight = lax.ppermute(straight, 'date', straight_way)  1.17 us
    ppermute x1, waiting for transfers between devices, two_chip_maps(): crossed = lax.ppermute(crossed, 'date', crossed_way)  0.99 us
    ppermute x1, starting transfers between devices, two_chip_maps(): sibling = lax.ppermute(sibling, 'date', sibling_way)  0.79 us
    ppermute x1, waiting for transfers between devices, two_chip_maps(): sibling_halo = lax.ppermute(halo, 'date', sibling_way)  0.56 us
  transfers between devices with their start and end apart: 7, of which 3 were waited for; matrix products, arithmetic and copies ran while one was open for 1% of the time, Pallas kernels for 13%

profile of v6, /device:TPU:0, one launch (start us, length us, event | category | flops | bytes accessed | tf_op | source)
XLA Modules:
  0.0 16.5 jit_solution(5031466068326817123)
XLA Ops:
  0.6 0.0 copy-start.2
  0.6 0.0 copy-start
  0.6 3.0 %collective-permute-start = (bf16[2,2,5,4,360]{4,3,2,1,0:T(4,128)(2,1)}, bf16[2,2,5,4,360]{4,3,2,1,0:T(4,128)(2,1)S(1)}, u32[]{:S(2)}, u32[]{:S(2)}) collective-permute-start(bf16[2,2,5,4,360]{4,3,2,1,0:T(4,128)(2,1)} %param.7), channel_id=1, source_target_pairs={{0,16},{8,24},{16,0},{24,8},{1,17},{9,25},{17,1},{25,9},{2,18},{10... | collective-permute-start | bytes 172808 | tf_op jit(solution)/shard_map/ppermute | solution.py:495
  3.7 0.0 copy-done.2
  3.7 0.0 copy-done
  3.7 0.0 copy-start.1
  3.7 0.2 shard_map.87
  3.9 1.2 %collective-permute-start.5 = (bf16[113,8,128]{2,1,0:T(8,128)(2,1)S(1)}, bf16[113,8,128]{2,1,0:T(8,128)(2,1)S(1)}, u32[]{:S(2)}, u32[]{:S(2)}) collective-permute-start(bf16[113,8,128]{2,1,0:T(8,128)(2,1)S(1)} %get-tuple-element.24), channel_id=1, source_target_pairs={{0,16},{8,24},{16,0},{24,8},{1,17},{9,25},{17,1},{25,9},{2,18},{10... | collective-permute-start | bytes 694280 | tf_op jit(solution)/shard_map/ppermute | solution.py:508
  5.0 0.0 copy-done.1
  5.0 0.0 copy-start.4
  5.0 0.4 %shard_map.89 = (bf16[113,8,128]{2,1,0:T(8,128)(2,1)S(1)}, bf16[10,8,1440]{2,1,0:T(8,128)(2,1)S(1)}, bf16[10,8,1440]{2,1,0:T(8,128)(2,1)S(1)}, f32[5,8,1440]{2,1,0:T(8,128)S(1)}) custom-call(bf16[20,16,1440]{2,1,0:T(8,128)(2,1)S(1)} %bitcast.8, bf16[10,16,1440]{2,1,0:T(8,128)(2,1)S(1)} %bitcast.9, bf16[20,4,360]{2,1,0:T(4,128)(2,1)S(1)} %get-tuple-element.16.own_ref._), custom_call_target="tpu_custom_call" | custom-call | flops 100000000 | tf_op jit(solution)/shard_map/pallas_call | solution.py:465
  5.4 0.0 copy-start.3
  5.4 0.3 %collective-permute-start.6 = (bf16[113,8,128]{2,1,0:T(8,128)(2,1)S(1)}, bf16[113,8,128]{2,1,0:T(8,128)(2,1)S(1)}, u32[]{:S(2)}, u32[]{:S(2)}) collective-permute-start(bf16[113,8,128]{2,1,0:T(8,128)(2,1)S(1)} %get-tuple-element.27), channel_id=1, source_target_pairs={{0,24},{8,16},{16,8},{24,0},{1,25},{9,17},{17,9},{25,1},{2,26},{10... | collective-permute-start | bytes 694280 | tf_op jit(solution)/shard_map/ppermute | solution.py:520
  5.8 0.8 %collective-permute-start.4 = (bf16[10,8,1440]{2,1,0:T(8,128)(2,1)S(1)}, bf16[10,8,1440]{2,1,0:T(8,128)(2,1)S(1)}, u32[]{:S(2)}, u32[]{:S(2)}) collective-permute-start(bf16[10,8,1440]{2,1,0:T(8,128)(2,1)S(1)} %get-tuple-element.19), channel_id=1, source_target_pairs={{0,8},{8,0},{16,24},{24,16},{1,9},{9,1},{17,25},{25,17},{2,10},{10... | collective-permute-start | bytes 691208 | tf_op jit(solution)/shard_map/ppermute | solution.py:521
  6.6 0.0 copy-done.4
  6.6 0.0 copy-done.3
  6.6 0.1 convert_select_fusion.lon_ref
  6.6 0.1 shard_map.90.table_ref
  6.8 0.0 collective-permute-done
  6.8 0.1 shard_map.88
  6.9 0.0 copy-start.6
  6.9 3.7 %collective-permute-start.2 = (bf16[40,2,360]{2,1,0:T(2,128)(2,1)S(1)}, bf16[40,2,360]{2,1,0:T(2,128)(2,1)S(1)}, u32[]{:S(2)}, u32[]{:S(2)}) collective-permute-start(bf16[40,2,360]{2,1,0:T(2,128)(2,1)S(1)} %get-tuple-element.18), channel_id=1, source_target_pairs={{0,1},{1,2},{2,3},{3,4},{4,5},{5,6},{6,7},{8,9},{9,10},{10,11},{11... | collective-permute-start | bytes 172808 | tf_op jit(solution)/shard_map/ppermute | solution.py:541
  10.7 0.0 copy-done.6
  10.7 0.0 copy-start.5
  10.7 0.1 collective-permute-start.1
  10.8 1.7 %collective-permute-done.2.halo_ref = bf16[40,2,360]{2,1,0:T(2,128)(2,1)S(1)} collective-permute-done((bf16[40,2,360]{2,1,0:T(2,128)(2,1)S(1)}, bf16[40,2,360]{2,1,0:T(2,128)(2,1)S(1)}, u32[]{:S(2)}, u32[]{:S(2)}) %collective-permute-start.2) | collective-permute-done | bytes 57632 | tf_op jit(solution)/shard_map/ppermute | solution.py:541
  12.5 0.0 collective-permute-start.3
  12.5 0.0 copy-done.5
  12.5 0.7 %shard_map.91 = (f32[2,5,8,1440]{3,2,1,0:T(8,128)S(1)}, f32[80,1440]{1,0:T(8,128)S(1)}) custom-call(bf16[40,4,360]{2,1,0:T(4,128)(2,1)S(1)} %get-tuple-element.17.coarse_ref, bf16[40,2,360]{2,1,0:T(2,128)(2,1)S(1)} %collective-permute-done.2.halo_ref, bf16[10,8,1440]{2,1,0:T(8,128)(2,1)S(1)} %get-tuple-element.21.truth_ref, ...), custom_call_target="tpu_custom_call" | custom-call | tf_op jit(solution)/shard_map/pallas_call | solution.py:465
  13.2 0.6 %collective-permute-done.3.halo_ref = bf16[40,2,360]{2,1,0:T(2,128)(2,1)S(1)} collective-permute-done((bf16[40,2,360]{2,1,0:T(2,128)(2,1)S(1)}, bf16[40,2,360]{2,1,0:T(2,128)(2,1)S(1)}, u32[]{:S(2)}, u32[]{:S(2)}) %collective-permute-start.3) | collective-permute-done | bytes 57632 | tf_op jit(solution)/shard_map/ppermute | solution.py:543
  13.7 0.0 collective-permute-done.1.coarse_ref
  13.8 0.0 collective-permute-done.4.truth_ref
  13.8 0.0 collective-permute-done.5.straight_ref
  13.8 0.8 %shard_map.92 = (f32[2,5,8,1440]{3,2,1,0:T(8,128)S(1)}, f32[80,1440]{1,0:T(8,128)S(1)}) custom-call(bf16[40,4,360]{2,1,0:T(4,128)(2,1)S(1)} %collective-permute-done.1.coarse_ref, bf16[40,2,360]{2,1,0:T(2,128)(2,1)S(1)} %collective-permute-done.3.halo_ref, bf16[10,8,1440]{2,1,0:T(8,128)(2,1)S(1)} %collective-permute-done.4.truth_ref, ...), custom_call_target="tpu_custom_call" | custom-call | tf_op jit(solution)/shard_map/pallas_call | solution.py:465
  14.5 1.0 %collective-permute-done.6.crossed_ref = bf16[113,8,128]{2,1,0:T(8,128)(2,1)S(1)} collective-permute-done((bf16[113,8,128]{2,1,0:T(8,128)(2,1)S(1)}, bf16[113,8,128]{2,1,0:T(8,128)(2,1)S(1)}, u32[]{:S(2)}, u32[]{:S(2)}) %collective-permute-start.6) | collective-permute-done | bytes 231456 | tf_op jit(solution)/shard_map/ppermute | solution.py:520
  15.5 0.9 %shard_map.93 = (f32[10,4,1440]{2,1,0:T(4,128)}, f32[10,4,1440]{2,1,0:T(4,128)}) custom-call(f32[2,5,8,1440]{3,2,1,0:T(8,128)S(1)} %get-tuple-element.25.before_ref, f32[80,1440]{1,0:T(8,128)S(1)} %get-tuple-element.26.fine_ref, bf16[113,8,128]{2,1,0:T(8,128)(2,1)S(1)} %collective-permute-done.6.crossed_ref, f32[5,8,1440]{2,1,0:T(8,128)S(1)} %get-tuple-element.20.normals_ref), custom_call_target="tpu_custom_call" | custom-call | tf_op jit(solution)/shard_map/pallas_call | solution.py:465
  (6 shorter events, 0.0 us)
Async XLA Ops:
  0.6 3.0 %copy-start.2 = (bf16[2,2,5,4,360]{4,3,2,1,0:T(4,128)(2,1)S(1)}, bf16[2,2,5,4,360]{4,3,2,1,0:T(4,128)(2,1)}, u32[]{:S(2)}) copy-start(bf16[2,2,5,4,360]{4,3,2,1,0:T(4,128)(2,1)} %param.7) | copy-start | bytes 172804
  0.6 3.0 %copy-start = (bf16[2,2,5,16,1440]{4,3,2,1,0:T(8,128)(2,1)S(1)}, bf16[2,2,5,16,1440]{4,3,2,1,0:T(8,128)(2,1)}, u32[]{:S(2)}) copy-start(bf16[2,2,5,16,1440]{4,3,2,1,0:T(8,128)(2,1)} %param.8) | copy-start | bytes 2764804
  0.6 6.2 %collective-permute-start = (bf16[2,2,5,4,360]{4,3,2,1,0:T(4,128)(2,1)}, bf16[2,2,5,4,360]{4,3,2,1,0:T(4,128)(2,1)S(1)}, u32[]{:S(2)}, u32[]{:S(2)}) collective-permute-start(bf16[2,2,5,4,360]{4,3,2,1,0:T(4,128)(2,1)} %param.7), channel_id=1, source_target_pairs={{0,16},{8,24},{16,0},{24,8},{1,17},{9,25},{17,1},{25,9},{2,18},{10... | collective-permute-start | bytes 172808 | tf_op jit(solution)/shard_map/ppermute | solution.py:495
  3.7 1.3 %copy-start.1 = (bf16[2,5,16,1440]{3,2,1,0:T(8,128)(2,1)S(1)}, bf16[2,5,16,1440]{3,2,1,0:T(8,128)(2,1)}, u32[]{:S(2)}) copy-start(bf16[2,5,16,1440]{3,2,1,0:T(8,128)(2,1)} %param.9) | copy-start | bytes 1382404
  3.9 9.9 %collective-permute-start.5 = (bf16[113,8,128]{2,1,0:T(8,128)(2,1)S(1)}, bf16[113,8,128]{2,1,0:T(8,128)(2,1)S(1)}, u32[]{:S(2)}, u32[]{:S(2)}) collective-permute-start(bf16[113,8,128]{2,1,0:T(8,128)(2,1)S(1)} %get-tuple-element.24), channel_id=1, source_target_pairs={{0,16},{8,24},{16,0},{24,8},{1,17},{9,25},{17,1},{25,9},{2,18},{10... | collective-permute-start | bytes 694280 | tf_op jit(solution)/shard_map/ppermute | solution.py:508
  5.0 1.5 %copy-start.4 = (s32[1440]{0:T(1024)S(1)}, s32[1440]{0:T(1024)}, u32[]{:S(2)}) copy-start(s32[1440]{0:T(1024)} %param.12) | copy-start | bytes 17284
  5.4 1.1 %copy-start.3 = (bf16[4,1440]{1,0:T(4,128)(2,1)S(1)}, bf16[4,1440]{1,0:T(4,128)(2,1)}, u32[]{:S(2)}) copy-start(bf16[4,1440]{1,0:T(4,128)(2,1)} %param.13) | copy-start | bytes 34564
  5.4 10.1 %collective-permute-start.6 = (bf16[113,8,128]{2,1,0:T(8,128)(2,1)S(1)}, bf16[113,8,128]{2,1,0:T(8,128)(2,1)S(1)}, u32[]{:S(2)}, u32[]{:S(2)}) collective-permute-start(bf16[113,8,128]{2,1,0:T(8,128)(2,1)S(1)} %get-tuple-element.27), channel_id=1, source_target_pairs={{0,24},{8,16},{16,8},{24,0},{1,25},{9,17},{17,9},{25,1},{2,26},{10... | collective-permute-start | bytes 694280 | tf_op jit(solution)/shard_map/ppermute | solution.py:520
  5.8 8.0 %collective-permute-start.4 = (bf16[10,8,1440]{2,1,0:T(8,128)(2,1)S(1)}, bf16[10,8,1440]{2,1,0:T(8,128)(2,1)S(1)}, u32[]{:S(2)}, u32[]{:S(2)}) collective-permute-start(bf16[10,8,1440]{2,1,0:T(8,128)(2,1)S(1)} %get-tuple-element.19), channel_id=1, source_target_pairs={{0,8},{8,0},{16,24},{24,16},{1,9},{9,1},{17,25},{25,17},{2,10},{10... | collective-permute-start | bytes 691208 | tf_op jit(solution)/shard_map/ppermute | solution.py:521
  6.9 3.7 %copy-start.6 = (s32[16]{0:T(128)S(1)}, s32[16]{0:T(128)}, u32[]{:S(2)}) copy-start(s32[16]{0:T(128)} %param.10) | copy-start | bytes 196
  6.9 5.6 %collective-permute-start.2 = (bf16[40,2,360]{2,1,0:T(2,128)(2,1)S(1)}, bf16[40,2,360]{2,1,0:T(2,128)(2,1)S(1)}, u32[]{:S(2)}, u32[]{:S(2)}) collective-permute-start(bf16[40,2,360]{2,1,0:T(2,128)(2,1)S(1)} %get-tuple-element.18), channel_id=1, source_target_pairs={{0,1},{1,2},{2,3},{3,4},{4,5},{5,6},{6,7},{8,9},{9,10},{10,11},{11... | collective-permute-start | bytes 172808 | tf_op jit(solution)/shard_map/ppermute | solution.py:541
  10.7 1.8 %copy-start.5 = (f32[16,4]{0,1:T(4,128)S(1)}, f32[16,4]{0,1:T(4,128)}, u32[]{:S(2)}) copy-start(f32[16,4]{0,1:T(4,128)} %param.11) | copy-start | bytes 772
  10.7 3.0 %collective-permute-start.1 = (bf16[40,4,360]{2,1,0:T(4,128)(2,1)S(1)}, bf16[40,4,360]{2,1,0:T(4,128)(2,1)S(1)}, u32[]{:S(2)}, u32[]{:S(2)}) collective-permute-start(bf16[40,4,360]{2,1,0:T(4,128)(2,1)S(1)} %get-tuple-element.17.coarse_ref), channel_id=1, source_target_pairs={{0,8},{8,0},{16,24},{24,16},{1,9},{9,1},{17,25},{25,17},{2,10},{10... | collective-permute-start | bytes 345608 | tf_op jit(solution)/shard_map/ppermute | solution.py:542
  12.5 1.2 %collective-permute-start.3 = (bf16[40,2,360]{2,1,0:T(2,128)(2,1)S(1)}, bf16[40,2,360]{2,1,0:T(2,128)(2,1)S(1)}, u32[]{:S(2)}, u32[]{:S(2)}) collective-permute-start(bf16[40,2,360]{2,1,0:T(2,128)(2,1)S(1)} %collective-permute-done.2.halo_ref), channel_id=1, source_target_pairs={{0,8},{8,0},{16,24},{24,16},{1,9},{9,1},{17,25},{25,17},{2,10},{10... | collective-permute-start | bytes 172808 | tf_op jit(solution)/shard_map/ppermute | solution.py:543

commit v7 on v6

--- a/solution.py
+++ b/solution.py
@@ -310,10 +310,11 @@
 def shift_rows_kernel(own_ref, peer_ref, both_ref, rows_ref):
     lower = lower_chip()
     fields, coarse_rows, _ = own_ref.shape
+    depth = both_ref.shape[2]
     for index in range(2 * fields):
-        block = (own_ref if index < fields else peer_ref)[index % fields]
-        both_ref[index] = block
-        block = block.astype(jnp.float32)
+        block = (own_ref if index < fields else peer_ref)[index % fields].astype(jnp.float32)
+        block = wrapped_rows(block, depth)
+        both_ref[index] = block.astype(both_ref.dtype)
         rows_ref[index] = jnp.where(lower, block[coarse_rows - 2 :], block[:2]).astype(jnp.bfloat16)
 
 
@@ -347,7 +348,7 @@
                 edge = jnp.where(outside, 0.0, halo_ref[index].astype(jnp.float32))
                 below = jnp.concatenate([edge, inner], axis=0)
                 above = jnp.concatenate([inner, edge], axis=0)
-                wrapped = wrapped_rows(jnp.where(lower, below, above), depth)
+                wrapped = jnp.where(lower, below, above)
                 sources.append(jnp.where(first, wrapped[: TAPS + 1], wrapped[1 : TAPS + 2]))
             total = 0.0
             for tap in range(TAPS + 1):
@@ -529,8 +530,8 @@
     coarse, edges = kernel_call(
         shift_rows_kernel,
         [
-            jax.ShapeDtypeStruct((2 * fields, coarse_rows, sparse), bfloat16),
-            jax.ShapeDtypeStruct((2 * fields, 2, sparse), bfloat16),
+            jax.ShapeDtypeStruct((2 * fields, coarse_rows, depth), bfloat16),
+            jax.ShapeDtypeStruct((2 * fields, 2, depth), bfloat16),
         ],
         [],
         8,

time: 16.6 us -> 16.6 us (level)
  waiting for transfers between devices: 3.28 us -> 3.09 us
  Pallas kernels: 3.15 us -> 3.33 us
    pallas_call x8, Pallas kernels: 3.15 us -> 3.33 us  [kernel_call(): pl.pallas_call(kernel, out_shape=out_shape, in_specs=[vmem] * len(operand...]
  transfers between devices with their start and end apart: 7 -> 7, of which waited for: 3 -> 3; matrix products, arithmetic and copies ran while one was open for 1% -> 1% of each run, Pallas kernels for 13% -> 15%
where the time goes in v7:
time: 16.6 us; the launch traced here: 16.5 us
  starting transfers between devices  9.08 us (55%)
  Pallas kernels  3.33 us (20%)
  waiting for transfers between devices  3.09 us (19%)
  between operations  0.8 us (5%)
    ppermute x1, starting transfers between devices, two_chip_maps(): halo = lax.ppermute(edges, ('date', 'band'), chain)  3.73 us
    pallas_call x8, Pallas kernels, kernel_call(): pl.pallas_call(kernel, out_shape=out_shape, in_specs=[vmem] * len(operand...  3.33 us
    ppermute x1, starting transfers between devices, two_chip_maps(): lax.ppermute(model_prognosis, 'date', straight_way).reshape(own.shape)  3 us
    ppermute x1, waiting for transfers between devices, two_chip_maps(): halo = lax.ppermute(edges, ('date', 'band'), chain)  1.71 us
    ppermute x1, starting transfers between devices, two_chip_maps(): straight = lax.ppermute(straight, 'date', straight_way)  1.17 us
    ppermute x1, waiting for transfers between devices, two_chip_maps(): crossed = lax.ppermute(crossed, 'date', crossed_way)  0.84 us
    ppermute x1, starting transfers between devices, two_chip_maps(): sibling = lax.ppermute(sibling, 'date', sibling_way)  0.79 us
    ppermute x1, waiting for transfers between devices, two_chip_maps(): sibling_halo = lax.ppermute(halo, 'date', sibling_way)  0.53 us
  transfers between devices with their start and end apart: 7, of which 3 were waited for; matrix products, arithmetic and copies ran while one was open for 1% of the time, Pallas kernels for 15%

profile of v7, /device:TPU:0, one launch (start us, length us, event | category | flops | bytes accessed | tf_op | source)
XLA Modules:
  0.0 16.5 jit_solution(732033349455319185)
XLA Ops:
  0.6 0.0 copy-start.2
  0.6 0.0 copy-start
  0.6 3.0 %collective-permute-start = (bf16[2,2,5,4,360]{4,3,2,1,0:T(4,128)(2,1)}, bf16[2,2,5,4,360]{4,3,2,1,0:T(4,128)(2,1)S(1)}, u32[]{:S(2)}, u32[]{:S(2)}) collective-permute-start(bf16[2,2,5,4,360]{4,3,2,1,0:T(4,128)(2,1)} %param.7), channel_id=1, source_target_pairs={{0,16},{8,24},{16,0},{24,8},{1,17},{9,25},{17,1},{25,9},{2,18},{10... | collective-permute-start | bytes 172808 | tf_op jit(solution)/shard_map/ppermute | solution.py:496
  3.7 0.0 copy-done.2
  3.7 0.0 copy-done
  3.7 0.0 copy-start.1
  3.7 0.2 shard_map.87
  3.9 1.2 %collective-permute-start.5 = (bf16[113,8,128]{2,1,0:T(8,128)(2,1)S(1)}, bf16[113,8,128]{2,1,0:T(8,128)(2,1)S(1)}, u32[]{:S(2)}, u32[]{:S(2)}) collective-permute-start(bf16[113,8,128]{2,1,0:T(8,128)(2,1)S(1)} %get-tuple-element.24), channel_id=1, source_target_pairs={{0,16},{8,24},{16,0},{24,8},{1,17},{9,25},{17,1},{25,9},{2,18},{10... | collective-permute-start | bytes 694280 | tf_op jit(solution)/shard_map/ppermute | solution.py:509
  5.0 0.0 copy-done.1
  5.0 0.0 copy-start.4
  5.0 0.4 %shard_map.89 = (bf16[113,8,128]{2,1,0:T(8,128)(2,1)S(1)}, bf16[10,8,1440]{2,1,0:T(8,128)(2,1)S(1)}, bf16[10,8,1440]{2,1,0:T(8,128)(2,1)S(1)}, f32[5,8,1440]{2,1,0:T(8,128)S(1)}) custom-call(bf16[20,16,1440]{2,1,0:T(8,128)(2,1)S(1)} %bitcast.8, bf16[10,16,1440]{2,1,0:T(8,128)(2,1)S(1)} %bitcast.9, bf16[20,4,360]{2,1,0:T(4,128)(2,1)S(1)} %get-tuple-element.16.own_ref._), custom_call_target="tpu_custom_call" | custom-call | flops 100000000 | tf_op jit(solution)/shard_map/pallas_call | solution.py:466
  5.4 0.0 copy-start.3
  5.4 0.3 %collective-permute-start.6 = (bf16[113,8,128]{2,1,0:T(8,128)(2,1)S(1)}, bf16[113,8,128]{2,1,0:T(8,128)(2,1)S(1)}, u32[]{:S(2)}, u32[]{:S(2)}) collective-permute-start(bf16[113,8,128]{2,1,0:T(8,128)(2,1)S(1)} %get-tuple-element.27), channel_id=1, source_target_pairs={{0,24},{8,16},{16,8},{24,0},{1,25},{9,17},{17,9},{25,1},{2,26},{10... | collective-permute-start | bytes 694280 | tf_op jit(solution)/shard_map/ppermute | solution.py:521
  5.8 0.8 %collective-permute-start.4 = (bf16[10,8,1440]{2,1,0:T(8,128)(2,1)S(1)}, bf16[10,8,1440]{2,1,0:T(8,128)(2,1)S(1)}, u32[]{:S(2)}, u32[]{:S(2)}) collective-permute-start(bf16[10,8,1440]{2,1,0:T(8,128)(2,1)S(1)} %get-tuple-element.19), channel_id=1, source_target_pairs={{0,8},{8,0},{16,24},{24,16},{1,9},{9,1},{17,25},{25,17},{2,10},{10... | collective-permute-start | bytes 691208 | tf_op jit(solution)/shard_map/ppermute | solution.py:522
  6.6 0.0 copy-done.4
  6.6 0.0 copy-done.3
  6.6 0.1 convert_select_fusion.lon_ref
  6.6 0.1 shard_map.90.table_ref
  6.8 0.0 collective-permute-done
  6.8 0.2 %shard_map.88 = (bf16[40,4,384]{2,1,0:T(4,128)(2,1)S(1)}, bf16[40,2,384]{2,1,0:T(2,128)(2,1)S(1)}) custom-call(bf16[20,4,360]{2,1,0:T(4,128)(2,1)S(1)} %get-tuple-element.16.own_ref._, bf16[20,4,360]{2,1,0:T(4,128)(2,1)S(1)} %bitcast.11), custom_call_target="tpu_custom_call" | custom-call | flops 100000000 | tf_op jit(solution)/shard_map/pallas_call | solution.py:466
  7.0 0.0 copy-start.6
  7.0 3.7 %collective-permute-start.2 = (bf16[40,2,384]{2,1,0:T(2,128)(2,1)S(1)}, bf16[40,2,384]{2,1,0:T(2,128)(2,1)S(1)}, u32[]{:S(2)}, u32[]{:S(2)}) collective-permute-start(bf16[40,2,384]{2,1,0:T(2,128)(2,1)S(1)} %get-tuple-element.18), channel_id=1, source_target_pairs={{0,1},{1,2},{2,3},{3,4},{4,5},{5,6},{6,7},{8,9},{9,10},{10,11},{11... | collective-permute-start | bytes 184328 | tf_op jit(solution)/shard_map/ppermute | solution.py:542
  10.8 0.0 copy-done.6
  10.8 0.0 copy-start.5
  10.8 0.1 collective-permute-start.1
  10.9 1.7 %collective-permute-done.2.halo_ref = bf16[40,2,384]{2,1,0:T(2,128)(2,1)S(1)} collective-permute-done((bf16[40,2,384]{2,1,0:T(2,128)(2,1)S(1)}, bf16[40,2,384]{2,1,0:T(2,128)(2,1)S(1)}, u32[]{:S(2)}, u32[]{:S(2)}) %collective-permute-start.2) | collective-permute-done | bytes 61472 | tf_op jit(solution)/shard_map/ppermute | solution.py:542
  12.6 0.0 collective-permute-start.3
  12.6 0.0 copy-done.5
  12.6 0.7 %shard_map.91 = (f32[2,5,8,1440]{3,2,1,0:T(8,128)S(1)}, f32[80,1440]{1,0:T(8,128)S(1)}) custom-call(bf16[40,4,384]{2,1,0:T(4,128)(2,1)S(1)} %get-tuple-element.17.coarse_ref, bf16[40,2,384]{2,1,0:T(2,128)(2,1)S(1)} %collective-permute-done.2.halo_ref, bf16[10,8,1440]{2,1,0:T(8,128)(2,1)S(1)} %get-tuple-element.21.truth_ref, ...), custom_call_target="tpu_custom_call" | custom-call | tf_op jit(solution)/shard_map/pallas_call | solution.py:466
  13.3 0.5 %collective-permute-done.3.halo_ref = bf16[40,2,384]{2,1,0:T(2,128)(2,1)S(1)} collective-permute-done((bf16[40,2,384]{2,1,0:T(2,128)(2,1)S(1)}, bf16[40,2,384]{2,1,0:T(2,128)(2,1)S(1)}, u32[]{:S(2)}, u32[]{:S(2)}) %collective-permute-start.3) | collective-permute-done | bytes 61472 | tf_op jit(solution)/shard_map/ppermute | solution.py:544
  13.9 0.0 collective-permute-done.1.coarse_ref
  13.9 0.0 collective-permute-done.4.truth_ref
  13.9 0.0 collective-permute-done.5.straight_ref
  13.9 0.8 %shard_map.92 = (f32[2,5,8,1440]{3,2,1,0:T(8,128)S(1)}, f32[80,1440]{1,0:T(8,128)S(1)}) custom-call(bf16[40,4,384]{2,1,0:T(4,128)(2,1)S(1)} %collective-permute-done.1.coarse_ref, bf16[40,2,384]{2,1,0:T(2,128)(2,1)S(1)} %collective-permute-done.3.halo_ref, bf16[10,8,1440]{2,1,0:T(8,128)(2,1)S(1)} %collective-permute-done.4.truth_ref, ...), custom_call_target="tpu_custom_call" | custom-call | tf_op jit(solution)/shard_map/pallas_call | solution.py:466
  14.7 0.8 %collective-permute-done.6.crossed_ref = bf16[113,8,128]{2,1,0:T(8,128)(2,1)S(1)} collective-permute-done((bf16[113,8,128]{2,1,0:T(8,128)(2,1)S(1)}, bf16[113,8,128]{2,1,0:T(8,128)(2,1)S(1)}, u32[]{:S(2)}, u32[]{:S(2)}) %collective-permute-start.6) | collective-permute-done | bytes 231456 | tf_op jit(solution)/shard_map/ppermute | solution.py:521
  15.5 0.9 %shard_map.93 = (f32[10,4,1440]{2,1,0:T(4,128)}, f32[10,4,1440]{2,1,0:T(4,128)}) custom-call(f32[2,5,8,1440]{3,2,1,0:T(8,128)S(1)} %get-tuple-element.25.before_ref, f32[80,1440]{1,0:T(8,128)S(1)} %get-tuple-element.26.fine_ref, bf16[113,8,128]{2,1,0:T(8,128)(2,1)S(1)} %collective-permute-done.6.crossed_ref, f32[5,8,1440]{2,1,0:T(8,128)S(1)} %get-tuple-element.20.normals_ref), custom_call_target="tpu_custom_call" | custom-call | tf_op jit(solution)/shard_map/pallas_call | solution.py:466
  (6 shorter events, 0.0 us)
Async XLA Ops:
  0.6 3.0 %copy-start.2 = (bf16[2,2,5,4,360]{4,3,2,1,0:T(4,128)(2,1)S(1)}, bf16[2,2,5,4,360]{4,3,2,1,0:T(4,128)(2,1)}, u32[]{:S(2)}) copy-start(bf16[2,2,5,4,360]{4,3,2,1,0:T(4,128)(2,1)} %param.7) | copy-start | bytes 172804
  0.6 3.0 %copy-start = (bf16[2,2,5,16,1440]{4,3,2,1,0:T(8,128)(2,1)S(1)}, bf16[2,2,5,16,1440]{4,3,2,1,0:T(8,128)(2,1)}, u32[]{:S(2)}) copy-start(bf16[2,2,5,16,1440]{4,3,2,1,0:T(8,128)(2,1)} %param.8) | copy-start | bytes 2764804
  0.6 6.2 %collective-permute-start = (bf16[2,2,5,4,360]{4,3,2,1,0:T(4,128)(2,1)}, bf16[2,2,5,4,360]{4,3,2,1,0:T(4,128)(2,1)S(1)}, u32[]{:S(2)}, u32[]{:S(2)}) collective-permute-start(bf16[2,2,5,4,360]{4,3,2,1,0:T(4,128)(2,1)} %param.7), channel_id=1, source_target_pairs={{0,16},{8,24},{16,0},{24,8},{1,17},{9,25},{17,1},{25,9},{2,18},{10... | collective-permute-start | bytes 172808 | tf_op jit(solution)/shard_map/ppermute | solution.py:496
  3.7 1.3 %copy-start.1 = (bf16[2,5,16,1440]{3,2,1,0:T(8,128)(2,1)S(1)}, bf16[2,5,16,1440]{3,2,1,0:T(8,128)(2,1)}, u32[]{:S(2)}) copy-start(bf16[2,5,16,1440]{3,2,1,0:T(8,128)(2,1)} %param.9) | copy-start | bytes 1382404
  3.9 10.0 %collective-permute-start.5 = (bf16[113,8,128]{2,1,0:T(8,128)(2,1)S(1)}, bf16[113,8,128]{2,1,0:T(8,128)(2,1)S(1)}, u32[]{:S(2)}, u32[]{:S(2)}) collective-permute-start(bf16[113,8,128]{2,1,0:T(8,128)(2,1)S(1)} %get-tuple-element.24), channel_id=1, source_target_pairs={{0,16},{8,24},{16,0},{24,8},{1,17},{9,25},{17,1},{25,9},{2,18},{10... | collective-permute-start | bytes 694280 | tf_op jit(solution)/shard_map/ppermute | solution.py:509
  5.0 1.5 %copy-start.4 = (s32[1440]{0:T(1024)S(1)}, s32[1440]{0:T(1024)}, u32[]{:S(2)}) copy-start(s32[1440]{0:T(1024)} %param.12) | copy-start | bytes 17284
  5.4 1.1 %copy-start.3 = (bf16[4,1440]{1,0:T(4,128)(2,1)S(1)}, bf16[4,1440]{1,0:T(4,128)(2,1)}, u32[]{:S(2)}) copy-start(bf16[4,1440]{1,0:T(4,128)(2,1)} %param.13) | copy-start | bytes 34564
  5.4 10.1 %collective-permute-start.6 = (bf16[113,8,128]{2,1,0:T(8,128)(2,1)S(1)}, bf16[113,8,128]{2,1,0:T(8,128)(2,1)S(1)}, u32[]{:S(2)}, u32[]{:S(2)}) collective-permute-start(bf16[113,8,128]{2,1,0:T(8,128)(2,1)S(1)} %get-tuple-element.27), channel_id=1, source_target_pairs={{0,24},{8,16},{16,8},{24,0},{1,25},{9,17},{17,9},{25,1},{2,26},{10... | collective-permute-start | bytes 694280 | tf_op jit(solution)/shard_map/ppermute | solution.py:521
  5.8 8.1 %collective-permute-start.4 = (bf16[10,8,1440]{2,1,0:T(8,128)(2,1)S(1)}, bf16[10,8,1440]{2,1,0:T(8,128)(2,1)S(1)}, u32[]{:S(2)}, u32[]{:S(2)}) collective-permute-start(bf16[10,8,1440]{2,1,0:T(8,128)(2,1)S(1)} %get-tuple-element.19), channel_id=1, source_target_pairs={{0,8},{8,0},{16,24},{24,16},{1,9},{9,1},{17,25},{25,17},{2,10},{10... | collective-permute-start | bytes 691208 | tf_op jit(solution)/shard_map/ppermute | solution.py:522
  7.0 3.8 %copy-start.6 = (s32[16]{0:T(128)S(1)}, s32[16]{0:T(128)}, u32[]{:S(2)}) copy-start(s32[16]{0:T(128)} %param.10) | copy-start | bytes 196
  7.0 5.6 %collective-permute-start.2 = (bf16[40,2,384]{2,1,0:T(2,128)(2,1)S(1)}, bf16[40,2,384]{2,1,0:T(2,128)(2,1)S(1)}, u32[]{:S(2)}, u32[]{:S(2)}) collective-permute-start(bf16[40,2,384]{2,1,0:T(2,128)(2,1)S(1)} %get-tuple-element.18), channel_id=1, source_target_pairs={{0,1},{1,2},{2,3},{3,4},{4,5},{5,6},{6,7},{8,9},{9,10},{10,11},{11... | collective-permute-start | bytes 184328 | tf_op jit(solution)/shard_map/ppermute | solution.py:542
  10.8 1.8 %copy-start.5 = (f32[16,4]{0,1:T(4,128)S(1)}, f32[16,4]{0,1:T(4,128)}, u32[]{:S(2)}) copy-start(f32[16,4]{0,1:T(4,128)} %param.11) | copy-start | bytes 772
  10.8 3.0 %collective-permute-start.1 = (bf16[40,4,384]{2,1,0:T(4,128)(2,1)S(1)}, bf16[40,4,384]{2,1,0:T(4,128)(2,1)S(1)}, u32[]{:S(2)}, u32[]{:S(2)}) collective-permute-start(bf16[40,4,384]{2,1,0:T(4,128)(2,1)S(1)} %get-tuple-element.17.coarse_ref), channel_id=1, source_target_pairs={{0,8},{8,0},{16,24},{24,16},{1,9},{9,1},{17,25},{25,17},{2,10},{10... | collective-permute-start | bytes 368648 | tf_op jit(solution)/shard_map/ppermute | solution.py:543
  12.6 1.2 %collective-permute-start.3 = (bf16[40,2,384]{2,1,0:T(2,128)(2,1)S(1)}, bf16[40,2,384]{2,1,0:T(2,128)(2,1)S(1)}, u32[]{:S(2)}, u32[]{:S(2)}) collective-permute-start(bf16[40,2,384]{2,1,0:T(2,128)(2,1)S(1)} %collective-permute-done.2.halo_ref), channel_id=1, source_target_pairs={{0,8},{8,0},{16,24},{24,16},{1,9},{9,1},{17,25},{25,17},{2,10},{10... | collective-permute-start | bytes 184328 | tf_op jit(solution)/shard_map/ppermute | solution.py:544

commit v8 on v5

--- a/solution.py
+++ b/solution.py
@@ -233,7 +233,7 @@
 def by_owner(ref, entries, lower):
     blocks = [ref[entry] for entry in entries]
     half = blocks[0].shape[0] // 2
-    blocks = [jnp.where(lower, block[:half], block[half:]).astype(jnp.float32) for block in blocks]
+    blocks = [jnp.where(lower, block[:half], block[half:]) for block in blocks]
     owned = half // 2
     return (
         jnp.concatenate([block[:owned] for block in blocks], axis=0),
@@ -255,8 +255,8 @@
     if tail:
         share = LANES // tail
         tails = [block[:, full * LANES :] for block in blocks]
-        tails += [jnp.zeros((rows, tail), jnp.float32)] * (-len(tails) % share)
-        filler = [jnp.zeros((rows, LANES - share * tail), jnp.float32)] if LANES % tail else []
+        tails += [jnp.zeros((rows, tail), blocks[0].dtype)] * (-len(tails) % share)
+        filler = [jnp.zeros((rows, LANES - share * tail), blocks[0].dtype)] if LANES % tail else []
         for at in range(0, len(tails), share):
             joined = jnp.concatenate(tails[at : at + share] + filler, axis=1)
             out_ref[len(blocks) * full + at // share] = joined.astype(out_ref.dtype)
@@ -302,7 +302,7 @@
         sibling_ref[at] = jnp.where(first, two, one).astype(sibling_ref.dtype)
     for pair in range(0, pairs, 2):
         one, two = by_owner(normal_ref, [pair, pair + 1], lower)
-        normals_ref[pair // 2] = jnp.where(first, one, two)
+        normals_ref[pair // 2] = jnp.where(first, one, two).astype(jnp.float32)
 
 
 def shift_rows_kernel(own_ref, peer_ref, both_ref, rows_ref):

time: 16.7 us -> 16.7 us (level)
  no operation moved by 1% of the time
where the time goes in v8:
time: 16.7 us; the launch traced here: 16.5 us
  starting transfers between devices  9.09 us (54%)
  waiting for transfers between devices  3.34 us (20%)
  Pallas kernels  3.08 us (18%)
  between operations  0.79 us (5%)
    ppermute x1, starting transfers between devices, two_chip_maps(): halo = lax.ppermute(edges, ('date', 'band'), chain)  3.72 us
    pallas_call x8, Pallas kernels, kernel_call(): pl.pallas_call(kernel, out_shape=out_shape, in_specs=[vmem] * len(operand...  3.08 us
    ppermute x1, starting transfers between devices, two_chip_maps(): lax.ppermute(model_prognosis, 'date', straight_way).reshape(own.shape)  3 us
    ppermute x1, waiting for transfers between devices, two_chip_maps(): halo = lax.ppermute(edges, ('date', 'band'), chain)  1.7 us
    ppermute x1, starting transfers between devices, two_chip_maps(): straight = lax.ppermute(straight, 'date', straight_way)  1.17 us
    ppermute x1, starting transfers between devices, two_chip_maps(): sibling = lax.ppermute(sibling, 'date', sibling_way)  1.1 us
    ppermute x1, waiting for transfers between devices, two_chip_maps(): crossed = lax.ppermute(crossed, 'date', crossed_way)  1.06 us
    ppermute x1, waiting for transfers between devices, two_chip_maps(): sibling_halo = lax.ppermute(halo, 'date', sibling_way)  0.56 us
  transfers between devices with their start and end apart: 7, of which 3 were waited for; matrix products, arithmetic and copies ran while one was open for 1% of the time, Pallas kernels for 13%

profile of v8, /device:TPU:0, one launch (start us, length us, event | category | flops | bytes accessed | tf_op | source)
XLA Modules:
  0.0 16.5 jit_solution(12076440577989974264)
XLA Ops:
  0.6 0.0 copy-start.2
  0.6 0.0 copy-start
  0.6 3.0 %collective-permute-start = (bf16[2,2,5,4,360]{4,3,2,1,0:T(4,128)(2,1)}, bf16[2,2,5,4,360]{4,3,2,1,0:T(4,128)(2,1)S(1)}, u32[]{:S(2)}, u32[]{:S(2)}) collective-permute-start(bf16[2,2,5,4,360]{4,3,2,1,0:T(4,128)(2,1)} %param.7), channel_id=1, source_target_pairs={{0,16},{8,24},{16,0},{24,8},{1,17},{9,25},{17,1},{25,9},{2,18},{10... | collective-permute-start | bytes 172808 | tf_op jit(solution)/shard_map/ppermute | solution.py:493
  3.7 0.0 copy-done.2
  3.7 0.0 copy-done
  3.7 0.0 copy-start.1
  3.7 0.2 %shard_map.87 = (bf16[113,8,128]{2,1,0:T(8,128)(2,1)S(1)}, bf16[113,8,128]{2,1,0:T(8,128)(2,1)S(1)}, bf16[20,4,360]{2,1,0:T(4,128)(2,1)S(1)}) custom-call(bf16[20,16,1440]{2,1,0:T(8,128)(2,1)S(1)} %bitcast.7, bf16[20,4,360]{2,1,0:T(4,128)(2,1)S(1)} %bitcast.10, s32[72,256]{1,0:T(8,128)S(1)} %shard_map.86._.tap_ref), custom_call_target="tpu_custom_call" | custom-call | flops 100000000 | tf_op jit(solution)/shard_map/pallas_call | solution.py:463
  3.9 1.2 %collective-permute-start.5 = (bf16[113,8,128]{2,1,0:T(8,128)(2,1)S(1)}, bf16[113,8,128]{2,1,0:T(8,128)(2,1)S(1)}, u32[]{:S(2)}, u32[]{:S(2)}) collective-permute-start(bf16[113,8,128]{2,1,0:T(8,128)(2,1)S(1)} %get-tuple-element.24), channel_id=1, source_target_pairs={{0,16},{8,24},{16,0},{24,8},{1,17},{9,25},{17,1},{25,9},{2,18},{10... | collective-permute-start | bytes 694280 | tf_op jit(solution)/shard_map/ppermute | solution.py:506
  5.1 0.0 collective-permute-start.6
  5.1 0.0 copy-done.1
  5.1 0.0 copy-start.4
  5.1 0.2 %shard_map.89 = (bf16[10,8,1440]{2,1,0:T(8,128)(2,1)S(1)}, bf16[10,8,1440]{2,1,0:T(8,128)(2,1)S(1)}, f32[5,8,1440]{2,1,0:T(8,128)S(1)}) custom-call(bf16[20,16,1440]{2,1,0:T(8,128)(2,1)S(1)} %bitcast.8, bf16[10,16,1440]{2,1,0:T(8,128)(2,1)S(1)} %bitcast.9), custom_call_target="tpu_custom_call" | custom-call | flops 100000000 | tf_op jit(solution)/shard_map/pallas_call | solution.py:463
  5.4 0.0 copy-start.3
  5.4 1.1 %collective-permute-start.4 = (bf16[10,8,1440]{2,1,0:T(8,128)(2,1)S(1)}, bf16[10,8,1440]{2,1,0:T(8,128)(2,1)S(1)}, u32[]{:S(2)}, u32[]{:S(2)}) collective-permute-start(bf16[10,8,1440]{2,1,0:T(8,128)(2,1)S(1)} %get-tuple-element.19), channel_id=1, source_target_pairs={{0,8},{8,0},{16,24},{24,16},{1,9},{9,1},{17,25},{25,17},{2,10},{10... | collective-permute-start | bytes 691208 | tf_op jit(solution)/shard_map/ppermute | solution.py:518
  6.5 0.0 copy-done.4
  6.5 0.0 copy-done.3
  6.5 0.1 convert_select_fusion.lon_ref
  6.6 0.1 shard_map.90.table_ref
  6.7 0.0 collective-permute-done
  6.7 0.1 shard_map.88
  6.8 0.0 copy-start.6
  6.8 3.7 %collective-permute-start.2 = (bf16[40,2,360]{2,1,0:T(2,128)(2,1)S(1)}, bf16[40,2,360]{2,1,0:T(2,128)(2,1)S(1)}, u32[]{:S(2)}, u32[]{:S(2)}) collective-permute-start(bf16[40,2,360]{2,1,0:T(2,128)(2,1)S(1)} %get-tuple-element.18), channel_id=1, source_target_pairs={{0,1},{1,2},{2,3},{3,4},{4,5},{5,6},{6,7},{8,9},{9,10},{10,11},{11... | collective-permute-start | bytes 172808 | tf_op jit(solution)/shard_map/ppermute | solution.py:538
  10.6 0.0 copy-done.6
  10.6 0.0 copy-start.5
  10.6 0.1 collective-permute-start.1
  10.7 1.7 %collective-permute-done.2.halo_ref = bf16[40,2,360]{2,1,0:T(2,128)(2,1)S(1)} collective-permute-done((bf16[40,2,360]{2,1,0:T(2,128)(2,1)S(1)}, bf16[40,2,360]{2,1,0:T(2,128)(2,1)S(1)}, u32[]{:S(2)}, u32[]{:S(2)}) %collective-permute-start.2) | collective-permute-done | bytes 57632 | tf_op jit(solution)/shard_map/ppermute | solution.py:538
  12.4 0.0 collective-permute-start.3
  12.4 0.0 copy-done.5
  12.4 0.7 %shard_map.91 = (f32[2,5,8,1440]{3,2,1,0:T(8,128)S(1)}, f32[80,1440]{1,0:T(8,128)S(1)}) custom-call(bf16[40,4,360]{2,1,0:T(4,128)(2,1)S(1)} %get-tuple-element.17.coarse_ref, bf16[40,2,360]{2,1,0:T(2,128)(2,1)S(1)} %collective-permute-done.2.halo_ref, bf16[10,8,1440]{2,1,0:T(8,128)(2,1)S(1)} %get-tuple-element.21.truth_ref, ...), custom_call_target="tpu_custom_call" | custom-call | tf_op jit(solution)/shard_map/pallas_call | solution.py:463
  13.1 0.6 %collective-permute-done.3.halo_ref = bf16[40,2,360]{2,1,0:T(2,128)(2,1)S(1)} collective-permute-done((bf16[40,2,360]{2,1,0:T(2,128)(2,1)S(1)}, bf16[40,2,360]{2,1,0:T(2,128)(2,1)S(1)}, u32[]{:S(2)}, u32[]{:S(2)}) %collective-permute-start.3) | collective-permute-done | bytes 57632 | tf_op jit(solution)/shard_map/ppermute | solution.py:540
  13.7 0.0 collective-permute-done.1.coarse_ref
  13.7 0.0 collective-permute-done.4.truth_ref
  13.7 0.0 collective-permute-done.5.straight_ref
  13.7 0.8 %shard_map.92 = (f32[2,5,8,1440]{3,2,1,0:T(8,128)S(1)}, f32[80,1440]{1,0:T(8,128)S(1)}) custom-call(bf16[40,4,360]{2,1,0:T(4,128)(2,1)S(1)} %collective-permute-done.1.coarse_ref, bf16[40,2,360]{2,1,0:T(2,128)(2,1)S(1)} %collective-permute-done.3.halo_ref, bf16[10,8,1440]{2,1,0:T(8,128)(2,1)S(1)} %collective-permute-done.4.truth_ref, ...), custom_call_target="tpu_custom_call" | custom-call | tf_op jit(solution)/shard_map/pallas_call | solution.py:463
  14.5 1.1 %collective-permute-done.6.crossed_ref = bf16[113,8,128]{2,1,0:T(8,128)(2,1)S(1)} collective-permute-done((bf16[113,8,128]{2,1,0:T(8,128)(2,1)S(1)}, bf16[113,8,128]{2,1,0:T(8,128)(2,1)S(1)}, u32[]{:S(2)}, u32[]{:S(2)}) %collective-permute-start.6) | collective-permute-done | bytes 231456 | tf_op jit(solution)/shard_map/ppermute | solution.py:507
  15.5 0.9 %shard_map.93 = (f32[10,4,1440]{2,1,0:T(4,128)}, f32[10,4,1440]{2,1,0:T(4,128)}) custom-call(f32[2,5,8,1440]{3,2,1,0:T(8,128)S(1)} %get-tuple-element.25.before_ref, f32[80,1440]{1,0:T(8,128)S(1)} %get-tuple-element.26.fine_ref, bf16[113,8,128]{2,1,0:T(8,128)(2,1)S(1)} %collective-permute-done.6.crossed_ref, f32[5,8,1440]{2,1,0:T(8,128)S(1)} %get-tuple-element.20.normals_ref), custom_call_target="tpu_custom_call" | custom-call | tf_op jit(solution)/shard_map/pallas_call | solution.py:463
  (6 shorter events, 0.0 us)
Async XLA Ops:
  0.6 3.0 %copy-start.2 = (bf16[2,2,5,4,360]{4,3,2,1,0:T(4,128)(2,1)S(1)}, bf16[2,2,5,4,360]{4,3,2,1,0:T(4,128)(2,1)}, u32[]{:S(2)}) copy-start(bf16[2,2,5,4,360]{4,3,2,1,0:T(4,128)(2,1)} %param.7) | copy-start | bytes 172804
  0.6 3.0 %copy-start = (bf16[2,2,5,16,1440]{4,3,2,1,0:T(8,128)(2,1)S(1)}, bf16[2,2,5,16,1440]{4,3,2,1,0:T(8,128)(2,1)}, u32[]{:S(2)}) copy-start(bf16[2,2,5,16,1440]{4,3,2,1,0:T(8,128)(2,1)} %param.8) | copy-start | bytes 2764804
  0.6 6.1 %collective-permute-start = (bf16[2,2,5,4,360]{4,3,2,1,0:T(4,128)(2,1)}, bf16[2,2,5,4,360]{4,3,2,1,0:T(4,128)(2,1)S(1)}, u32[]{:S(2)}, u32[]{:S(2)}) collective-permute-start(bf16[2,2,5,4,360]{4,3,2,1,0:T(4,128)(2,1)} %param.7), channel_id=1, source_target_pairs={{0,16},{8,24},{16,0},{24,8},{1,17},{9,25},{17,1},{25,9},{2,18},{10... | collective-permute-start | bytes 172808 | tf_op jit(solution)/shard_map/ppermute | solution.py:493
  3.7 1.4 %copy-start.1 = (bf16[2,5,16,1440]{3,2,1,0:T(8,128)(2,1)S(1)}, bf16[2,5,16,1440]{3,2,1,0:T(8,128)(2,1)}, u32[]{:S(2)}) copy-start(bf16[2,5,16,1440]{3,2,1,0:T(8,128)(2,1)} %param.9) | copy-start | bytes 1382404
  3.9 9.8 %collective-permute-start.5 = (bf16[113,8,128]{2,1,0:T(8,128)(2,1)S(1)}, bf16[113,8,128]{2,1,0:T(8,128)(2,1)S(1)}, u32[]{:S(2)}, u32[]{:S(2)}) collective-permute-start(bf16[113,8,128]{2,1,0:T(8,128)(2,1)S(1)} %get-tuple-element.24), channel_id=1, source_target_pairs={{0,16},{8,24},{16,0},{24,8},{1,17},{9,25},{17,1},{25,9},{2,18},{10... | collective-permute-start | bytes 694280 | tf_op jit(solution)/shard_map/ppermute | solution.py:506
  5.1 10.4 %collective-permute-start.6 = (bf16[113,8,128]{2,1,0:T(8,128)(2,1)S(1)}, bf16[113,8,128]{2,1,0:T(8,128)(2,1)S(1)}, u32[]{:S(2)}, u32[]{:S(2)}) collective-permute-start(bf16[113,8,128]{2,1,0:T(8,128)(2,1)S(1)} %get-tuple-element.27), channel_id=1, source_target_pairs={{0,24},{8,16},{16,8},{24,0},{1,25},{9,17},{17,9},{25,1},{2,26},{10... | collective-permute-start | bytes 694280 | tf_op jit(solution)/shard_map/ppermute | solution.py:507
  5.1 1.4 %copy-start.4 = (s32[1440]{0:T(1024)S(1)}, s32[1440]{0:T(1024)}, u32[]{:S(2)}) copy-start(s32[1440]{0:T(1024)} %param.12) | copy-start | bytes 17284
  5.4 1.1 %copy-start.3 = (bf16[4,1440]{1,0:T(4,128)(2,1)S(1)}, bf16[4,1440]{1,0:T(4,128)(2,1)}, u32[]{:S(2)}) copy-start(bf16[4,1440]{1,0:T(4,128)(2,1)} %param.13) | copy-start | bytes 34564
  5.4 8.3 %collective-permute-start.4 = (bf16[10,8,1440]{2,1,0:T(8,128)(2,1)S(1)}, bf16[10,8,1440]{2,1,0:T(8,128)(2,1)S(1)}, u32[]{:S(2)}, u32[]{:S(2)}) collective-permute-start(bf16[10,8,1440]{2,1,0:T(8,128)(2,1)S(1)} %get-tuple-element.19), channel_id=1, source_target_pairs={{0,8},{8,0},{16,24},{24,16},{1,9},{9,1},{17,25},{25,17},{2,10},{10... | collective-permute-start | bytes 691208 | tf_op jit(solution)/shard_map/ppermute | solution.py:518
  6.8 3.7 %copy-start.6 = (s32[16]{0:T(128)S(1)}, s32[16]{0:T(128)}, u32[]{:S(2)}) copy-start(s32[16]{0:T(128)} %param.10) | copy-start | bytes 196
  6.8 5.6 %collective-permute-start.2 = (bf16[40,2,360]{2,1,0:T(2,128)(2,1)S(1)}, bf16[40,2,360]{2,1,0:T(2,128)(2,1)S(1)}, u32[]{:S(2)}, u32[]{:S(2)}) collective-permute-start(bf16[40,2,360]{2,1,0:T(2,128)(2,1)S(1)} %get-tuple-element.18), channel_id=1, source_target_pairs={{0,1},{1,2},{2,3},{3,4},{4,5},{5,6},{6,7},{8,9},{9,10},{10,11},{11... | collective-permute-start | bytes 172808 | tf_op jit(solution)/shard_map/ppermute | solution.py:538
  10.6 1.8 %copy-start.5 = (f32[16,4]{0,1:T(4,128)S(1)}, f32[16,4]{0,1:T(4,128)}, u32[]{:S(2)}) copy-start(f32[16,4]{0,1:T(4,128)} %param.11) | copy-start | bytes 772
  10.6 3.0 %collective-permute-start.1 = (bf16[40,4,360]{2,1,0:T(4,128)(2,1)S(1)}, bf16[40,4,360]{2,1,0:T(4,128)(2,1)S(1)}, u32[]{:S(2)}, u32[]{:S(2)}) collective-permute-start(bf16[40,4,360]{2,1,0:T(4,128)(2,1)S(1)} %get-tuple-element.17.coarse_ref), channel_id=1, source_target_pairs={{0,8},{8,0},{16,24},{24,16},{1,9},{9,1},{17,25},{25,17},{2,10},{10... | collective-permute-start | bytes 345608 | tf_op jit(solution)/shard_map/ppermute | solution.py:539
  12.4 1.2 %collective-permute-start.3 = (bf16[40,2,360]{2,1,0:T(2,128)(2,1)S(1)}, bf16[40,2,360]{2,1,0:T(2,128)(2,1)S(1)}, u32[]{:S(2)}, u32[]{:S(2)}) collective-permute-start(bf16[40,2,360]{2,1,0:T(2,128)(2,1)S(1)} %collective-permute-done.2.halo_ref), channel_id=1, source_target_pairs={{0,8},{8,0},{16,24},{24,16},{1,9},{9,1},{17,25},{25,17},{2,10},{10... | collective-permute-start | bytes 172808 | tf_op jit(solution)/shard_map/ppermute | solution.py:540
